TPU v7x, 32 devices: a whole 2x2x4 slice. The times are simulated.
32 devices in a mesh: gx: 8 (over y, x, core), gy: 4 (over z).
Axes of the slice: x: 2, y: 2, z: 4, core: 2. Of those that a mesh axis runs over, the one named last changes fastest.
Arguments:
- qm_density: float32 [288, 288, 288], P('gx', 'gy'), may hold values from -6 to 6
- mm_coords: float32 [8, 4, 3, 1024], P('gx', 'gy'), may hold values from 0 to 1
- mm_charge: float32 [8, 4, 1024], P('gx', 'gy'), may hold values from -1.8 to 1.8
- mm_types: int32 [8, 4, 1024], P('gx', 'gy'), may hold values from 0 to 15
- type_radius: float32 [16], replicated, may hold values from 0.02 to 0.2
- mm_cells: int32 [8, 4, 1024], P('gx', 'gy'), may hold values from 0 to 746495
- block_counts: int32 [8, 4, 32], P('gx', 'gy'), may hold values from 17 to 32
- block_owner: int32 [8, 4, 32, 1], P('gx', 'gy'), may hold values from 0 to 7; in each aligned block of 32 rows (0 to 31, 32 to 63, ..., all dimensions but the last counted through in order) at most 8 rows name the same one
- neighbour_tiles: int32 [8, 4, 32, 3], P('gx', 'gy'), may hold values from 0 to 8, all different within a row
Outputs:
- potential: float32 [288, 288, 288], P('gx', 'gy')
- mm_potential: float32 [8, 4, 1024], P('gx', 'gy')
- pair_force: float32 [8, 4, 3, 1024], P('gx', 'gy')
Inputs may be any that keep to these rules, and one draw needn't show every extreme that they name: `block_owner`: within one tile no grid owner is named by more than 8 blocks, a bound that the blocks of some tile reach. `neighbour_tiles`: A block's 3 tiles are different.
All inputs are finite; a program needn't handle non-finite values.
Results may differ from a plain program's by a relative error of at most 0.0003.
Values sent between devices are 32-bit elements; how exact they have to be, the bound alone decides.
No kernel may reach another device: no remote copies, remote signals or barrier semaphores. Data moves between devices by JAX's collectives and lax.ppermute only.
A program may use at most 64 MiB of HBM per device.

v0:
```python
import functools

import jax
import jax.numpy as jnp
import ml_dtypes
import numpy as np
from jax import lax
from jax.experimental import pallas as pl
from jax.experimental.pallas import tpu as pltpu
from jax.sharding import PartitionSpec as P

SCREENING = 0.003
HIGH_ACCURACY = lax.Precision.HIGHEST
COPIES = 4
MIB = 1024 * 1024


def round_up(value, unit):
    return -(-value // unit) * unit


def sine_matrix(length):
    nodes = np.arange(length, dtype=np.float64)
    return np.sqrt(2.0 / length) * np.sin(np.pi * np.outer(nodes, nodes) / length)


def cas_matrix(length):
    nodes = np.arange(length)
    angle = 2.0 * np.pi * (np.outer(nodes, nodes) % length) / length
    return np.cos(angle) + np.sin(angle)


def stiffness(count, length):
    return 4.0 * np.sin(np.pi * np.arange(count) / length) ** 2


def split_pair(matrix):
    full = np.asarray(matrix, np.float32)
    high = full.astype(ml_dtypes.bfloat16)
    low = (full - high.astype(np.float32)).astype(ml_dtypes.bfloat16)
    return high, low


def table_triple(matrix, axis):
    high, low = split_pair(matrix)
    return np.concatenate([high, low, high], axis=axis)


def f32(table):
    return np.asarray(table, np.float32)


class Plan:
    def __init__(self, x_len, y_len, grid, n_gx, n_gy):
        self.x_len, self.y_len, self.grid = x_len, y_len, grid
        self.n_gx, self.n_gy = n_gx, n_gy
        self.y_pad = round_up(y_len, 8)
        self.x_pad = round_up(x_len, 8)
        self.lanes = round_up(grid, 128)
        self.lane_tiles = self.lanes // 128
        self.planes = x_len * self.y_pad
        self.span = self.lane_tiles * self.planes * 128
        self.parts = n_gx * n_gy
        self.modes = -(-grid // self.parts)
        self.half = round_up(y_len + x_len, 128)
        self.kx_pad = round_up(n_gx, 8)
        self.j_pad = round_up(n_gy, 8)
        self.stack_rows = round_up(3 * self.y_pad + 2 * self.x_pad, 128)

    def y_matrix(self):
        out = np.zeros((self.y_pad, self.y_pad))
        out[: self.y_len, : self.y_len] = sine_matrix(self.y_len)
        return out

    def z_matrix(self):
        out = np.zeros((self.lanes, self.lanes))
        out[: self.grid, : self.grid] = cas_matrix(self.grid) / np.sqrt(self.grid)
        return out

    def diagonal(self):
        z_part = np.zeros(self.lanes)
        z_part[: self.grid] = stiffness(self.grid, self.grid)
        y_part = stiffness(self.y_pad, 2 * self.y_len)
        return 2.0 + y_part[:, None] + z_part[None, :] + SCREENING

    def edge_weights(self):
        sine_y = self.y_matrix()
        both = np.stack([sine_y[1], sine_y[self.y_len - 1]])
        return np.broadcast_to(both[:, :, None], (2, self.y_pad, 128))

    def interface_table(self):
        x_len, y_len, half = self.x_len, self.y_len, self.half
        y_pad, x_pad = self.y_pad, self.x_pad
        sine_y = sine_matrix(y_len)
        out = np.zeros((self.stack_rows, 2 * half))
        out[:y_len, :y_len] = sine_y
        row = y_pad
        out[row : row + y_len, half : half + y_len] = sine_y
        row += y_pad
        out[row : row + y_len, :y_len] = np.eye(y_len)
        row += y_pad
        out[row + 1 : row + x_len, y_len + 1 : y_len + x_len] = np.eye(x_len - 1)
        row += x_pad
        far = half + y_len
        out[row + 1 : row + x_len, far + 1 : far + x_len] = np.eye(x_len - 1)
        return out

    def gather_table(self):
        n_gx, n_gy, parts = self.n_gx, self.n_gy, self.parts
        cas_x = cas_matrix(n_gx)
        out = np.zeros((n_gy * self.kx_pad + n_gx * self.j_pad, 2 * parts))
        for i in range(n_gx):
            for j in range(n_gy):
                col = i * n_gy + j
                base = j * self.kx_pad
                out[base : base + n_gx, col] = cas_x[:, i]
                out[base : base + n_gx, parts + col] = cas_x[:, (i + 1) % n_gx]
                base = n_gy * self.kx_pad + i * self.j_pad
                out[base + j, col] = 1.0
                out[base + (j + 1) % n_gy, parts + col] = 1.0
        return out

    def line_tables(self):
        scaled = cas_matrix(self.grid) / np.sqrt(self.grid)
        along_y = np.zeros((self.n_gy, self.half, self.lanes))
        along_x = np.zeros((self.n_gx, self.half, self.lanes))
        y_len, x_len, grid = self.y_len, self.x_len, self.grid
        for j in range(self.n_gy):
            along_y[j, :y_len, :grid] = scaled[j * y_len : (j + 1) * y_len]
        for i in range(self.n_gx):
            along_x[i, y_len : y_len + x_len, :grid] = scaled[i * x_len : (i + 1) * x_len]
        return along_y.reshape(-1, self.lanes), along_x.reshape(-1, self.lanes)

    def expand_table(self):
        ratio = self.grid // self.n_gy
        full = cas_matrix(self.grid)
        out = np.zeros((self.j_pad, self.lanes))
        for j in range(self.n_gy):
            out[j, : self.grid] = full[(j * ratio) % self.grid]
        return out


def dot(a, b, dims=((1,), (0,)), precision=None):
    return lax.dot_general(
        a, b, (dims, ((), ())), precision=precision, preferred_element_type=jnp.float32
    )


def value_triple(value, axis):
    high = value.astype(jnp.bfloat16).astype(jnp.float32)
    return jnp.concatenate([high, high, value - high], axis=axis).astype(jnp.bfloat16)


def left_apply(table, value):
    return dot(table, value_triple(value, 0))


def right_apply(value, table):
    return dot(value_triple(value, 1), table)


def slab_count(plan):
    if plan.y_pad != plan.y_len:
        return 1
    return max(count for count in (4, 3, 2, 1) if plan.x_len % count == 0)


def inverse(value):
    guess = pl.reciprocal(value, approx=True)
    guess = guess * (2.0 - value * guess)
    return guess * (2.0 - value * guess)


def owned_blocks(plan, codes, first_code, n_blocks, block_atoms, visit):
    base = first_code[0]

    def tile(source, carry):
        def block(number, inner):
            start = number * block_atoms
            lead = codes[source, start].astype(jnp.int32) - base

            @pl.when((lead >= 0) & (lead < plan.span))
            def _():
                visit(source, number, start, base)

            return inner

        return lax.fori_loop(0, n_blocks, block, carry)

    lax.fori_loop(0, plan.n_gx, tile, 0)


def chunked_loop(count, unroll, body, init):
    while count % unroll:
        unroll -= 1

    def group(step, carry):
        for k in range(unroll):
            carry = body(step * unroll + k, carry)
        return carry

    return lax.fori_loop(0, count // unroll, group, init)


def forward_kernel(
    plan,
    n_blocks,
    block_atoms,
    codes,
    first_code,
    density,
    z_table,
    y_table,
    diagonal,
    edge_y,
    interface,
    spectrum,
    message,
    *scratch,
):
    added = scratch[:COPIES]
    solved, factors, stack, heads, edge_rows, turned = scratch[COPIES:]
    x_len, y_len, y_pad, x_pad = plan.x_len, plan.y_len, plan.y_pad, plan.x_pad
    grid, lane_count, planes = plan.grid, plan.lanes, plan.planes
    slabs = slab_count(plan)
    tile_atoms = n_blocks * block_atoms
    lane_ids = lax.broadcasted_iota(jnp.int32, (1, 128), 1)

    def clear(step, carry):
        for copy in added:
            copy[pl.ds(pl.multiple_of(step * y_pad, 8), y_pad), :] = jnp.zeros(
                (y_pad, 128), jnp.float32
            )
        return carry

    lax.fori_loop(0, plan.lane_tiles * x_len, clear, 0)

    def deposit(source, number, start, base):
        for lead in range(0, block_atoms, COPIES):
            places, rows = [], []
            for k in range(COPIES):
                code = codes[source, start + lead + k].astype(jnp.int32) - base
                charge = codes[source, tile_atoms + start + lead + k]
                place = pl.ds(lax.shift_right_logical(code, 7), 1)
                hit = jnp.where(lane_ids == (code & 127), charge, 0.0)
                places.append(place)
                rows.append(added[k][place, :] + hit)
            for k in range(COPIES):
                added[k][places[k], :] = rows[k]

    owned_blocks(plan, codes, first_code, n_blocks, block_atoms, deposit)

    def transform(step, carry):
        start = step * slabs
        count = slabs * y_pad
        pieces = []
        for tile in range(plan.lane_tiles):
            low = tile * 128
            width = min(128, grid - low)
            piece = density[pl.ds(start, slabs), :, low : low + width]
            if y_pad == y_len:
                piece = piece.reshape(count, width)
            else:
                rows = jnp.zeros((y_pad - y_len, width), jnp.float32)
                piece = jnp.concatenate([piece[0], rows], axis=0)
            if width < 128:
                rest = jnp.zeros((count, 128 - width), jnp.float32)
                piece = jnp.concatenate([piece, rest], axis=1)
            place = pl.ds(pl.multiple_of(tile * planes + start * y_pad, 8), count)
            for copy in added:
                piece = piece + copy[place, :]
            pieces.append(piece)
        lines = right_apply(jnp.concatenate(pieces, axis=1), z_table[...])
        lines = lines.reshape(slabs, y_pad, lane_count)
        for slab in range(slabs):
            x = start + slab
            for tile in range(plan.lane_tiles):
                heads[tile, pl.ds(x, 1), :] = lines[slab, 0:1, tile * 128 : tile * 128 + 128]
            spectrum[x] = left_apply(y_table[...], lines[slab])

        @pl.when(step == 0)
        def _():
            stack[2 * y_pad : 3 * y_pad, :] = lines[0]

        return carry

    chunked_loop(x_len // slabs, 3, transform, 0)
    stack[3 * y_pad :, :] = jnp.zeros((stack.shape[0] - 3 * y_pad, lane_count), jnp.float32)
    for tile in range(plan.lane_tiles):
        lanes = slice(tile * 128, tile * 128 + 128)
        near_weight = edge_y[0]
        far_weight = edge_y[1]

        def eliminate(step, carry):
            factor, value = carry
            x = step + 1
            factor = inverse(diagonal[:, lanes] - factor)
            value = (spectrum[x, :, lanes] + value) * factor
            factors[x] = factor
            solved[x] = value
            return factor, value

        def substitute(step, value):
            x = x_len - 1 - step
            value = solved[x] + factors[x] * value
            near_row = jnp.sum(value * near_weight, axis=0, keepdims=True)
            far_row = jnp.sum(value * far_weight, axis=0, keepdims=True)
            edge_rows[0, pl.ds(x, 1), :] = near_row + heads[tile, pl.ds(x, 1), :]
            edge_rows[1, pl.ds(x, 1), :] = far_row
            return value

        zero = jnp.zeros((y_pad, 128), jnp.float32)
        chunked_loop(x_len - 1, 5, eliminate, (zero, zero))
        stack[y_pad : 2 * y_pad, lanes] = solved[x_len - 1]
        stack[0:y_pad, lanes] = chunked_loop(x_len - 1, 5, substitute, zero)
        for side in range(2):
            row = 3 * y_pad + side * x_pad
            stack[row + 1 : row + x_len, lanes] = edge_rows[side, 1:x_len, :]
    turned[...] = right_apply(jnp.transpose(stack[...]), interface[...])
    total = plan.parts * plan.modes
    for mode in range(grid):
        message[mode] = turned[mode : mode + 1, :]
    if total > grid:
        message[grid:total] = jnp.zeros((total - grid, 1, 2 * plan.half), jnp.float32)


def interface_kernel(
    plan,
    first_mode,
    stiff_z,
    incoming,
    gather,
    scatter,
    along_y,
    along_x,
    along_y_back,
    along_x_back,
    expand,
    expand_back,
    stiff_x,
    stiff_y,
    outgoing,
    rows,
    folded_y,
    folded_x,
    lines,
):
    grid, half, parts, modes = plan.grid, plan.half, plan.parts, plan.modes
    kx_pad, j_pad, n_gx, n_gy = plan.kx_pad, plan.j_pad, plan.n_gx, plan.n_gy
    lane_count = plan.lanes
    groups = grid // n_gx

    def collect(source, carry):
        for mode in range(modes):
            both = incoming[source * modes + mode]
            rows[mode, pl.ds(source, 1), :] = both[:, :half]
            rows[mode, pl.ds(parts + source, 1), :] = both[:, half:]
        return carry

    lax.fori_loop(0, parts, collect, 0)
    for mode in range(modes):
        lines[mode] = left_apply(gather[...], rows[mode])
    base = n_gy * kx_pad
    y_slots = [slice(j * kx_pad, (j + 1) * kx_pad) for j in range(n_gy)]
    x_slots = [slice(base + i * j_pad, base + (i + 1) * j_pad) for i in range(n_gx)]

    def side_by_side(slots, count):
        return jnp.concatenate(
            [lines[:, slot, :].reshape(modes * count, half) for slot in slots], axis=1
        )

    folded_y[...] = right_apply(side_by_side(y_slots, kx_pad), along_y[...]).reshape(
        modes, kx_pad, lane_count
    )
    folded_x[...] = right_apply(side_by_side(x_slots, j_pad), along_x[...]).reshape(
        modes, j_pad, lane_count
    )

    def solve(mode, carry):
        across = folded_x[mode, :, :grid]
        high = across.astype(jnp.bfloat16).astype(jnp.float32)
        across = jnp.concatenate([high, high, across - high], axis=0)
        spread = dot(across, expand[...], ((0,), (0,)))
        number = spread.reshape(groups, kx_pad, lane_count) + folded_y[mode][None]
        bottom = stiff_x[...] + (stiff_y[...] + stiff_z[first_mode[0] + mode])
        value = number * inverse(bottom).reshape(groups, kx_pad, lane_count)
        folded_y[mode] = jnp.sum(value, axis=0)
        value = value_triple(value.reshape(grid, lane_count), 1)
        folded_x[mode, :, :grid] = dot(expand_back[...], value, ((1,), (1,)))
        return carry

    chunked_loop(modes, 3, solve, 0)
    all_y = right_apply(folded_y[...].reshape(modes * kx_pad, lane_count), along_y_back[...])
    for j, slot in enumerate(y_slots):
        lines[:, slot, :] = all_y[:, j * half : (j + 1) * half].reshape(modes, kx_pad, half)
    all_x = right_apply(folded_x[...].reshape(modes * j_pad, lane_count), along_x_back[...])
    for i, slot in enumerate(x_slots):
        lines[:, slot, :] = all_x[:, i * half : (i + 1) * half].reshape(modes, j_pad, half)
    for mode in range(modes):
        rows[mode] = left_apply(scatter[...], lines[mode])

    def distribute(target, carry):
        for mode in range(modes):
            outgoing[target * modes + mode, :, :half] = rows[mode, pl.ds(target, 1), :]
            outgoing[target * modes + mode, :, half:] = rows[mode, pl.ds(parts + target, 1), :]
        return carry

    lax.fori_loop(0, parts, distribute, 0)


def backward_kernel(
    plan,
    n_blocks,
    block_atoms,
    codes,
    first_code,
    spectrum,
    message,
    z_table,
    y_table,
    diagonal,
    edge_y,
    interface,
    potential,
    values,
    lookup,
    work,
    solved,
    factors,
    stack,
    heads,
    edge_rows,
    turned,
    picked,
):
    x_len, y_len, y_pad, x_pad = plan.x_len, plan.y_len, plan.y_pad, plan.x_pad
    grid, lane_count, planes = plan.grid, plan.lanes, plan.planes
    slabs = slab_count(plan)
    for mode in range(grid):
        turned[mode : mode + 1, :] = message[mode]
    if lane_count > grid:
        turned[grid:, :] = jnp.zeros((lane_count - grid, turned.shape[1]), jnp.float32)
    stack[...] = dot(interface[...], value_triple(turned[...], 1), ((1,), (1,)))
    for tile in range(plan.lane_tiles):
        lanes = slice(tile * 128, tile * 128 + 128)
        near_weight = edge_y[0]
        far_weight = edge_y[1]
        heads[tile] = stack[3 * y_pad : 3 * y_pad + x_pad, lanes]
        edge_rows[...] = stack[3 * y_pad + x_pad : 3 * y_pad + 2 * x_pad, lanes]

        def eliminate(step, carry):
            factor, value = carry
            x = step + 1
            factor = inverse(diagonal[:, lanes] - factor)
            load = spectrum[x, :, lanes] + near_weight * heads[tile, pl.ds(x, 1), :]
            load = load + far_weight * edge_rows[pl.ds(x, 1), :]
            value = (load + value) * factor
            factors[x] = factor
            solved[x] = value
            return factor, value

        def substitute(step, value):
            x = x_len - 1 - step
            value = solved[x] + factors[x] * value
            work[x, :, lanes] = value
            return value

        zero = jnp.zeros((y_pad, 128), jnp.float32)
        chunked_loop(x_len - 1, 5, eliminate, (zero, stack[0:y_pad, lanes]))
        chunked_loop(x_len - 1, 5, substitute, stack[y_pad : 2 * y_pad, lanes])
    work[0] = jnp.zeros((y_pad, lane_count), jnp.float32)

    def transform(step, carry):
        start = step * slabs
        for slab in range(slabs):
            x = start + slab
            work[x] = left_apply(y_table[...], work[x])
            for tile in range(plan.lane_tiles):
                lanes = slice(tile * 128, tile * 128 + 128)
                work[x, 0:1, lanes] = heads[tile, pl.ds(x, 1), :]

        @pl.when(step == 0)
        def _():
            work[0] = stack[2 * y_pad : 3 * y_pad, :]

        lines = work[pl.ds(start, slabs)].reshape(slabs * y_pad, lane_count)
        lines = right_apply(lines, z_table[...])
        for tile in range(plan.lane_tiles):
            low = tile * 128
            place = pl.ds(pl.multiple_of(tile * planes + start * y_pad, 8), slabs * y_pad)
            lookup[place, :] = lines[:, low : low + 128]
        lines = lines.reshape(slabs, y_pad, lane_count)
        potential[pl.ds(start, slabs)] = lines[:, :y_len, :grid]
        return carry

    chunked_loop(x_len // slabs, 3, transform, 0)
    values[...] = jnp.zeros(values.shape, jnp.float32)
    lane_ids = lax.broadcasted_iota(jnp.int32, (1, 128), 1)
    shape = (block_atoms, 128)
    own_lane = lax.broadcasted_iota(jnp.int32, shape, 0) == lax.broadcasted_iota(
        jnp.int32, shape, 1
    )

    def sample(source, number, start, base):
        for atom in range(block_atoms):
            code = codes[source, start + atom].astype(jnp.int32) - base
            row = lookup[pl.ds(lax.shift_right_logical(code, 7), 1), :]
            picked[atom : atom + 1, :] = jnp.where(lane_ids == (code & 127), row, 0.0)
        found = jnp.sum(picked[...], axis=1, keepdims=True)
        found = jnp.sum(jnp.where(own_lane, found, 0.0), axis=0, keepdims=True)
        values[pl.ds(source * n_blocks + number, 1), :] = found

    owned_blocks(plan, codes, first_code, n_blocks, block_atoms, sample)


def pair_kernel(
    n_blocks, block_atoms, listed, listing, low, middle, high, forces, table, columns, results
):
    tile_atoms = n_blocks * block_atoms
    sides = (low, middle, high)
    for step_x in range(3):
        for step_y in range(3):
            table[step_x * 3 + step_y, 0:5, :] = sides[step_y][step_x]
    columns[0:8, :] = table[4]
    columns[5:, :] = jnp.zeros((columns.shape[0] - 5, tile_atoms), jnp.float32)
    results[...] = jnp.transpose(columns[...])
    lane_ids = lax.broadcasted_iota(jnp.int32, (block_atoms, 128), 1)

    def block(number, carry):
        place = pl.ds(pl.multiple_of(number * block_atoms, block_atoms), block_atoms)
        own = results[place, :]
        mine = [jnp.broadcast_to(own[:, k : k + 1], (block_atoms, 128)) for k in range(5)]
        zero = jnp.zeros((block_atoms, 128), jnp.float32)

        def tile(slot, sums):
            force_x, force_y, force_z = sums
            which = listing[number, slot]
            shift_x = (which // 3 - 1).astype(jnp.float32)
            shift_y = (which % 3 - 1).astype(jnp.float32)
            for start in range(0, tile_atoms, 128):
                lanes = slice(start, start + 128)
                sep_x = mine[0] - (table[which, 0:1, lanes] + shift_x)
                sep_y = mine[1] - (table[which, 1:2, lanes] + shift_y)
                sep_z = mine[2] - table[which, 2:3, lanes]
                reach = mine[4] + table[which, 4:5, lanes]
                root = lax.rsqrt(sep_x * sep_x + sep_y * sep_y + sep_z * sep_z + reach * reach)
                strength = table[which, 3:4, lanes] * root * root * root
                force_x = force_x + strength * sep_x
                force_y = force_y + strength * sep_y
                force_z = force_z + strength * sep_z
            return force_x, force_y, force_z

        sums = lax.fori_loop(0, listed, tile, (zero, zero, zero))
        out = zero
        for axis in range(3):
            force = mine[3] * jnp.sum(sums[axis], axis=1, keepdims=True)
            out = jnp.where(lane_ids == axis, force, out)
        results[place, :] = out
        return carry

    lax.fori_loop(0, n_blocks, block, 0)
    columns[...] = jnp.transpose(results[...])
    forces[...] = columns[0:3, :]


VMEM = pl.BlockSpec(memory_space=pltpu.VMEM)
SMEM = pl.BlockSpec(memory_space=pltpu.SMEM)


def shaped(*shape):
    return jax.ShapeDtypeStruct(shape, jnp.float32)


def buffer(*shape):
    return pltpu.VMEM(shape, jnp.float32)


def limit(mib):
    return pltpu.CompilerParams(vmem_limit_bytes=mib * MIB)


def solve_poisson(plan, density, codes, first_code, n_blocks, block_atoms):
    x_len, y_len, grid = density.shape
    y_pad, x_pad, half, lanes = plan.y_pad, plan.x_pad, plan.half, plan.lanes
    total = plan.parts * plan.modes
    z_table = table_triple(plan.z_matrix(), 0)
    y_table = table_triple(plan.y_matrix(), 1)
    diagonal = f32(plan.diagonal())
    edge_y = f32(plan.edge_weights())
    interface = plan.interface_table()
    shared = [
        buffer(x_len, y_pad, 128),
        buffer(x_len, y_pad, 128),
        buffer(plan.stack_rows, lanes),
        buffer(plan.lane_tiles, x_pad, 128),
    ]
    spectrum, message = pl.pallas_call(
        functools.partial(forward_kernel, plan, n_blocks, block_atoms),
        out_shape=(shaped(x_len, y_pad, lanes), shaped(total, 1, 2 * half)),
        in_specs=[SMEM] * 2 + [VMEM] * 6,
        out_specs=(VMEM, VMEM),
        scratch_shapes=[buffer(plan.lane_tiles * plan.planes, 128)] * COPIES
        + shared
        + [buffer(2, x_pad, 128), buffer(lanes, 2 * half)],
        compiler_params=limit(44),
        name="forward_solve",
    )(
        codes,
        first_code,
        density,
        z_table,
        y_table,
        diagonal,
        edge_y,
        table_triple(interface, 0),
    )
    incoming = lax.all_to_all(message, ("gx", "gy"), split_axis=0, concat_axis=0, tiled=True)
    gather = plan.gather_table()
    along_y, along_x = plan.line_tables()
    expand = plan.expand_table()
    position = lax.axis_index("gx") * plan.n_gy + lax.axis_index("gy")
    first_mode = (position * plan.modes).astype(jnp.int32).reshape(1)
    stiff = stiffness(grid, grid)
    padded_z = np.zeros(total)
    padded_z[:grid] = stiff
    padded_y = np.zeros((1, lanes))
    padded_y[0, :grid] = stiff
    outgoing = pl.pallas_call(
        functools.partial(interface_kernel, plan),
        out_shape=shaped(total, 1, 2 * half),
        in_specs=[SMEM] * 2 + [VMEM] * 11,
        out_specs=VMEM,
        scratch_shapes=[
            buffer(plan.modes, 2 * plan.parts, half),
            buffer(plan.modes, plan.kx_pad, lanes),
            buffer(plan.modes, plan.j_pad, lanes),
            buffer(plan.modes, gather.shape[0], half),
        ],
        compiler_params=limit(40),
        name="interface_solve",
    )(
        first_mode,
        f32((padded_z + SCREENING) * grid),
        incoming,
        table_triple(gather, 1),
        table_triple(gather.T, 1),
        table_triple(along_y, 0),
        table_triple(along_x, 0),
        table_triple(along_y.reshape(-1, lanes).T, 0),
        table_triple(along_x.reshape(-1, lanes).T, 0),
        f32(table_triple(expand, 0)),
        table_triple(expand, 1),
        f32(stiff[:, None] * grid),
        f32(padded_y * grid),
    )
    returned = lax.all_to_all(outgoing, ("gx", "gy"), split_axis=0, concat_axis=0, tiled=True)
    return pl.pallas_call(
        functools.partial(backward_kernel, plan, n_blocks, block_atoms),
        out_shape=(shaped(x_len, y_len, grid), shaped(plan.n_gx * n_blocks, 128)),
        in_specs=[SMEM] * 2 + [VMEM] * 7,
        out_specs=(VMEM, VMEM),
        scratch_shapes=[
            buffer(plan.lane_tiles * plan.planes, 128),
            buffer(x_len, y_pad, lanes),
        ]
        + shared
        + [buffer(x_pad, 128), buffer(lanes, 2 * half), buffer(block_atoms, 128)],
        compiler_params=limit(36),
        name="backward_solve",
    )(
        codes,
        first_code,
        spectrum,
        returned,
        z_table,
        y_table,
        diagonal,
        edge_y,
        table_triple(interface, 1),
    )


def shifted(block, axis, step):
    count = lax.axis_size(axis)
    return lax.ppermute(block, axis, [(i, (i + step) % count) for i in range(count)])


def body(
    qm_density,
    mm_coords,
    mm_charge,
    mm_types,
    type_radius,
    mm_cells,
    block_counts,
    block_owner,
    neighbour_tiles,
):
    n_blocks = block_counts.shape[2]
    tile_atoms = mm_charge.shape[2]
    block_atoms = tile_atoms // n_blocks
    x_local, local_y_rows, grid_len = qm_density.shape
    n_gx = lax.axis_size("gx")
    plan = Plan(x_local, local_y_rows, grid_len, n_gx, lax.axis_size("gy"))
    atoms = jnp.arange(tile_atoms, dtype=jnp.int32)
    per_atom = jnp.repeat(
        jnp.stack([block_counts.reshape(n_blocks), block_owner.reshape(n_blocks)]),
        block_atoms,
        axis=1,
    )
    live = (atoms % block_atoms < per_atom[0]).astype(jnp.float32)
    charge_live = mm_charge.reshape(tile_atoms) * live
    cells = mm_cells.reshape(tile_atoms)
    line, depth = cells // grid_len, cells % grid_len
    plane = (line // local_y_rows) * plan.y_pad + line % local_y_rows
    code = ((depth // 128) * plan.planes + plane) * 128 + depth % 128
    code = (per_atom[1] * plan.span + code).astype(jnp.float32)
    payload = jnp.concatenate([code, charge_live]).reshape(1, 2 * tile_atoms)
    type_count = type_radius.shape[0]
    type_match = mm_types.reshape(1, tile_atoms) == jnp.arange(type_count)[:, None]
    atom_radius = jnp.sum(jnp.where(type_match, type_radius[:, None], 0.0), axis=0)
    atom_rows = jnp.concatenate(
        [mm_coords.reshape(3, tile_atoms), charge_live[None, :], atom_radius[None, :]], axis=0
    )[None]
    copies = jnp.broadcast_to(payload[None], (n_gx, 1, 2 * tile_atoms))
    codes = lax.all_to_all(copies, "gx", split_axis=0, concat_axis=0, tiled=True)
    codes = codes.reshape(n_gx, 2 * tile_atoms)
    first_code = (lax.axis_index("gx") * plan.span).astype(jnp.int32).reshape(1)
    triple = jnp.concatenate(
        [shifted(atom_rows, "gx", 1), atom_rows, shifted(atom_rows, "gx", -1)], axis=0
    )
    below, above = shifted(triple, "gy", 1), shifted(triple, "gy", -1)
    listed = neighbour_tiles.shape[3]
    pair_force = pl.pallas_call(
        functools.partial(pair_kernel, n_blocks, block_atoms, listed),
        out_shape=shaped(3, tile_atoms),
        in_specs=[SMEM] + [VMEM] * 3,
        out_specs=VMEM,
        scratch_shapes=[
            buffer(9, 8, tile_atoms),
            buffer(128, tile_atoms),
            buffer(tile_atoms, 128),
        ],
        compiler_params=limit(16),
        cost_estimate=pl.CostEstimate(
            flops=21 * listed * tile_atoms * tile_atoms,
            bytes_accessed=4 * 50 * tile_atoms,
            transcendentals=listed * tile_atoms * tile_atoms,
        ),
        name="pair_forces",
    )(neighbour_tiles.reshape(n_blocks, listed), below, triple, above)
    potential, values = solve_poisson(
        plan, qm_density, codes, first_code, n_blocks, block_atoms
    )
    values = lax.all_to_all(values, "gx", split_axis=0, concat_axis=0, tiled=True)
    sampled = jnp.sum(values.reshape(n_gx, n_blocks, 128), axis=0)[:, :block_atoms]
    mm_potential = (sampled.reshape(tile_atoms) * live).reshape(1, 1, tile_atoms)
    return (potential, mm_potential, pair_force.reshape(1, 1, 3, tile_atoms))


def solution(mesh):
    placed = (
        P("gx", "gy", None),
        P("gx", "gy", None, None),
        P("gx", "gy", None),
        P("gx", "gy", None),
        P(),
        P("gx", "gy", None),
        P("gx", "gy", None),
        P("gx", "gy", None, None),
        P("gx", "gy", None, None),
    )
    return jax.shard_map(
        body,
        mesh=mesh,
        in_specs=placed,
        out_specs=(P("gx", "gy", None), P("gx", "gy", None), P("gx", "gy", None, None)),
        check_vma=False,
    )
```

profile of v0, /device:TPU:0, one launch (start us, length us, event | category | flops | bytes accessed | tf_op | source)
XLA Modules:
  0.0 166.6 jit_solution(8891742859157201634)
XLA Ops:
  0.6 0.7 compare_reduce_fusion
  1.3 0.7 broadcast_divide_fusion
  2.1 0.7 multiply_bitcast_fusion
  2.9 0.7 broadcast_in_dim.38
  3.7 0.7 fusion.17
  4.4 0.7 broadcast_in_dim.40
  5.1 5.2 %all-to-all-start = ((f32[8,1,2048]{2,1,0:T(1,128)}), f32[8,1,2048]{2,1,0:T(1,128)S(1)}, u32[]{:S(2)}, u32[]{:S(2)}) async-start(f32[8,1,2048]{2,1,0:T(1,128)} %broadcast_in_dim.40), calls=%async_computation | async-start | bytes 131072 | tf_op jit(solution)/shard_map/all_to_all | solution.py:726
  10.2 5.0 %all-to-all-done = f32[8,1,2048]{2,1,0:T(1,128)S(1)} async-done(((f32[8,1,2048]{2,1,0:T(1,128)}), f32[8,1,2048]{2,1,0:T(1,128)S(1)}, u32[]{:S(2)}, u32[]{:S(2)}) %all-to-all-start) | async-done | bytes 65568 | tf_op jit(solution)/shard_map/all_to_all | solution.py:726
  15.3 2.1 %copy-done = f32[36,72,288]{2,1,0:T(8,128)S(1)} copy-done((f32[36,72,288]{2,1,0:T(8,128)S(1)}, f32[36,72,288]{2,1,0:T(8,128)}, u32[]{:S(2)}) %copy-start) | copy-done | bytes 2986008
  17.4 1.2 copy-done.3
  18.6 1.1 copy-done.13
  19.7 0.9 copy-done.14
  20.6 0.9 copy-done.16
  21.5 0.8 copy-done.18
  22.2 24.4 %forward_solve.1 = (f32[36,72,384]{2,1,0:T(8,128)S(1)}, f32[288,1,256]{2,1,0:T(1,128)}) custom-call(f32[8,2048]{1,0:T(8,128)S(1)} %bitcast.24, s32[1]{0:T(128)} %bitcast.5.first_code, f32[36,72,288]{2,1,0:T(8,128)S(1)} %copy-done, bf16[1152,384]{1,0:T(8,128)(2,1)S(1)} %copy-done.3, bf16[72,216]{1,0:T(8,128)(2,1)S(1)} %copy-done.18, ...), custom_call_target="tpu_custom_call" | custom-call | tf_op jit(solution)/shard_map/forward_solve/pallas_call | solution.py:597
  46.6 1.9 %copy-done.1 = f32[36,72,384]{2,1,0:T(8,128)} copy-done((f32[36,72,384]{2,1,0:T(8,128)}, f32[36,72,384]{2,1,0:T(8,128)S(1)}, u32[]{:S(2)}) %copy-start.1) | copy-done | bytes 3981336
  48.6 12.5 %all-to-all-start.1 = ((f32[288,1,256]{2,1,0:T(1,128)}), f32[288,1,256]{2,1,0:T(1,128)S(1)}, u32[]{:S(2)}, u32[]{:S(2)}) async-start(f32[288,1,256]{2,1,0:T(1,128)} %get-tuple-element.8), calls=%async_computation.1 | async-start | bytes 589824 | tf_op jit(solution)/shard_map/all_to_all | solution.py:617
  61.0 10.6 %all-to-all-done.1.incoming = f32[288,1,256]{2,1,0:T(1,128)S(1)} async-done(((f32[288,1,256]{2,1,0:T(1,128)}), f32[288,1,256]{2,1,0:T(1,128)S(1)}, u32[]{:S(2)}, u32[]{:S(2)}) %all-to-all-start.1) | async-done | bytes 294944 | tf_op jit(solution)/shard_map/all_to_all | solution.py:617
  71.7 1.7 copy-done.6
  73.3 1.3 copy-done.7
  74.6 1.3 copy-done.8
  75.9 0.9 copy-done.20
  76.8 0.8 copy-done.21
  77.6 0.8 copy-done.22
  78.4 0.8 copy-done.23
  79.1 0.7 copy-done.24
  79.9 7.5 %interface_solve.1 = f32[288,1,256]{2,1,0:T(1,128)S(1)} custom-call(s32[1]{0:T(128)} %bitcast.6.first_mode, f32[288]{0:T(512)S(1)} %copy-done.25, f32[288,1,256]{2,1,0:T(1,128)S(1)} %all-to-all-done.1.incoming, bf16[96,192]{1,0:T(8,128)(2,1)S(1)} %copy-done.22, bf16[64,288]{1,0:T(8,128)(2,1)S(1)} %copy-done.21, bf16[1536,384]{1,0:T(8,128)(2,1)S(1)} %copy-done.8, ...), custom_call_target="tpu_custom_call" | custom-call | tf_op jit(solution)/shard_map/interface_solve/pallas_call | solution.py:628
  87.3 0.7 copy-done.9
  88.0 3.0 %all-to-all-start.2 = ((f32[288,1,256]{2,1,0:T(1,128)}), f32[288,1,256]{2,1,0:T(1,128)S(1)}, u32[]{:S(2)}, u32[]{:S(2)}) async-start(f32[288,1,256]{2,1,0:T(1,128)} %copy-done.9), calls=%async_computation.2 | async-start | bytes 589824 | tf_op jit(solution)/shard_map/all_to_all | solution.py:656
  91.1 0.8 broadcast_in_dim.42
  91.9 0.7 copy.41
  92.6 0.7 select_reduce_fusion
  93.4 2.5 %collective-permute-start.1 = (f32[1,5,1024]{2,1,0:T(8,128)S(1)}, f32[1,5,1024]{2,1,0:T(8,128)S(1)}, u32[]{:S(2)}, u32[]{:S(2)}) collective-permute-start(f32[1,5,1024]{2,1,0:T(8,128)S(1)} %maximum_bitcast_fusion), channel_id=1, source_target_pairs={{0,28},{4,0},{8,4},{12,8},{16,12},{20,16},{24,20},{28,24},{1,29},{... | collective-permute-start | bytes 61448 | tf_op jit(solution)/shard_map/ppermute | solution.py:685
  95.9 5.8 %all-to-all-done.2.message = f32[288,1,256]{2,1,0:T(1,128)S(1)} async-done(((f32[288,1,256]{2,1,0:T(1,128)}), f32[288,1,256]{2,1,0:T(1,128)S(1)}, u32[]{:S(2)}, u32[]{:S(2)}) %all-to-all-start.2) | async-done | bytes 294944 | tf_op jit(solution)/shard_map/all_to_all | solution.py:656
  101.7 2.1 %copy-done.2 = f32[36,72,384]{2,1,0:T(8,128)S(1)} copy-done((f32[36,72,384]{2,1,0:T(8,128)S(1)}, f32[36,72,384]{2,1,0:T(8,128)}, u32[]{:S(2)}) %copy-start.2) | copy-done | bytes 3981336
  103.8 0.8 copy-done.11
  104.6 1.1 copy-done.12
  105.7 0.9 copy-done.15
  106.6 0.9 copy-done.17
  107.5 0.8 copy-done.19
  108.3 22.2 %backward_solve.1 = (f32[36,72,288]{2,1,0:T(8,128)}, f32[256,128]{1,0:T(8,128)}) custom-call(f32[8,2048]{1,0:T(8,128)S(1)} %bitcast.25, s32[1]{0:T(128)} %bitcast.5.first_code, f32[36,72,384]{2,1,0:T(8,128)S(1)} %copy-done.2, f32[288,1,256]{2,1,0:T(1,128)S(1)} %all-to-all-done.2.message, bf16[1152,384]{1,0:T(8,128)(2,1)S(1)} %copy-done.4, ...), custom_call_target="tpu_custom_call" | custom-call | tf_op jit(solution)/shard_map/backward_solve/pallas_call | solution.py:657
  130.5 9.7 %all-to-all-start.3 = ((f32[8,32,128]{2,1,0:T(8,128)}), f32[8,32,128]{2,1,0:T(8,128)S(1)}, u32[]{:S(2)}, u32[]{:S(2)}) async-start(f32[8,32,128]{2,1,0:T(8,128)} %bitcast.7), calls=%async_computation.3 | async-start | bytes 262144 | tf_op jit(solution)/shard_map/all_to_all | solution.py:755
  140.2 1.0 collective-permute-start.3
  141.1 1.1 collective-permute-start.2
  142.4 3.0 %collective-permute-done.3.high = f32[3,5,1024]{2,1,0:T(8,128)S(1)} collective-permute-done((f32[3,5,1024]{2,1,0:T(8,128)S(1)}, f32[3,5,1024]{2,1,0:T(8,128)S(1)}, u32[]{:S(2)}, u32[]{:S(2)}) %collective-permute-start.3) | collective-permute-done | bytes 61472 | tf_op jit(solution)/shard_map/ppermute | solution.py:685
  145.4 2.4 %collective-permute-done.2.low = f32[3,5,1024]{2,1,0:T(8,128)S(1)} collective-permute-done((f32[3,5,1024]{2,1,0:T(8,128)S(1)}, f32[3,5,1024]{2,1,0:T(8,128)S(1)}, u32[]{:S(2)}, u32[]{:S(2)}) %collective-permute-start.2) | collective-permute-done | bytes 61472 | tf_op jit(solution)/shard_map/ppermute | solution.py:685
  147.8 17.5 %pair_forces.1 = f32[3,1024]{1,0:T(4,128)S(1)} custom-call(s32[32,3]{1,0:T(8,128)S(1)} %bitcast.27, f32[3,5,1024]{2,1,0:T(8,128)S(1)} %collective-permute-done.2.low, f32[3,5,1024]{2,1,0:T(8,128)S(1)} %pad_maximum_fusion.middle, f32[3,5,1024]{2,1,0:T(8,128)S(1)} %collective-permute-done.3.high), custom_call_target="tpu_custom_call" | custom-call | flops 66060288 | bytes 204800 | tf_op jit(solution)/shard_map/pair_forces/pallas_call | solution.py:734
  165.3 0.6 copy.34
  (60 shorter events, 1.3 us)
Async XLA Ops:
  3.6 43.0 %copy-start.27 = (s32[32,32]{1,0:T(8,128)}, s32[32,32]{1,0:T(8,128)S(1)}, u32[]{:S(2)}) copy-start(s32[32,32]{1,0:T(8,128)S(1)} %broadcast_in_dim.38) | copy-start | bytes 12292
  5.1 10.2 %all-to-all-start = ((f32[8,1,2048]{2,1,0:T(1,128)}), f32[8,1,2048]{2,1,0:T(1,128)S(1)}, u32[]{:S(2)}, u32[]{:S(2)}) async-start(f32[8,1,2048]{2,1,0:T(1,128)} %broadcast_in_dim.40), calls=%async_computation | async-start | bytes 131072 | tf_op jit(solution)/shard_map/all_to_all | solution.py:726
  15.3 31.4 %copy-start.10 = (f32[8,1,2048]{2,0,1:T(8,128)}, f32[8,1,2048]{2,0,1:T(8,128)S(1)}, u32[]{:S(2)}) copy-start(f32[8,1,2048]{2,0,1:T(8,128)S(1)} %copy.40) | copy-start | bytes 196612
  15.3 2.2 %copy-start = (f32[36,72,288]{2,1,0:T(8,128)S(1)}, f32[36,72,288]{2,1,0:T(8,128)}, u32[]{:S(2)}) copy-start(f32[36,72,288]{2,1,0:T(8,128)} %density.1) | copy-start | bytes 8957956
  17.4 1.2 copy-start.3
  18.6 1.1 copy-start.13
  19.7 0.9 copy-start.14
  20.6 0.9 copy-start.16
  21.4 0.8 copy-start.18
  22.2 49.4 %copy-start.5 = (bf16[1152,1024]{1,0:T(8,128)(2,1)S(1)}, bf16[1152,1024]{1,0:T(8,128)(2,1)}, u32[]{:S(2)}) copy-start(bf16[1152,1024]{1,0:T(8,128)(2,1)} %constant.139.clone.along_x_back) | copy-start | bytes 7077892
  22.2 49.4 %copy-start.25 = (f32[288]{0:T(512)S(1)}, f32[288]{0:T(512)}, u32[]{:S(2)}) copy-start(f32[288]{0:T(512)} %constant.133.clone.stiff_z) | copy-start | bytes 3460
  22.2 49.4 %copy-start.26 = (f32[1,384]{1,0:T(1,128)S(1)}, f32[1,384]{1,0:T(1,128)}, u32[]{:S(2)}) copy-start(f32[1,384]{1,0:T(1,128)} %constant.143.clone.stiff_y) | copy-start | bytes 4612
  46.6 1.9 %copy-start.1 = (f32[36,72,384]{2,1,0:T(8,128)}, f32[36,72,384]{2,1,0:T(8,128)S(1)}, u32[]{:S(2)}) copy-start(f32[36,72,384]{2,1,0:T(8,128)S(1)} %get-tuple-element.7.spectrum) | copy-start | bytes 11943940
  48.6 23.1 %all-to-all-start.1 = ((f32[288,1,256]{2,1,0:T(1,128)}), f32[288,1,256]{2,1,0:T(1,128)S(1)}, u32[]{:S(2)}, u32[]{:S(2)}) async-start(f32[288,1,256]{2,1,0:T(1,128)} %get-tuple-element.8), calls=%async_computation.1 | async-start | bytes 589824 | tf_op jit(solution)/shard_map/all_to_all | solution.py:617
  71.6 1.7 %copy-start.6 = (bf16[3072,384]{1,0:T(8,128)(2,1)S(1)}, bf16[3072,384]{1,0:T(8,128)(2,1)}, u32[]{:S(2)}) copy-start(bf16[3072,384]{1,0:T(8,128)(2,1)} %constant.137.clone.along_x) | copy-start | bytes 7077892
  73.3 1.3 copy-start.7
  74.6 1.3 copy-start.8
  75.9 0.9 copy-start.20
  76.8 0.8 copy-start.21
  77.6 0.8 copy-start.22
  78.4 0.8 copy-start.23
  79.1 0.7 copy-start.24
  79.9 12.7 %copy-start.30 = (s32[1,1,1024]{2,1,0:T(1,128)S(1)}, s32[1,1,1024]{2,1,0:T(1,128)}, u32[]{:S(2)}) copy-start(s32[1,1,1024]{2,1,0:T(1,128)} %param.29) | copy-start | bytes 12292
  79.9 13.5 %copy-start.29 = (f32[1,1,1024]{2,1,0:T(1,128)S(1)}, f32[1,1,1024]{2,1,0:T(1,128)}, u32[]{:S(2)}) copy-start(f32[1,1,1024]{2,1,0:T(1,128)} %param.28) | copy-start | bytes 12292
  79.9 21.8 %copy-start.4 = (bf16[1152,384]{1,0:T(8,128)(2,1)S(1)}, bf16[1152,384]{1,0:T(8,128)(2,1)}, u32[]{:S(2)}) copy-start(bf16[1152,384]{1,0:T(8,128)(2,1)} %constant.128.clone.z_table) | copy-start | bytes 2654212
  87.3 0.7 copy-start.9
  88.0 13.6 %all-to-all-start.2 = ((f32[288,1,256]{2,1,0:T(1,128)}), f32[288,1,256]{2,1,0:T(1,128)S(1)}, u32[]{:S(2)}, u32[]{:S(2)}) async-start(f32[288,1,256]{2,1,0:T(1,128)} %copy-done.9), calls=%async_computation.2 | async-start | bytes 589824 | tf_op jit(solution)/shard_map/all_to_all | solution.py:656
  93.4 46.7 %collective-permute-start.1 = (f32[1,5,1024]{2,1,0:T(8,128)S(1)}, f32[1,5,1024]{2,1,0:T(8,128)S(1)}, u32[]{:S(2)}, u32[]{:S(2)}) collective-permute-start(f32[1,5,1024]{2,1,0:T(8,128)S(1)} %maximum_bitcast_fusion), channel_id=1, source_target_pairs={{0,28},{4,0},{8,4},{12,8},{16,12},{20,16},{24,20},{28,24},{1,29},{... | collective-permute-start | bytes 61448 | tf_op jit(solution)/shard_map/ppermute | solution.py:685
  95.9 44.3 %collective-permute-start = (f32[1,5,1024]{2,1,0:T(8,128)S(1)}, f32[1,5,1024]{2,1,0:T(8,128)S(1)}, u32[]{:S(2)}, u32[]{:S(2)}) collective-permute-start(f32[1,5,1024]{2,1,0:T(8,128)S(1)} %maximum_bitcast_fusion), channel_id=1, source_target_pairs={{0,4},{4,8},{8,12},{12,16},{16,20},{20,24},{24,28},{28,0},{1,5},{5... | collective-permute-start | bytes 61448 | tf_op jit(solution)/shard_map/ppermute | solution.py:685
  101.7 2.1 %copy-start.2 = (f32[36,72,384]{2,1,0:T(8,128)S(1)}, f32[36,72,384]{2,1,0:T(8,128)}, u32[]{:S(2)}) copy-start(f32[36,72,384]{2,1,0:T(8,128)} %copy-done.1) | copy-start | bytes 11943940
  103.8 0.8 copy-start.11
  104.6 1.1 copy-start.12
  105.7 0.9 copy-start.15
  106.6 0.9 copy-start.17
  107.5 0.8 copy-start.19
  108.3 34.0 %copy-start.28 = (s32[32,32]{1,0:T(8,128)S(1)}, s32[32,32]{1,0:T(8,128)}, u32[]{:S(2)}) copy-start(s32[32,32]{1,0:T(8,128)} %copy-done.27) | copy-start | bytes 12292
  108.3 34.1 %copy-start.31 = (s32[1,1,32,3]{2,1,3,0:T(1,128)S(1)}, s32[1,1,32,3]{2,1,3,0:T(1,128)}, u32[]{:S(2)}) copy-start(s32[1,1,32,3]{2,1,3,0:T(1,128)} %param.34) | copy-start | bytes 1156
  130.5 35.5 %all-to-all-start.3 = ((f32[8,32,128]{2,1,0:T(8,128)}), f32[8,32,128]{2,1,0:T(8,128)S(1)}, u32[]{:S(2)}, u32[]{:S(2)}) async-start(f32[8,32,128]{2,1,0:T(8,128)} %bitcast.7), calls=%async_computation.3 | async-start | bytes 262144 | tf_op jit(solution)/shard_map/all_to_all | solution.py:755
  140.2 5.3 %collective-permute-start.3 = (f32[3,5,1024]{2,1,0:T(8,128)S(1)}, f32[3,5,1024]{2,1,0:T(8,128)S(1)}, u32[]{:S(2)}, u32[]{:S(2)}) collective-permute-start(f32[3,5,1024]{2,1,0:T(8,128)S(1)} %pad_maximum_fusion.middle), channel_id=1, source_target_pairs={{0,3},{1,0},{2,1},{3,2},{4,7},{5,4},{6,5},{7,6},{8,11},{9,8},{10,9... | collective-permute-start | bytes 184328 | tf_op jit(solution)/shard_map/ppermute | solution.py:685
  141.1 6.7 %collective-permute-start.2 = (f32[3,5,1024]{2,1,0:T(8,128)S(1)}, f32[3,5,1024]{2,1,0:T(8,128)S(1)}, u32[]{:S(2)}, u32[]{:S(2)}) collective-permute-start(f32[3,5,1024]{2,1,0:T(8,128)S(1)} %pad_maximum_fusion.middle), channel_id=1, source_target_pairs={{0,1},{1,2},{2,3},{3,0},{4,5},{5,6},{6,7},{7,4},{8,9},{9,10},{10,1... | collective-permute-start | bytes 184328 | tf_op jit(solution)/shard_map/ppermute | solution.py:685
where the time goes:
time: 169 us; the launch traced here: 167 us
  Pallas kernels  71.5 us (42%)
  starting transfers between devices  34.9 us (21%)
  local copies, waits for them, and re-layouts  28.4 us (17%)
  waiting for transfers between devices  26.8 us (16%)
  other arithmetic  4.2 us (2%)
    unnamed x67, local copies, waits for them, and re-layouts  25.7 us
    pallas_call x1, Pallas kernels, solve_poisson(): pl.pallas_call(functools.partial(forward_kernel, plan, n_blocks, block_at...  24.4 us
    pallas_call x1, Pallas kernels, solve_poisson(): pl.pallas_call(functools.partial(backward_kernel, plan, n_blocks, block_a...  22.2 us
    pallas_call x1, Pallas kernels, body(): pl.pallas_call(functools.partial(pair_kernel, n_blocks, block_atoms, list...  17.5 us
    all_to_all x1, starting transfers between devices, solve_poisson(): lax.all_to_all(message, ('gx', 'gy'), split_axis=0, concat_axis=0, tiled=...  12.5 us
    all_to_all x1, waiting for transfers between devices, solve_poisson(): lax.all_to_all(message, ('gx', 'gy'), split_axis=0, concat_axis=0, tiled=...  10.6 us
    all_to_all x1, starting transfers between devices, body(): lax.all_to_all(values, 'gx', split_axis=0, concat_axis=0, tiled=True)  9.66 us
    pallas_call x1, Pallas kernels, solve_poisson(): pl.pallas_call(functools.partial(interface_kernel, plan), out_shape=shape...  7.46 us
  transfers between devices with their start and end apart: 8, of which 5 were waited for; matrix products, arithmetic and copies ran while one was open for 2% of the time, Pallas kernels for 24%

commit v1 on v0

--- a/solution.py
+++ b/solution.py
@@ -12,6 +12,7 @@
 SCREENING = 0.003
 HIGH_ACCURACY = lax.Precision.HIGHEST
 COPIES = 4
+VMEM_MIB = 60
 MIB = 1024 * 1024
 
 
@@ -171,23 +172,27 @@
     return guess * (2.0 - value * guess)
 
 
-def owned_blocks(plan, codes, first_code, n_blocks, block_atoms, visit):
-    base = first_code[0]
-
-    def tile(source, carry):
-        def block(number, inner):
-            start = number * block_atoms
-            lead = codes[source, start].astype(jnp.int32) - base
-
-            @pl.when((lead >= 0) & (lead < plan.span))
-            def _():
-                visit(source, number, start, base)
-
-            return inner
-
-        return lax.fori_loop(0, n_blocks, block, carry)
-
-    lax.fori_loop(0, plan.n_gx, tile, 0)
+def start_copies(pairs, sems):
+    copies = [
+        pltpu.make_async_copy(source, target, sems.at[k])
+        for k, (source, target) in enumerate(pairs)
+    ]
+    for copy in copies:
+        copy.start()
+    return copies
+
+
+def list_owned(plan, places, blocks, n_blocks, block_atoms):
+    rows = plan.lane_tiles * plan.planes
+
+    def tile(source, count):
+        for number in range(n_blocks):
+            lead = places[source, number * block_atoms]
+            blocks[count] = source * n_blocks + number
+            count = count + jnp.where((lead >= 0) & (lead < rows), 1, 0)
+        return count
+
+    return lax.fori_loop(0, plan.n_gx, tile, 0)
 
 
 def chunked_loop(count, unroll, body, init):
@@ -206,25 +211,51 @@
     plan,
     n_blocks,
     block_atoms,
-    codes,
     first_code,
-    density,
-    z_table,
-    y_table,
-    diagonal,
-    edge_y,
-    interface,
-    spectrum,
+    codes_hbm,
+    density_hbm,
+    z_table_hbm,
+    y_table_hbm,
+    diagonal_hbm,
+    edge_y_hbm,
+    interface_hbm,
+    spectrum_hbm,
+    places_hbm,
     message,
     *scratch,
 ):
     added = scratch[:COPIES]
-    solved, factors, stack, heads, edge_rows, turned = scratch[COPIES:]
+    solved, factors, stack, heads, edge_rows, turned = scratch[COPIES : COPIES + 6]
+    codes, density, z_table, y_table, diagonal, edge_y, interface = scratch[COPIES + 6 : COPIES + 13]
+    spectrum, place_rows, places, charges, blocks, sems = scratch[COPIES + 13 :]
     x_len, y_len, y_pad, x_pad = plan.x_len, plan.y_len, plan.y_pad, plan.x_pad
     grid, lane_count, planes = plan.grid, plan.lanes, plan.planes
     slabs = slab_count(plan)
     tile_atoms = n_blocks * block_atoms
     lane_ids = lax.broadcasted_iota(jnp.int32, (1, 128), 1)
+    loads = start_copies(
+        [
+            (codes_hbm, codes),
+            (codes_hbm.at[:, pl.ds(tile_atoms, tile_atoms)], charges),
+            (density_hbm, density),
+            (z_table_hbm, z_table),
+            (y_table_hbm, y_table),
+            (diagonal_hbm, diagonal),
+            (edge_y_hbm, edge_y),
+            (interface_hbm, interface),
+        ],
+        sems,
+    )
+    loads[0].wait()
+    code = codes[:, :tile_atoms].astype(jnp.int32) - first_code[0]
+    place_rows[:, :tile_atoms] = lax.shift_right_arithmetic(code, 7)
+    place_rows[:, tile_atoms:] = code & 127
+    place_copies = [
+        pltpu.make_async_copy(place_rows, places, sems.at[8]),
+        pltpu.make_async_copy(place_rows, places_hbm, sems.at[9]),
+    ]
+    for copy in place_copies:
+        copy.start()
 
     def clear(step, carry):
         for copy in added:
@@ -233,22 +264,29 @@
             )
         return carry
 
-    lax.fori_loop(0, plan.lane_tiles * x_len, clear, 0)
-
-    def deposit(source, number, start, base):
+    chunked_loop(plan.lane_tiles * x_len, 4, clear, 0)
+    loads[1].wait()
+    place_copies[0].wait()
+    count = list_owned(plan, places, blocks, n_blocks, block_atoms)
+
+    def deposit(slot, carry):
+        block = blocks[slot]
+        source = block // n_blocks
+        start = (block - source * n_blocks) * block_atoms
         for lead in range(0, block_atoms, COPIES):
-            places, rows = [], []
+            rows = [pl.ds(places[source, start + lead + k], 1) for k in range(COPIES)]
+            sums = []
             for k in range(COPIES):
-                code = codes[source, start + lead + k].astype(jnp.int32) - base
-                charge = codes[source, tile_atoms + start + lead + k]
-                place = pl.ds(lax.shift_right_logical(code, 7), 1)
-                hit = jnp.where(lane_ids == (code & 127), charge, 0.0)
-                places.append(place)
-                rows.append(added[k][place, :] + hit)
+                lane = places[source, start + lead + k + tile_atoms]
+                charge = charges[source, start + lead + k]
+                sums.append(added[k][rows[k], :] + jnp.where(lane_ids == lane, charge, 0.0))
             for k in range(COPIES):
-                added[k][places[k], :] = rows[k]
-
-    owned_blocks(plan, codes, first_code, n_blocks, block_atoms, deposit)
+                added[k][rows[k], :] = sums[k]
+        return carry
+
+    lax.fori_loop(0, count, deposit, 0)
+    for copy in loads[2:5]:
+        copy.wait()
 
     def transform(step, carry):
         start = step * slabs
@@ -285,6 +323,10 @@
         return carry
 
     chunked_loop(x_len // slabs, 3, transform, 0)
+    spectrum_copy = pltpu.make_async_copy(spectrum, spectrum_hbm, sems.at[10])
+    spectrum_copy.start()
+    for copy in loads[5:8]:
+        copy.wait()
     stack[3 * y_pad :, :] = jnp.zeros((stack.shape[0] - 3 * y_pad, lane_count), jnp.float32)
     for tile in range(plan.lane_tiles):
         lanes = slice(tile * 128, tile * 128 + 128)
@@ -322,29 +364,60 @@
         message[mode] = turned[mode : mode + 1, :]
     if total > grid:
         message[grid:total] = jnp.zeros((total - grid, 1, 2 * plan.half), jnp.float32)
+    spectrum_copy.wait()
+    place_copies[1].wait()
 
 
 def interface_kernel(
     plan,
     first_mode,
     stiff_z,
-    incoming,
-    gather,
-    scatter,
-    along_y,
-    along_x,
-    along_y_back,
-    along_x_back,
-    expand,
-    expand_back,
-    stiff_x,
-    stiff_y,
+    earlier_hbm,
+    incoming_hbm,
+    gather_hbm,
+    along_y_hbm,
+    along_x_hbm,
+    expand_hbm,
+    expand_back_hbm,
+    stiff_x_hbm,
+    stiff_y_hbm,
+    along_y_back_hbm,
+    along_x_back_hbm,
+    scatter_hbm,
     outgoing,
     rows,
     folded_y,
     folded_x,
     lines,
+    incoming,
+    gather,
+    along_y,
+    along_x,
+    expand,
+    expand_back,
+    stiff_x,
+    stiff_y,
+    along_y_back,
+    along_x_back,
+    scatter,
+    sems,
 ):
+    loads = start_copies(
+        [
+            (incoming_hbm, incoming),
+            (gather_hbm, gather),
+            (along_y_hbm, along_y),
+            (along_x_hbm, along_x),
+            (expand_hbm, expand),
+            (expand_back_hbm, expand_back),
+            (stiff_x_hbm, stiff_x),
+            (stiff_y_hbm, stiff_y),
+            (along_y_back_hbm, along_y_back),
+            (along_x_back_hbm, along_x_back),
+            (scatter_hbm, scatter),
+        ],
+        sems,
+    )
     grid, half, parts, modes = plan.grid, plan.half, plan.parts, plan.modes
     kx_pad, j_pad, n_gx, n_gy = plan.kx_pad, plan.j_pad, plan.n_gx, plan.n_gy
     lane_count = plan.lanes
@@ -357,7 +430,9 @@
             rows[mode, pl.ds(parts + source, 1), :] = both[:, half:]
         return carry
 
+    loads[0].wait()
     lax.fori_loop(0, parts, collect, 0)
+    loads[1].wait()
     for mode in range(modes):
         lines[mode] = left_apply(gather[...], rows[mode])
     base = n_gy * kx_pad
@@ -369,6 +444,8 @@
             [lines[:, slot, :].reshape(modes * count, half) for slot in slots], axis=1
         )
 
+    loads[2].wait()
+    loads[3].wait()
     folded_y[...] = right_apply(side_by_side(y_slots, kx_pad), along_y[...]).reshape(
         modes, kx_pad, lane_count
     )
@@ -389,7 +466,11 @@
         folded_x[mode, :, :grid] = dot(expand_back[...], value, ((1,), (1,)))
         return carry
 
+    for copy in loads[4:8]:
+        copy.wait()
     chunked_loop(modes, 3, solve, 0)
+    for copy in loads[8:]:
+        copy.wait()
     all_y = right_apply(folded_y[...].reshape(modes * kx_pad, lane_count), along_y_back[...])
     for j, slot in enumerate(y_slots):
         lines[:, slot, :] = all_y[:, j * half : (j + 1) * half].reshape(modes, kx_pad, half)
@@ -412,16 +493,15 @@
     plan,
     n_blocks,
     block_atoms,
-    codes,
-    first_code,
-    spectrum,
-    message,
-    z_table,
-    y_table,
-    diagonal,
-    edge_y,
-    interface,
-    potential,
+    places_hbm,
+    message_hbm,
+    interface_hbm,
+    diagonal_hbm,
+    edge_y_hbm,
+    spectrum_hbm,
+    y_table_hbm,
+    z_table_hbm,
+    potential_hbm,
     values,
     lookup,
     work,
@@ -432,15 +512,46 @@
     edge_rows,
     turned,
     picked,
+    potential,
+    places,
+    message,
+    interface,
+    diagonal,
+    edge_y,
+    spectrum,
+    y_table,
+    z_table,
+    blocks,
+    sems,
 ):
     x_len, y_len, y_pad, x_pad = plan.x_len, plan.y_len, plan.y_pad, plan.x_pad
     grid, lane_count, planes = plan.grid, plan.lanes, plan.planes
     slabs = slab_count(plan)
+    tile_atoms = n_blocks * block_atoms
+    loads = start_copies(
+        [
+            (message_hbm, message),
+            (interface_hbm, interface),
+            (places_hbm, places),
+            (diagonal_hbm, diagonal),
+            (edge_y_hbm, edge_y),
+            (spectrum_hbm, spectrum),
+            (y_table_hbm, y_table),
+            (z_table_hbm, z_table),
+        ],
+        sems,
+    )
+    loads[0].wait()
     for mode in range(grid):
         turned[mode : mode + 1, :] = message[mode]
     if lane_count > grid:
         turned[grid:, :] = jnp.zeros((lane_count - grid, turned.shape[1]), jnp.float32)
+    loads[1].wait()
     stack[...] = dot(interface[...], value_triple(turned[...], 1), ((1,), (1,)))
+    loads[2].wait()
+    count = list_owned(plan, places, blocks, n_blocks, block_atoms)
+    for copy in loads[3:]:
+        copy.wait()
     for tile in range(plan.lane_tiles):
         lanes = slice(tile * 128, tile * 128 + 128)
         near_weight = edge_y[0]
@@ -494,6 +605,8 @@
         return carry
 
     chunked_loop(x_len // slabs, 3, transform, 0)
+    potential_copy = pltpu.make_async_copy(potential, potential_hbm, sems.at[8])
+    potential_copy.start()
     values[...] = jnp.zeros(values.shape, jnp.float32)
     lane_ids = lax.broadcasted_iota(jnp.int32, (1, 128), 1)
     shape = (block_atoms, 128)
@@ -501,16 +614,57 @@
         jnp.int32, shape, 1
     )
 
-    def sample(source, number, start, base):
+    def sample(slot, carry):
+        block = blocks[slot]
+        source = block // n_blocks
+        start = (block - source * n_blocks) * block_atoms
         for atom in range(block_atoms):
-            code = codes[source, start + atom].astype(jnp.int32) - base
-            row = lookup[pl.ds(lax.shift_right_logical(code, 7), 1), :]
-            picked[atom : atom + 1, :] = jnp.where(lane_ids == (code & 127), row, 0.0)
+            row = lookup[pl.ds(places[source, start + atom], 1), :]
+            lane = places[source, start + atom + tile_atoms]
+            picked[atom : atom + 1, :] = jnp.where(lane_ids == lane, row, 0.0)
         found = jnp.sum(picked[...], axis=1, keepdims=True)
         found = jnp.sum(jnp.where(own_lane, found, 0.0), axis=0, keepdims=True)
-        values[pl.ds(source * n_blocks + number, 1), :] = found
-
-    owned_blocks(plan, codes, first_code, n_blocks, block_atoms, sample)
+        values[pl.ds(block, 1), :] = found
+        return carry
+
+    lax.fori_loop(0, count, sample, 0)
+    potential_copy.wait()
+
+
+def prepare_kernel(
+    plan, n_blocks, block_atoms, counts, owners, type_radius, coords, charge, types, cells,
+    copies, atom_rows,
+):
+    tile_atoms = n_blocks * block_atoms
+    lane = lax.broadcasted_iota(jnp.int32, (1, 128), 1)
+    slot = lane // block_atoms
+    atom = lane - slot * block_atoms
+    per_row = 128 // block_atoms
+    for start in range(0, tile_atoms, 128):
+        lanes = slice(start, start + 128)
+        first = start // block_atoms
+        count = jnp.full((1, 128), counts[0, first], jnp.int32)
+        owner = jnp.full((1, 128), owners[0, first], jnp.int32)
+        for k in range(1, per_row):
+            count = jnp.where(slot >= k, counts[0, first + k], count)
+            owner = jnp.where(slot >= k, owners[0, first + k], owner)
+        live = jnp.where(atom < count, charge[0, :, lanes], 0.0)
+        cell = cells[0, :, lanes]
+        line = jnp.floor((cell.astype(jnp.float32) + 0.5) * (1.0 / plan.grid)).astype(jnp.int32)
+        depth = cell - line * plan.grid
+        x = jnp.floor((line.astype(jnp.float32) + 0.5) * (1.0 / plan.y_len)).astype(jnp.int32)
+        plane = x * plan.y_pad + (line - x * plan.y_len)
+        code = ((depth >> 7) * plan.planes + plane) * 128 + (depth & 127)
+        code = (owner * plan.span + code).astype(jnp.float32)
+        for target in range(plan.n_gx):
+            copies[target, :, lanes] = code
+            copies[target, :, tile_atoms + start : tile_atoms + start + 128] = live
+        radius = jnp.zeros((1, 128), jnp.float32)
+        for kind in range(type_radius.shape[0]):
+            radius = jnp.where(types[0, :, lanes] == kind, type_radius[kind], radius)
+        atom_rows[0, 0:3, lanes] = coords[0, 0, :, lanes]
+        atom_rows[0, 3:4, lanes] = live
+        atom_rows[0, 4:5, lanes] = radius
 
 
 def pair_kernel(
@@ -520,40 +674,50 @@
     sides = (low, middle, high)
     for step_x in range(3):
         for step_y in range(3):
-            table[step_x * 3 + step_y, 0:5, :] = sides[step_y][step_x]
-    columns[0:8, :] = table[4]
+            rows = sides[step_y][step_x]
+            shifts = (step_x - 1.0, step_y - 1.0, 0.0, 0.0, 0.0)
+            for k in range(5):
+                row = rows[k : k + 1, :]
+                if shifts[k]:
+                    row = row + shifts[k]
+                table[step_x * 3 + step_y, k] = jnp.broadcast_to(row, (8, tile_atoms))
+    columns[0:5, :] = middle[1]
     columns[5:, :] = jnp.zeros((columns.shape[0] - 5, tile_atoms), jnp.float32)
     results[...] = jnp.transpose(columns[...])
     lane_ids = lax.broadcasted_iota(jnp.int32, (block_atoms, 128), 1)
+    groups = block_atoms // 8
 
     def block(number, carry):
         place = pl.ds(pl.multiple_of(number * block_atoms, block_atoms), block_atoms)
         own = results[place, :]
-        mine = [jnp.broadcast_to(own[:, k : k + 1], (block_atoms, 128)) for k in range(5)]
-        zero = jnp.zeros((block_atoms, 128), jnp.float32)
+        mine = [
+            jnp.broadcast_to(own[:, k : k + 1], (block_atoms, 128)).reshape(groups, 8, 128)
+            for k in range(5)
+        ]
+        zero = jnp.zeros((groups, 8, 128), jnp.float32)
 
         def tile(slot, sums):
             force_x, force_y, force_z = sums
             which = listing[number, slot]
-            shift_x = (which // 3 - 1).astype(jnp.float32)
-            shift_y = (which % 3 - 1).astype(jnp.float32)
             for start in range(0, tile_atoms, 128):
                 lanes = slice(start, start + 128)
-                sep_x = mine[0] - (table[which, 0:1, lanes] + shift_x)
-                sep_y = mine[1] - (table[which, 1:2, lanes] + shift_y)
-                sep_z = mine[2] - table[which, 2:3, lanes]
-                reach = mine[4] + table[which, 4:5, lanes]
+                other = [table[which, k, :, lanes][None] for k in range(5)]
+                sep_x = mine[0] - other[0]
+                sep_y = mine[1] - other[1]
+                sep_z = mine[2] - other[2]
+                reach = mine[4] + other[4]
                 root = lax.rsqrt(sep_x * sep_x + sep_y * sep_y + sep_z * sep_z + reach * reach)
-                strength = table[which, 3:4, lanes] * root * root * root
+                strength = other[3] * root * (root * root)
                 force_x = force_x + strength * sep_x
                 force_y = force_y + strength * sep_y
                 force_z = force_z + strength * sep_z
             return force_x, force_y, force_z
 
         sums = lax.fori_loop(0, listed, tile, (zero, zero, zero))
-        out = zero
+        out = jnp.zeros((block_atoms, 128), jnp.float32)
         for axis in range(3):
-            force = mine[3] * jnp.sum(sums[axis], axis=1, keepdims=True)
+            total = sums[axis].reshape(block_atoms, 128)
+            force = own[:, 3:4] * jnp.sum(total, axis=1, keepdims=True)
             out = jnp.where(lane_ids == axis, force, out)
         results[place, :] = out
         return carry
@@ -565,6 +729,7 @@
 
 VMEM = pl.BlockSpec(memory_space=pltpu.VMEM)
 SMEM = pl.BlockSpec(memory_space=pltpu.SMEM)
+HBM = pl.BlockSpec(memory_space=pl.ANY)
 
 
 def shaped(*shape):
@@ -575,11 +740,15 @@
     return pltpu.VMEM(shape, jnp.float32)
 
 
+def like(table):
+    return pltpu.VMEM(table.shape, table.dtype)
+
+
 def limit(mib):
     return pltpu.CompilerParams(vmem_limit_bytes=mib * MIB)
 
 
-def solve_poisson(plan, density, codes, first_code, n_blocks, block_atoms):
+def solve_poisson(plan, density, codes, first_code, n_blocks, block_atoms, earlier):
     x_len, y_len, grid = density.shape
     y_pad, x_pad, half, lanes = plan.y_pad, plan.x_pad, plan.half, plan.lanes
     total = plan.parts * plan.modes
@@ -587,33 +756,46 @@
     y_table = table_triple(plan.y_matrix(), 1)
     diagonal = f32(plan.diagonal())
     edge_y = f32(plan.edge_weights())
-    interface = plan.interface_table()
+    interface = table_triple(plan.interface_table(), 0)
+    interface_back = table_triple(plan.interface_table(), 1)
+    n_rows, tile_atoms = codes.shape[0], n_blocks * block_atoms
     shared = [
         buffer(x_len, y_pad, 128),
         buffer(x_len, y_pad, 128),
         buffer(plan.stack_rows, lanes),
         buffer(plan.lane_tiles, x_pad, 128),
     ]
-    spectrum, message = pl.pallas_call(
+    spectrum, places, message = pl.pallas_call(
         functools.partial(forward_kernel, plan, n_blocks, block_atoms),
-        out_shape=(shaped(x_len, y_pad, lanes), shaped(total, 1, 2 * half)),
-        in_specs=[SMEM] * 2 + [VMEM] * 6,
-        out_specs=(VMEM, VMEM),
+        out_shape=(
+            shaped(x_len, y_pad, lanes),
+            jax.ShapeDtypeStruct((n_rows, 2 * tile_atoms), jnp.int32),
+            shaped(total, 1, 2 * half),
+        ),
+        in_specs=[SMEM] + [HBM] * 7,
+        out_specs=(HBM, HBM, VMEM),
         scratch_shapes=[buffer(plan.lane_tiles * plan.planes, 128)] * COPIES
         + shared
-        + [buffer(2, x_pad, 128), buffer(lanes, 2 * half)],
-        compiler_params=limit(44),
+        + [
+            buffer(2, x_pad, 128),
+            buffer(lanes, 2 * half),
+            buffer(n_rows, 2 * tile_atoms),
+            buffer(x_len, y_len, grid),
+            like(z_table),
+            like(y_table),
+            like(diagonal),
+            like(edge_y),
+            like(interface),
+            buffer(x_len, y_pad, lanes),
+            pltpu.VMEM((n_rows, 2 * tile_atoms), jnp.int32),
+            pltpu.SMEM((n_rows, 2 * tile_atoms), jnp.int32),
+            pltpu.SMEM((n_rows, tile_atoms), jnp.float32),
+            pltpu.SMEM((n_rows * n_blocks,), jnp.int32),
+            pltpu.SemaphoreType.DMA((11,)),
+        ],
+        compiler_params=limit(VMEM_MIB),
         name="forward_solve",
-    )(
-        codes,
-        first_code,
-        density,
-        z_table,
-        y_table,
-        diagonal,
-        edge_y,
-        table_triple(interface, 0),
-    )
+    )(first_code, codes, density, z_table, y_table, diagonal, edge_y, interface)
     incoming = lax.all_to_all(message, ("gx", "gy"), split_axis=0, concat_axis=0, tiled=True)
     gather = plan.gather_table()
     along_y, along_x = plan.line_tables()
@@ -625,59 +807,65 @@
     padded_z[:grid] = stiff
     padded_y = np.zeros((1, lanes))
     padded_y[0, :grid] = stiff
+    tables = [
+        table_triple(gather, 1),
+        table_triple(along_y, 0),
+        table_triple(along_x, 0),
+        f32(table_triple(expand, 0)),
+        table_triple(expand, 1),
+        f32(stiff[:, None] * grid),
+        f32(padded_y * grid),
+        table_triple(along_y.T, 0),
+        table_triple(along_x.T, 0),
+        table_triple(gather.T, 1),
+    ]
     outgoing = pl.pallas_call(
         functools.partial(interface_kernel, plan),
         out_shape=shaped(total, 1, 2 * half),
-        in_specs=[SMEM] * 2 + [VMEM] * 11,
+        in_specs=[SMEM] * 2 + [HBM] * 12,
         out_specs=VMEM,
         scratch_shapes=[
             buffer(plan.modes, 2 * plan.parts, half),
             buffer(plan.modes, plan.kx_pad, lanes),
             buffer(plan.modes, plan.j_pad, lanes),
             buffer(plan.modes, gather.shape[0], half),
+            buffer(total, 1, 2 * half),
+            *[like(table) for table in tables],
+            pltpu.SemaphoreType.DMA((11,)),
         ],
-        compiler_params=limit(40),
+        compiler_params=limit(VMEM_MIB),
         name="interface_solve",
-    )(
-        first_mode,
-        f32((padded_z + SCREENING) * grid),
-        incoming,
-        table_triple(gather, 1),
-        table_triple(gather.T, 1),
-        table_triple(along_y, 0),
-        table_triple(along_x, 0),
-        table_triple(along_y.reshape(-1, lanes).T, 0),
-        table_triple(along_x.reshape(-1, lanes).T, 0),
-        f32(table_triple(expand, 0)),
-        table_triple(expand, 1),
-        f32(stiff[:, None] * grid),
-        f32(padded_y * grid),
-    )
+    )(first_mode, f32((padded_z + SCREENING) * grid), earlier, incoming, *tables)
     returned = lax.all_to_all(outgoing, ("gx", "gy"), split_axis=0, concat_axis=0, tiled=True)
     return pl.pallas_call(
         functools.partial(backward_kernel, plan, n_blocks, block_atoms),
         out_shape=(shaped(x_len, y_len, grid), shaped(plan.n_gx * n_blocks, 128)),
-        in_specs=[SMEM] * 2 + [VMEM] * 7,
-        out_specs=(VMEM, VMEM),
+        in_specs=[HBM] * 8,
+        out_specs=(HBM, VMEM),
         scratch_shapes=[
             buffer(plan.lane_tiles * plan.planes, 128),
             buffer(x_len, y_pad, lanes),
         ]
         + shared
-        + [buffer(x_pad, 128), buffer(lanes, 2 * half), buffer(block_atoms, 128)],
-        compiler_params=limit(36),
+        + [
+            buffer(x_pad, 128),
+            buffer(lanes, 2 * half),
+            buffer(block_atoms, 128),
+            buffer(x_len, y_len, grid),
+            pltpu.SMEM((n_rows, 2 * tile_atoms), jnp.int32),
+            buffer(total, 1, 2 * half),
+            like(interface_back),
+            like(diagonal),
+            like(edge_y),
+            buffer(x_len, y_pad, lanes),
+            like(y_table),
+            like(z_table),
+            pltpu.SMEM((n_rows * n_blocks,), jnp.int32),
+            pltpu.SemaphoreType.DMA((9,)),
+        ],
+        compiler_params=limit(VMEM_MIB),
         name="backward_solve",
-    )(
-        codes,
-        first_code,
-        spectrum,
-        returned,
-        z_table,
-        y_table,
-        diagonal,
-        edge_y,
-        table_triple(interface, 1),
-    )
+    )(places, returned, interface_back, diagonal, edge_y, spectrum, y_table, z_table)
 
 
 def shifted(block, axis, step):
@@ -702,27 +890,22 @@
     x_local, local_y_rows, grid_len = qm_density.shape
     n_gx = lax.axis_size("gx")
     plan = Plan(x_local, local_y_rows, grid_len, n_gx, lax.axis_size("gy"))
-    atoms = jnp.arange(tile_atoms, dtype=jnp.int32)
-    per_atom = jnp.repeat(
-        jnp.stack([block_counts.reshape(n_blocks), block_owner.reshape(n_blocks)]),
-        block_atoms,
-        axis=1,
-    )
-    live = (atoms % block_atoms < per_atom[0]).astype(jnp.float32)
-    charge_live = mm_charge.reshape(tile_atoms) * live
-    cells = mm_cells.reshape(tile_atoms)
-    line, depth = cells // grid_len, cells % grid_len
-    plane = (line // local_y_rows) * plan.y_pad + line % local_y_rows
-    code = ((depth // 128) * plan.planes + plane) * 128 + depth % 128
-    code = (per_atom[1] * plan.span + code).astype(jnp.float32)
-    payload = jnp.concatenate([code, charge_live]).reshape(1, 2 * tile_atoms)
-    type_count = type_radius.shape[0]
-    type_match = mm_types.reshape(1, tile_atoms) == jnp.arange(type_count)[:, None]
-    atom_radius = jnp.sum(jnp.where(type_match, type_radius[:, None], 0.0), axis=0)
-    atom_rows = jnp.concatenate(
-        [mm_coords.reshape(3, tile_atoms), charge_live[None, :], atom_radius[None, :]], axis=0
-    )[None]
-    copies = jnp.broadcast_to(payload[None], (n_gx, 1, 2 * tile_atoms))
+    copies, atom_rows = pl.pallas_call(
+        functools.partial(prepare_kernel, plan, n_blocks, block_atoms),
+        out_shape=(shaped(n_gx, 1, 2 * tile_atoms), shaped(1, 5, tile_atoms)),
+        in_specs=[SMEM] * 3 + [VMEM] * 4,
+        out_specs=(VMEM, VMEM),
+        compiler_params=limit(VMEM_MIB),
+        name="prepare_atoms",
+    )(
+        block_counts.reshape(1, n_blocks),
+        block_owner.reshape(1, n_blocks),
+        type_radius,
+        mm_coords,
+        mm_charge,
+        mm_types,
+        mm_cells,
+    )
     codes = lax.all_to_all(copies, "gx", split_axis=0, concat_axis=0, tiled=True)
     codes = codes.reshape(n_gx, 2 * tile_atoms)
     first_code = (lax.axis_index("gx") * plan.span).astype(jnp.int32).reshape(1)
@@ -737,11 +920,11 @@
         in_specs=[SMEM] + [VMEM] * 3,
         out_specs=VMEM,
         scratch_shapes=[
-            buffer(9, 8, tile_atoms),
+            buffer(9, 5, 8, tile_atoms),
             buffer(128, tile_atoms),
             buffer(tile_atoms, 128),
         ],
-        compiler_params=limit(16),
+        compiler_params=limit(VMEM_MIB),
         cost_estimate=pl.CostEstimate(
             flops=21 * listed * tile_atoms * tile_atoms,
             bytes_accessed=4 * 50 * tile_atoms,
@@ -750,11 +933,13 @@
         name="pair_forces",
     )(neighbour_tiles.reshape(n_blocks, listed), below, triple, above)
     potential, values = solve_poisson(
-        plan, qm_density, codes, first_code, n_blocks, block_atoms
+        plan, qm_density, codes, first_code, n_blocks, block_atoms, pair_force
     )
     values = lax.all_to_all(values, "gx", split_axis=0, concat_axis=0, tiled=True)
     sampled = jnp.sum(values.reshape(n_gx, n_blocks, 128), axis=0)[:, :block_atoms]
-    mm_potential = (sampled.reshape(tile_atoms) * live).reshape(1, 1, tile_atoms)
+    lanes = jnp.arange(block_atoms, dtype=jnp.int32)
+    live = lanes[None, :] < block_counts.reshape(n_blocks, 1)
+    mm_potential = jnp.where(live, sampled, 0.0).reshape(1, 1, tile_atoms)
     return (potential, mm_potential, pair_force.reshape(1, 1, 3, tile_atoms))
 
 

time: 169 us -> 145 us (0.86); the launches traced: 167 us -> 145 us
  local copies, waits for them, and re-layouts: 28.4 us -> 5.3 us
  blocking collectives: 0 us -> 13.9 us
  waiting for transfers between devices: 26.8 us -> 17.8 us
  starting transfers between devices: 34.9 us -> 39.9 us
  Pallas kernels: 71.5 us -> 66.9 us
  other arithmetic: 4.2 us -> 0.08 us
    unnamed x67 -> x21, local copies, waits for them, and re-layouts: 25.7 us -> 3.94 us
    all_to_all x0 -> x1, blocking collectives: none -> 13.9 us  [solve_poisson(): lax.all_to_all(outgoing, ('gx', 'gy'), split_axis=0, concat_axis=0, tiled...]
    all_to_all x1, waiting for transfers between devices: 10.6 us -> 0.01 us  [solve_poisson(): lax.all_to_all(message, ('gx', 'gy'), split_axis=0, concat_axis=0, tiled=...]
    pallas_call x1, Pallas kernels: 24.4 us -> 18.3 us  [solve_poisson(): pl.pallas_call(functools.partial(forward_kernel, plan, n_blocks, block_at...]
    pallas_call x1, Pallas kernels: 22.2 us -> 16.4 us  [solve_poisson(): pl.pallas_call(functools.partial(backward_kernel, plan, n_blocks, block_a...]
    all_to_all x1 -> x0, waiting for transfers between devices: 5.81 us -> none  [solve_poisson(): lax.all_to_all(outgoing, ('gx', 'gy'), split_axis=0, concat_axis=0, tiled...]
    all_to_all x1, waiting for transfers between devices: 0.01 us -> 4.91 us  [body(): lax.all_to_all(values, 'gx', split_axis=0, concat_axis=0, tiled=True)]
    ppermute x4, starting transfers between devices: 4.56 us -> 8.01 us  [shifted(): lax.ppermute(block, axis, [(i, (i + step) % count) for i in range(count)])]
  transfers between devices with their start and end apart: 8 -> 7, of which waited for: 5 -> 5; matrix products, arithmetic and copies ran while one was open for 2% -> 1% of each run, Pallas kernels for 24% -> 14%
where the time goes in v1:
time: 145 us
  Pallas kernels  66.9 us (46%)
  starting transfers between devices  39.9 us (28%)
  waiting for transfers between devices  17.8 us (12%)
  blocking collectives  13.9 us (10%)
  local copies, waits for them, and re-layouts  5.3 us (4%)
    pallas_call x1, Pallas kernels, body(): pl.pallas_call(functools.partial(pair_kernel, n_blocks, block_atoms, list...  20.6 us
    pallas_call x1, Pallas kernels, solve_poisson(): pl.pallas_call(functools.partial(forward_kernel, plan, n_blocks, block_at...  18.3 us
    pallas_call x1, Pallas kernels, solve_poisson(): pl.pallas_call(functools.partial(backward_kernel, plan, n_blocks, block_a...  16.4 us
    all_to_all x1, starting transfers between devices, solve_poisson(): lax.all_to_all(message, ('gx', 'gy'), split_axis=0, concat_axis=0, tiled=...  13.9 us
    all_to_all x1, blocking collectives, solve_poisson(): lax.all_to_all(outgoing, ('gx', 'gy'), split_axis=0, concat_axis=0, tiled...  13.9 us
    all_to_all x1, starting transfers between devices, body(): lax.all_to_all(values, 'gx', split_axis=0, concat_axis=0, tiled=True)  12.8 us
    pallas_call x1, Pallas kernels, solve_poisson(): pl.pallas_call(functools.partial(interface_kernel, plan), out_shape=shape...  10.1 us
    ppermute x4, starting transfers between devices, shifted(): lax.ppermute(block, axis, [(i, (i + step) % count) for i in range(count)])  8.01 us
  transfers between devices with their start and end apart: 7, of which 5 were waited for; matrix products, arithmetic and copies ran while one was open for 1% of the time, Pallas kernels for 14%

profile of v1, /device:TPU:0, one launch (start us, length us, event | category | flops | bytes accessed | tf_op | source)
XLA Modules:
  0.0 144.6 jit_solution(2416937335798576078)
XLA Ops:
  0.6 1.3 copy.33.coords
  1.9 1.5 %prepare_atoms.1 = (f32[8,1,2048]{2,1,0:T(1,128)}, f32[1,5,1024]{2,1,0:T(8,128)}) custom-call(s32[1,32]{1,0:T(1,128)} %bitcast.15, s32[1,32]{1,0:T(1,128)} %bitcast.17, f32[16]{0:T(128)} %type_radius.1, f32[1,1,3,1024]{3,2,1,0:T(4,128)} %copy.33.coords, f32[1,1,1024]{2,1,0:T(1,128)} %charge.1, s32[1,1,1024]{2,1,0:T(1,128)} %types.1, s32[1,1,1024]{2,1,0:T(1,128)} %cells.1), custom_call_target="tpu_custom_call" | custom-call | tf_op jit(solution)/shard_map/prepare_atoms/pallas_call | solution.py:893
  3.5 5.2 %all-to-all-start = ((f32[8,1,2048]{2,1,0:T(1,128)}), f32[8,1,2048]{2,1,0:T(1,128)S(1)}, u32[]{:S(2)}, u32[]{:S(2)}) async-start(f32[8,1,2048]{2,1,0:T(1,128)} %get-tuple-element.10), calls=%async_computation | async-start | bytes 131072 | tf_op jit(solution)/shard_map/all_to_all | solution.py:909
  8.7 5.0 %all-to-all-done = f32[8,1,2048]{2,1,0:T(1,128)S(1)} async-done(((f32[8,1,2048]{2,1,0:T(1,128)}), f32[8,1,2048]{2,1,0:T(1,128)S(1)}, u32[]{:S(2)}, u32[]{:S(2)}) %all-to-all-start) | async-done | bytes 65568 | tf_op jit(solution)/shard_map/all_to_all | solution.py:909
  13.7 0.6 copy.39
  14.3 0.0 copy-start.2
  14.3 0.0 copy-start.5
  14.3 18.3 %forward_solve.1 = (f32[36,72,384]{2,1,0:T(8,128)}, s32[8,2048]{1,0:T(8,128)}, f32[288,1,256]{2,1,0:T(1,128)}) custom-call(s32[1]{0:T(128)} %bitcast.first_code, f32[8,2048]{1,0:T(8,128)} %bitcast.11, f32[36,72,288]{2,1,0:T(8,128)} %density_hbm.1, bf16[1152,384]{1,0:T(8,128)(2,1)} %constant.51.clone.z_table_hbm, bf16[72,216]{1,0:T(8,128)(2,1)} %constant.52.clone.y_table_hbm, ...), custom_call_target="tpu_custom_call" | custom-call | tf_op jit(solution)/shard_map/forward_solve/pallas_call | solution.py:768
  32.7 13.9 %all-to-all-start.1 = ((f32[288,1,256]{2,1,0:T(1,128)}), f32[288,1,256]{2,1,0:T(1,128)S(1)}, u32[]{:S(2)}, u32[]{:S(2)}) async-start(f32[288,1,256]{2,1,0:T(1,128)} %get-tuple-element.13), calls=%async_computation.1 | async-start | bytes 589824 | tf_op jit(solution)/shard_map/all_to_all | solution.py:799
  46.6 0.0 copy-done.2
  46.6 0.3 collective-permute-start
  46.9 2.4 %collective-permute-start.1 = (f32[1,5,1024]{2,1,0:T(8,128)S(1)}, f32[1,5,1024]{2,1,0:T(8,128)S(1)}, u32[]{:S(2)}, u32[]{:S(2)}) collective-permute-start(f32[1,5,1024]{2,1,0:T(8,128)S(1)} %copy-done.2), channel_id=1, source_target_pairs={{0,28},{4,0},{8,4},{12,8},{16,12},{20,16},{24,20},{28,24},{1,29},{... | collective-permute-start | bytes 61448 | tf_op jit(solution)/shard_map/ppermute | solution.py:873
  49.3 2.1 %collective-permute-done = f32[1,5,1024]{2,1,0:T(8,128)S(1)} collective-permute-done((f32[1,5,1024]{2,1,0:T(8,128)S(1)}, f32[1,5,1024]{2,1,0:T(8,128)S(1)}, u32[]{:S(2)}, u32[]{:S(2)}) %collective-permute-start) | collective-permute-done | bytes 20512 | tf_op jit(solution)/shard_map/ppermute | solution.py:873
  51.4 0.0 collective-permute-done.1
  51.4 0.0 copy-start.3
  51.4 5.3 %collective-permute-start.3 = (f32[3,5,1024]{2,1,0:T(8,128)S(1)}, f32[3,5,1024]{2,1,0:T(8,128)S(1)}, u32[]{:S(2)}, u32[]{:S(2)}) collective-permute-start(f32[3,5,1024]{2,1,0:T(8,128)S(1)} %constant_dynamic-update-slice_fusion.middle), channel_id=1, source_target_pairs={{0,3},{1,0},{2,1},{3,2},{4,7},{5,4},{6,5},{7,6},{8,11},{9,8},{10,9... | collective-permute-start | bytes 184328 | tf_op jit(solution)/shard_map/ppermute | solution.py:873
  56.7 0.0 collective-permute-start.2
  56.7 0.0 copy-done.5
  56.7 0.7 copy.36
  57.4 1.9 %collective-permute-done.3.high = f32[3,5,1024]{2,1,0:T(8,128)S(1)} collective-permute-done((f32[3,5,1024]{2,1,0:T(8,128)S(1)}, f32[3,5,1024]{2,1,0:T(8,128)S(1)}, u32[]{:S(2)}, u32[]{:S(2)}) %collective-permute-start.3) | collective-permute-done | bytes 61472 | tf_op jit(solution)/shard_map/ppermute | solution.py:873
  59.3 0.0 copy-start.6
  59.3 3.8 %collective-permute-done.2.low = f32[3,5,1024]{2,1,0:T(8,128)S(1)} collective-permute-done((f32[3,5,1024]{2,1,0:T(8,128)S(1)}, f32[3,5,1024]{2,1,0:T(8,128)S(1)}, u32[]{:S(2)}, u32[]{:S(2)}) %collective-permute-start.2) | collective-permute-done | bytes 61472 | tf_op jit(solution)/shard_map/ppermute | solution.py:873
  63.1 0.0 copy-start.7
  63.2 0.0 copy-done.3
  63.2 0.0 copy-done.6
  63.2 0.6 copy-done.7
  63.8 20.6 %pair_forces.1.earlier_hbm = f32[3,1024]{1,0:T(4,128)} custom-call(s32[32,3]{1,0:T(8,128)} %bitcast.14, f32[3,5,1024]{2,1,0:T(8,128)} %copy-done.7, f32[3,5,1024]{2,1,0:T(8,128)} %copy-done.3, f32[3,5,1024]{2,1,0:T(8,128)} %copy-done.6), custom_call_target="tpu_custom_call" | custom-call | flops 66060288 | bytes 204800 | tf_op jit(solution)/shard_map/pair_forces/pallas_call | solution.py:917
  84.4 0.0 all-to-all-done.1.incoming_hbm
  84.4 0.0 copy-start
  84.4 0.7 copy-done
  85.1 10.1 %interface_solve.1 = f32[288,1,256]{2,1,0:T(1,128)} custom-call(s32[1]{0:T(128)} %bitcast.3.first_mode, f32[288]{0:T(512)} %constant.56.clone.stiff_z, f32[3,1024]{1,0:T(4,128)} %pair_forces.1.earlier_hbm, f32[288,1,256]{2,1,0:T(1,128)} %copy-done, bf16[96,192]{1,0:T(8,128)(2,1)} %constant.57.clone.gather_hbm, bf16[1536,384]{1,0:T(8,128)(2,1)} %constant.58.clone.along_y_hbm, ...), custom_call_target="tpu_custom_call" | custom-call | tf_op jit(solution)/shard_map/interface_solve/pallas_call | solution.py:822
  95.2 13.9 %all_to_all.24.message_hbm = f32[288,1,256]{2,1,0:T(1,128)} all-to-all(f32[288,1,256]{2,1,0:T(1,128)} %interface_solve.1), channel_id=1, replica_groups=mesh['gx'=8,'gy'=4] {'gx','gy'}, dimensions={0} | all-to-all | bytes 589824 | tf_op jit(solution)/shard_map/all_to_all | solution.py:839
  109.1 0.0 copy-start.1
  109.1 0.0 copy-start.4
  109.1 16.4 %backward_solve.1 = (f32[36,72,288]{2,1,0:T(8,128)}, f32[256,128]{1,0:T(8,128)}) custom-call(s32[8,2048]{1,0:T(8,128)} %get-tuple-element.11.places_hbm, f32[288,1,256]{2,1,0:T(1,128)} %all_to_all.24.message_hbm, bf16[384,768]{1,0:T(8,128)(2,1)} %constant.67.clone.interface_hbm, f32[72,384]{1,0:T(8,128)} %constant.53.clone.diagonal_hbm, ...), custom_call_target="tpu_custom_call" | custom-call | tf_op jit(solution)/shard_map/backward_solve/pallas_call | solution.py:840
  125.5 12.8 %all-to-all-start.3 = ((f32[8,32,128]{2,1,0:T(8,128)}), f32[8,32,128]{2,1,0:T(8,128)S(1)}, u32[]{:S(2)}, u32[]{:S(2)}) async-start(f32[8,32,128]{2,1,0:T(8,128)} %bitcast.12), calls=%async_computation.3 | async-start | bytes 262144 | tf_op jit(solution)/shard_map/all_to_all | solution.py:938
  138.3 0.0 copy-done.1
  138.3 0.6 copy.35
  138.9 4.9 %all-to-all-done.3 = f32[8,32,128]{2,1,0:T(8,128)S(1)} async-done(((f32[8,32,128]{2,1,0:T(8,128)}), f32[8,32,128]{2,1,0:T(8,128)S(1)}, u32[]{:S(2)}, u32[]{:S(2)}) %all-to-all-start.3) | async-done | bytes 131104 | tf_op jit(solution)/shard_map/all_to_all | solution.py:938
  143.9 0.0 copy-done.4
  143.9 0.1 slice_select_fusion
  143.9 0.7 reshape.42
  (4 shorter events, 0.0 us)
Async XLA Ops:
  3.5 10.2 %all-to-all-start = ((f32[8,1,2048]{2,1,0:T(1,128)}), f32[8,1,2048]{2,1,0:T(1,128)S(1)}, u32[]{:S(2)}, u32[]{:S(2)}) async-start(f32[8,1,2048]{2,1,0:T(1,128)} %get-tuple-element.10), calls=%async_computation | async-start | bytes 131072 | tf_op jit(solution)/shard_map/all_to_all | solution.py:909
  14.3 32.3 %copy-start.2 = (f32[1,5,1024]{2,1,0:T(8,128)S(1)}, f32[1,5,1024]{2,1,0:T(8,128)}, u32[]{:S(2)}) copy-start(f32[1,5,1024]{2,1,0:T(8,128)} %get-tuple-element.12) | copy-start | bytes 61444
  14.3 42.4 %copy-start.5 = (s32[1,1,32,3]{2,1,3,0:T(1,128)S(1)}, s32[1,1,32,3]{2,1,3,0:T(1,128)}, u32[]{:S(2)}) copy-start(s32[1,1,32,3]{2,1,3,0:T(1,128)} %param.34) | copy-start | bytes 1156
  32.7 51.7 %all-to-all-start.1 = ((f32[288,1,256]{2,1,0:T(1,128)}), f32[288,1,256]{2,1,0:T(1,128)S(1)}, u32[]{:S(2)}, u32[]{:S(2)}) async-start(f32[288,1,256]{2,1,0:T(1,128)} %get-tuple-element.13), calls=%async_computation.1 | async-start | bytes 589824 | tf_op jit(solution)/shard_map/all_to_all | solution.py:799
  46.6 4.8 %collective-permute-start = (f32[1,5,1024]{2,1,0:T(8,128)S(1)}, f32[1,5,1024]{2,1,0:T(8,128)S(1)}, u32[]{:S(2)}, u32[]{:S(2)}) collective-permute-start(f32[1,5,1024]{2,1,0:T(8,128)S(1)} %copy-done.2), channel_id=1, source_target_pairs={{0,4},{4,8},{8,12},{12,16},{16,20},{20,24},{24,28},{28,0},{1,5},{5... | collective-permute-start | bytes 61448 | tf_op jit(solution)/shard_map/ppermute | solution.py:873
  46.9 4.5 %collective-permute-start.1 = (f32[1,5,1024]{2,1,0:T(8,128)S(1)}, f32[1,5,1024]{2,1,0:T(8,128)S(1)}, u32[]{:S(2)}, u32[]{:S(2)}) collective-permute-start(f32[1,5,1024]{2,1,0:T(8,128)S(1)} %copy-done.2), channel_id=1, source_target_pairs={{0,28},{4,0},{8,4},{12,8},{16,12},{20,16},{24,20},{28,24},{1,29},{... | collective-permute-start | bytes 61448 | tf_op jit(solution)/shard_map/ppermute | solution.py:873
  51.4 11.7 %copy-start.3 = (f32[3,5,1024]{2,1,0:T(8,128)}, f32[3,5,1024]{2,1,0:T(8,128)S(1)}, u32[]{:S(2)}) copy-start(f32[3,5,1024]{2,1,0:T(8,128)S(1)} %constant_dynamic-update-slice_fusion.middle) | copy-start | bytes 184324
  51.4 7.9 %collective-permute-start.3 = (f32[3,5,1024]{2,1,0:T(8,128)S(1)}, f32[3,5,1024]{2,1,0:T(8,128)S(1)}, u32[]{:S(2)}, u32[]{:S(2)}) collective-permute-start(f32[3,5,1024]{2,1,0:T(8,128)S(1)} %constant_dynamic-update-slice_fusion.middle), channel_id=1, source_target_pairs={{0,3},{1,0},{2,1},{3,2},{4,7},{5,4},{6,5},{7,6},{8,11},{9,8},{10,9... | collective-permute-start | bytes 184328 | tf_op jit(solution)/shard_map/ppermute | solution.py:873
  56.7 6.4 %collective-permute-start.2 = (f32[3,5,1024]{2,1,0:T(8,128)S(1)}, f32[3,5,1024]{2,1,0:T(8,128)S(1)}, u32[]{:S(2)}, u32[]{:S(2)}) collective-permute-start(f32[3,5,1024]{2,1,0:T(8,128)S(1)} %constant_dynamic-update-slice_fusion.middle), channel_id=1, source_target_pairs={{0,1},{1,2},{2,3},{3,0},{4,5},{5,6},{6,7},{7,4},{8,9},{9,10},{10,1... | collective-permute-start | bytes 184328 | tf_op jit(solution)/shard_map/ppermute | solution.py:873
  59.3 3.8 %copy-start.6 = (f32[3,5,1024]{2,1,0:T(8,128)}, f32[3,5,1024]{2,1,0:T(8,128)S(1)}, u32[]{:S(2)}) copy-start(f32[3,5,1024]{2,1,0:T(8,128)S(1)} %collective-permute-done.3.high) | copy-start | bytes 184324
  63.1 0.6 copy-start.7
  84.4 0.7 copy-start
  109.1 29.2 %copy-start.1 = (f32[3,1024]{1,0:T(4,128)S(1)}, f32[3,1024]{1,0:T(4,128)}, u32[]{:S(2)}) copy-start(f32[3,1024]{1,0:T(4,128)} %pair_forces.1.earlier_hbm) | copy-start | bytes 36868
  109.1 34.8 %copy-start.4 = (s32[1,1,32]{2,1,0:T(1,128)S(1)}, s32[1,1,32]{2,1,0:T(1,128)}, u32[]{:S(2)}) copy-start(s32[1,1,32]{2,1,0:T(1,128)} %param.32) | copy-start | bytes 388
  125.5 18.4 %all-to-all-start.3 = ((f32[8,32,128]{2,1,0:T(8,128)}), f32[8,32,128]{2,1,0:T(8,128)S(1)}, u32[]{:S(2)}, u32[]{:S(2)}) async-start(f32[8,32,128]{2,1,0:T(8,128)} %bitcast.12), calls=%async_computation.3 | async-start | bytes 262144 | tf_op jit(solution)/shard_map/all_to_all | solution.py:938

commit v2 on v1

--- a/solution.py
+++ b/solution.py
@@ -11,7 +11,6 @@
 
 SCREENING = 0.003
 HIGH_ACCURACY = lax.Precision.HIGHEST
-COPIES = 4
 VMEM_MIB = 60
 MIB = 1024 * 1024
 
@@ -152,6 +151,13 @@
     return jnp.concatenate([high, high, value - high], axis=axis).astype(jnp.bfloat16)
 
 
+def split_table(source, target, axis):
+    value = source[...]
+    high = value.astype(jnp.bfloat16).astype(jnp.float32)
+    parts = jnp.concatenate([high, value - high, high], axis=axis)
+    target[...] = parts.astype(jnp.bfloat16)
+
+
 def left_apply(table, value):
     return dot(table, value_triple(value, 0))
 
@@ -207,27 +213,70 @@
     return lax.fori_loop(0, count // unroll, group, init)
 
 
+def mark_places(plan, codes, first_code, place_rows, tile_atoms, block_atoms):
+    lane = lax.broadcasted_iota(jnp.int32, (codes.shape[0], 128), 1) % block_atoms
+    for start in range(0, tile_atoms, 128):
+        lanes = slice(start, start + 128)
+        code = codes[:, lanes].astype(jnp.int32) - first_code
+        place = lax.shift_right_arithmetic(code, 7)
+        shared = jnp.zeros_like(place)
+        for step in range(1, block_atoms):
+            same = (pltpu.roll(place, step, 1) == place) & (lane >= step)
+            shared = jnp.where(same, 1, shared)
+        step = block_atoms // 2
+        while step:
+            shared = shared | pltpu.roll(shared, 128 - step, 1)
+            step //= 2
+        place_rows[:, lanes] = place
+        mark = jnp.where(lane == 0, shared * 128, 0)
+        place_rows[:, tile_atoms + start : tile_atoms + start + 128] = (code & 127) + mark
+
+
 def forward_kernel(
     plan,
     n_blocks,
     block_atoms,
     first_code,
-    codes_hbm,
-    density_hbm,
-    z_table_hbm,
-    y_table_hbm,
-    diagonal_hbm,
-    edge_y_hbm,
-    interface_hbm,
-    spectrum_hbm,
-    places_hbm,
-    message,
-    *scratch,
+    *refs,
 ):
-    added = scratch[:COPIES]
-    solved, factors, stack, heads, edge_rows, turned = scratch[COPIES : COPIES + 6]
-    codes, density, z_table, y_table, diagonal, edge_y, interface = scratch[COPIES + 6 : COPIES + 13]
-    spectrum, place_rows, places, charges, blocks, sems = scratch[COPIES + 13 :]
+    (
+        codes_hbm,
+        density_hbm,
+        z_full_hbm,
+        y_table_hbm,
+        diagonal_hbm,
+        edge_y_hbm,
+        interface_hbm,
+        _,
+        _,
+        spectrum_hbm,
+        places_hbm,
+        message,
+        added,
+        solved,
+        factors,
+        stack,
+        heads,
+        edge_rows,
+        turned,
+        codes_in,
+        codes,
+        density,
+        z_full,
+        z_table,
+        y_table,
+        diagonal,
+        edge_y,
+        interface_full,
+        interface,
+        spectrum,
+        place_rows,
+        charge_rows,
+        places,
+        charges,
+        blocks,
+        sems,
+    ) = refs
     x_len, y_len, y_pad, x_pad = plan.x_len, plan.y_len, plan.y_pad, plan.x_pad
     grid, lane_count, planes = plan.grid, plan.lanes, plan.planes
     slabs = slab_count(plan)
@@ -235,21 +284,23 @@
     lane_ids = lax.broadcasted_iota(jnp.int32, (1, 128), 1)
     loads = start_copies(
         [
-            (codes_hbm, codes),
-            (codes_hbm.at[:, pl.ds(tile_atoms, tile_atoms)], charges),
+            (codes_hbm, codes_in),
             (density_hbm, density),
-            (z_table_hbm, z_table),
+            (z_full_hbm, z_full),
             (y_table_hbm, y_table),
             (diagonal_hbm, diagonal),
             (edge_y_hbm, edge_y),
-            (interface_hbm, interface),
+            (interface_hbm, interface_full),
         ],
         sems,
     )
     loads[0].wait()
-    code = codes[:, :tile_atoms].astype(jnp.int32) - first_code[0]
-    place_rows[:, :tile_atoms] = lax.shift_right_arithmetic(code, 7)
-    place_rows[:, tile_atoms:] = code & 127
+    for source in range(plan.n_gx):
+        codes[source : source + 1, :] = codes_in[source, :, :tile_atoms]
+        charge_rows[source : source + 1, :] = codes_in[source, :, tile_atoms:]
+    charge_copy = pltpu.make_async_copy(charge_rows, charges, sems.at[7])
+    charge_copy.start()
+    mark_places(plan, codes, first_code[0], place_rows, tile_atoms, block_atoms)
     place_copies = [
         pltpu.make_async_copy(place_rows, places, sems.at[8]),
         pltpu.make_async_copy(place_rows, places_hbm, sems.at[9]),
@@ -258,14 +309,14 @@
         copy.start()
 
     def clear(step, carry):
-        for copy in added:
-            copy[pl.ds(pl.multiple_of(step * y_pad, 8), y_pad), :] = jnp.zeros(
-                (y_pad, 128), jnp.float32
-            )
+        place = pl.ds(pl.multiple_of(step * y_pad, 8), y_pad)
+        added[place, :] = jnp.zeros((y_pad, 128), jnp.float32)
         return carry
 
     chunked_loop(plan.lane_tiles * x_len, 4, clear, 0)
-    loads[1].wait()
+    loads[2].wait()
+    split_table(z_full, z_table, 0)
+    charge_copy.wait()
     place_copies[0].wait()
     count = list_owned(plan, places, blocks, n_blocks, block_atoms)
 
@@ -273,20 +324,32 @@
         block = blocks[slot]
         source = block // n_blocks
         start = (block - source * n_blocks) * block_atoms
-        for lead in range(0, block_atoms, COPIES):
-            rows = [pl.ds(places[source, start + lead + k], 1) for k in range(COPIES)]
-            sums = []
-            for k in range(COPIES):
-                lane = places[source, start + lead + k + tile_atoms]
-                charge = charges[source, start + lead + k]
-                sums.append(added[k][rows[k], :] + jnp.where(lane_ids == lane, charge, 0.0))
-            for k in range(COPIES):
-                added[k][rows[k], :] = sums[k]
+        lead = places[source, start + tile_atoms]
+
+        def row_of(k):
+            return pl.ds(places[source, start + k], 1)
+
+        def raised(k):
+            lane = places[source, start + k + tile_atoms] & 127
+            hit = jnp.where(lane_ids == lane, charges[source, start + k], 0.0)
+            return added[row_of(k), :] + hit
+
+        @pl.when(lead < 128)
+        def _():
+            rows = [raised(k) for k in range(block_atoms)]
+            for k in range(block_atoms):
+                added[row_of(k), :] = rows[k]
+
+        @pl.when(lead >= 128)
+        def _():
+            for k in range(block_atoms):
+                added[row_of(k), :] = raised(k)
+
         return carry
 
     lax.fori_loop(0, count, deposit, 0)
-    for copy in loads[2:5]:
-        copy.wait()
+    loads[1].wait()
+    loads[3].wait()
 
     def transform(step, carry):
         start = step * slabs
@@ -305,9 +368,7 @@
                 rest = jnp.zeros((count, 128 - width), jnp.float32)
                 piece = jnp.concatenate([piece, rest], axis=1)
             place = pl.ds(pl.multiple_of(tile * planes + start * y_pad, 8), count)
-            for copy in added:
-                piece = piece + copy[place, :]
-            pieces.append(piece)
+            pieces.append(piece + added[place, :])
         lines = right_apply(jnp.concatenate(pieces, axis=1), z_table[...])
         lines = lines.reshape(slabs, y_pad, lane_count)
         for slab in range(slabs):
@@ -325,8 +386,9 @@
     chunked_loop(x_len // slabs, 3, transform, 0)
     spectrum_copy = pltpu.make_async_copy(spectrum, spectrum_hbm, sems.at[10])
     spectrum_copy.start()
-    for copy in loads[5:8]:
+    for copy in loads[4:]:
         copy.wait()
+    split_table(interface_full, interface, 0)
     stack[3 * y_pad :, :] = jnp.zeros((stack.shape[0] - 3 * y_pad, lane_count), jnp.float32)
     for tile in range(plan.lane_tiles):
         lanes = slice(tile * 128, tile * 128 + 128)
@@ -372,7 +434,7 @@
     plan,
     first_mode,
     stiff_z,
-    earlier_hbm,
+    _,
     incoming_hbm,
     gather_hbm,
     along_y_hbm,
@@ -381,8 +443,6 @@
     expand_back_hbm,
     stiff_x_hbm,
     stiff_y_hbm,
-    along_y_back_hbm,
-    along_x_back_hbm,
     scatter_hbm,
     outgoing,
     rows,
@@ -391,29 +451,29 @@
     lines,
     incoming,
     gather,
-    along_y,
-    along_x,
+    along_y_full,
+    along_x_full,
     expand,
     expand_back,
     stiff_x,
     stiff_y,
+    scatter,
+    along_y,
+    along_x,
     along_y_back,
     along_x_back,
-    scatter,
     sems,
 ):
     loads = start_copies(
         [
             (incoming_hbm, incoming),
             (gather_hbm, gather),
-            (along_y_hbm, along_y),
-            (along_x_hbm, along_x),
+            (along_y_hbm, along_y_full),
+            (along_x_hbm, along_x_full),
             (expand_hbm, expand),
             (expand_back_hbm, expand_back),
             (stiff_x_hbm, stiff_x),
             (stiff_y_hbm, stiff_y),
-            (along_y_back_hbm, along_y_back),
-            (along_x_back_hbm, along_x_back),
             (scatter_hbm, scatter),
         ],
         sems,
@@ -445,7 +505,9 @@
         )
 
     loads[2].wait()
+    split_table(along_y_full, along_y, 0)
     loads[3].wait()
+    split_table(along_x_full, along_x, 0)
     folded_y[...] = right_apply(side_by_side(y_slots, kx_pad), along_y[...]).reshape(
         modes, kx_pad, lane_count
     )
@@ -469,12 +531,15 @@
     for copy in loads[4:8]:
         copy.wait()
     chunked_loop(modes, 3, solve, 0)
-    for copy in loads[8:]:
-        copy.wait()
-    all_y = right_apply(folded_y[...].reshape(modes * kx_pad, lane_count), along_y_back[...])
+    loads[8].wait()
+    split_table(along_y_full, along_y_back, 1)
+    split_table(along_x_full, along_x_back, 1)
+    all_y = folded_y[...].reshape(modes * kx_pad, lane_count)
+    all_y = dot(value_triple(all_y, 1), along_y_back[...], ((1,), (1,)))
     for j, slot in enumerate(y_slots):
         lines[:, slot, :] = all_y[:, j * half : (j + 1) * half].reshape(modes, kx_pad, half)
-    all_x = right_apply(folded_x[...].reshape(modes * j_pad, lane_count), along_x_back[...])
+    all_x = folded_x[...].reshape(modes * j_pad, lane_count)
+    all_x = dot(value_triple(all_x, 1), along_x_back[...], ((1,), (1,)))
     for i, slot in enumerate(x_slots):
         lines[:, slot, :] = all_x[:, i * half : (i + 1) * half].reshape(modes, j_pad, half)
     for mode in range(modes):
@@ -500,7 +565,8 @@
     edge_y_hbm,
     spectrum_hbm,
     y_table_hbm,
-    z_table_hbm,
+    z_full_hbm,
+    _,
     potential_hbm,
     values,
     lookup,
@@ -515,11 +581,13 @@
     potential,
     places,
     message,
+    interface_full,
     interface,
     diagonal,
     edge_y,
     spectrum,
     y_table,
+    z_full,
     z_table,
     blocks,
     sems,
@@ -531,13 +599,13 @@
     loads = start_copies(
         [
             (message_hbm, message),
-            (interface_hbm, interface),
+            (interface_hbm, interface_full),
             (places_hbm, places),
             (diagonal_hbm, diagonal),
             (edge_y_hbm, edge_y),
             (spectrum_hbm, spectrum),
             (y_table_hbm, y_table),
-            (z_table_hbm, z_table),
+            (z_full_hbm, z_full),
         ],
         sems,
     )
@@ -547,11 +615,13 @@
     if lane_count > grid:
         turned[grid:, :] = jnp.zeros((lane_count - grid, turned.shape[1]), jnp.float32)
     loads[1].wait()
+    split_table(interface_full, interface, 1)
     stack[...] = dot(interface[...], value_triple(turned[...], 1), ((1,), (1,)))
     loads[2].wait()
     count = list_owned(plan, places, blocks, n_blocks, block_atoms)
     for copy in loads[3:]:
         copy.wait()
+    split_table(z_full, z_table, 0)
     for tile in range(plan.lane_tiles):
         lanes = slice(tile * 128, tile * 128 + 128)
         near_weight = edge_y[0]
@@ -618,10 +688,14 @@
         block = blocks[slot]
         source = block // n_blocks
         start = (block - source * n_blocks) * block_atoms
-        for atom in range(block_atoms):
-            row = lookup[pl.ds(places[source, start + atom], 1), :]
-            lane = places[source, start + atom + tile_atoms]
-            picked[atom : atom + 1, :] = jnp.where(lane_ids == lane, row, 0.0)
+        for first in range(0, block_atoms, 16):
+            rows = []
+            for atom in range(first, first + 16):
+                row = lookup[pl.ds(places[source, start + atom], 1), :]
+                lane = places[source, start + atom + tile_atoms] & 127
+                rows.append(jnp.where(lane_ids == lane, row, 0.0))
+            for k in range(16):
+                picked[first + k : first + k + 1, :] = rows[k]
         found = jnp.sum(picked[...], axis=1, keepdims=True)
         found = jnp.sum(jnp.where(own_lane, found, 0.0), axis=0, keepdims=True)
         values[pl.ds(block, 1), :] = found
@@ -662,15 +736,18 @@
         radius = jnp.zeros((1, 128), jnp.float32)
         for kind in range(type_radius.shape[0]):
             radius = jnp.where(types[0, :, lanes] == kind, type_radius[kind], radius)
-        atom_rows[0, 0:3, lanes] = coords[0, 0, :, lanes]
+        atom_rows[0, 0:3, lanes] = coords[0, :, 0, lanes]
         atom_rows[0, 3:4, lanes] = live
         atom_rows[0, 4:5, lanes] = radius
 
 
 def pair_kernel(
-    n_blocks, block_atoms, listed, listing, low, middle, high, forces, table, columns, results
+    n_blocks, block_atoms, listed, part, n_parts, listing, low, middle, high, earlier, forces,
+    table, columns, results,
 ):
     tile_atoms = n_blocks * block_atoms
+    part_atoms = tile_atoms // n_parts
+    first = part * part_atoms
     sides = (low, middle, high)
     for step_x in range(3):
         for step_y in range(3):
@@ -681,50 +758,47 @@
                 if shifts[k]:
                     row = row + shifts[k]
                 table[step_x * 3 + step_y, k] = jnp.broadcast_to(row, (8, tile_atoms))
-    columns[0:5, :] = middle[1]
-    columns[5:, :] = jnp.zeros((columns.shape[0] - 5, tile_atoms), jnp.float32)
+    columns[0:5, :] = middle[1, :, first : first + part_atoms]
+    columns[5:, :] = jnp.zeros((columns.shape[0] - 5, part_atoms), jnp.float32)
     results[...] = jnp.transpose(columns[...])
-    lane_ids = lax.broadcasted_iota(jnp.int32, (block_atoms, 128), 1)
-    groups = block_atoms // 8
-
-    def block(number, carry):
-        place = pl.ds(pl.multiple_of(number * block_atoms, block_atoms), block_atoms)
+    lane_ids = lax.broadcasted_iota(jnp.int32, (16, 128), 1)
+
+    def group(number, carry):
+        place = pl.ds(pl.multiple_of(number * 16, 16), 16)
+        block = (first + number * 16) // block_atoms
         own = results[place, :]
         mine = [
-            jnp.broadcast_to(own[:, k : k + 1], (block_atoms, 128)).reshape(groups, 8, 128)
-            for k in range(5)
+            jnp.broadcast_to(own[:, k : k + 1], (16, 128)).reshape(2, 8, 128)
+            for k in (0, 1, 2, 4)
         ]
-        zero = jnp.zeros((groups, 8, 128), jnp.float32)
-
-        def tile(slot, sums):
-            force_x, force_y, force_z = sums
-            which = listing[number, slot]
+        force_x = force_y = force_z = jnp.zeros((2, 8, 128), jnp.float32)
+        for slot in range(listed):
+            which = listing[0, slot, 0, block]
             for start in range(0, tile_atoms, 128):
                 lanes = slice(start, start + 128)
-                other = [table[which, k, :, lanes][None] for k in range(5)]
-                sep_x = mine[0] - other[0]
-                sep_y = mine[1] - other[1]
-                sep_z = mine[2] - other[2]
-                reach = mine[4] + other[4]
+                sep_x = mine[0] - table[which, 0, :, lanes][None]
+                sep_y = mine[1] - table[which, 1, :, lanes][None]
+                sep_z = mine[2] - table[which, 2, :, lanes][None]
+                reach = mine[3] + table[which, 4, :, lanes][None]
                 root = lax.rsqrt(sep_x * sep_x + sep_y * sep_y + sep_z * sep_z + reach * reach)
-                strength = other[3] * root * (root * root)
+                strength = table[which, 3, :, lanes][None] * root * (root * root)
                 force_x = force_x + strength * sep_x
                 force_y = force_y + strength * sep_y
                 force_z = force_z + strength * sep_z
-            return force_x, force_y, force_z
-
-        sums = lax.fori_loop(0, listed, tile, (zero, zero, zero))
-        out = jnp.zeros((block_atoms, 128), jnp.float32)
-        for axis in range(3):
-            total = sums[axis].reshape(block_atoms, 128)
-            force = own[:, 3:4] * jnp.sum(total, axis=1, keepdims=True)
+        out = jnp.zeros((16, 128), jnp.float32)
+        for axis, total in enumerate((force_x, force_y, force_z)):
+            force = own[:, 3:4] * jnp.sum(total.reshape(16, 128), axis=1, keepdims=True)
             out = jnp.where(lane_ids == axis, force, out)
         results[place, :] = out
         return carry
 
-    lax.fori_loop(0, n_blocks, block, 0)
+    lax.fori_loop(0, part_atoms // 16, group, 0)
     columns[...] = jnp.transpose(results[...])
-    forces[...] = columns[0:3, :]
+    if first:
+        for axis in range(3):
+            forces[axis, :, :first] = earlier[axis, :, :first]
+    for axis in range(3):
+        forces[axis, :, first : first + part_atoms] = columns[axis : axis + 1, :]
 
 
 VMEM = pl.BlockSpec(memory_space=pltpu.VMEM)
@@ -748,16 +822,16 @@
     return pltpu.CompilerParams(vmem_limit_bytes=mib * MIB)
 
 
-def solve_poisson(plan, density, codes, first_code, n_blocks, block_atoms, earlier):
+def solve_poisson(plan, density, codes, first_code, n_blocks, block_atoms, neighbours, pair_part):
     x_len, y_len, grid = density.shape
     y_pad, x_pad, half, lanes = plan.y_pad, plan.x_pad, plan.half, plan.lanes
     total = plan.parts * plan.modes
-    z_table = table_triple(plan.z_matrix(), 0)
+    z_full = f32(plan.z_matrix())
     y_table = table_triple(plan.y_matrix(), 1)
     diagonal = f32(plan.diagonal())
     edge_y = f32(plan.edge_weights())
-    interface = table_triple(plan.interface_table(), 0)
-    interface_back = table_triple(plan.interface_table(), 1)
+    interface = f32(plan.interface_table())
+    bf16 = jnp.bfloat16
     n_rows, tile_atoms = codes.shape[0], n_blocks * block_atoms
     shared = [
         buffer(x_len, y_pad, 128),
@@ -772,22 +846,26 @@
             jax.ShapeDtypeStruct((n_rows, 2 * tile_atoms), jnp.int32),
             shaped(total, 1, 2 * half),
         ),
-        in_specs=[SMEM] + [HBM] * 7,
+        in_specs=[SMEM] + [HBM] * 9,
         out_specs=(HBM, HBM, VMEM),
-        scratch_shapes=[buffer(plan.lane_tiles * plan.planes, 128)] * COPIES
+        scratch_shapes=[buffer(plan.lane_tiles * plan.planes, 128)]
         + shared
         + [
             buffer(2, x_pad, 128),
             buffer(lanes, 2 * half),
-            buffer(n_rows, 2 * tile_atoms),
+            buffer(n_rows, 1, 2 * tile_atoms),
+            buffer(n_rows, tile_atoms),
             buffer(x_len, y_len, grid),
-            like(z_table),
+            like(z_full),
+            pltpu.VMEM((3 * lanes, lanes), bf16),
             like(y_table),
             like(diagonal),
             like(edge_y),
             like(interface),
+            pltpu.VMEM((3 * plan.stack_rows, 2 * half), bf16),
             buffer(x_len, y_pad, lanes),
             pltpu.VMEM((n_rows, 2 * tile_atoms), jnp.int32),
+            buffer(n_rows, tile_atoms),
             pltpu.SMEM((n_rows, 2 * tile_atoms), jnp.int32),
             pltpu.SMEM((n_rows, tile_atoms), jnp.float32),
             pltpu.SMEM((n_rows * n_blocks,), jnp.int32),
@@ -795,7 +873,8 @@
         ],
         compiler_params=limit(VMEM_MIB),
         name="forward_solve",
-    )(first_code, codes, density, z_table, y_table, diagonal, edge_y, interface)
+    )(first_code, codes, density, z_full, y_table, diagonal, edge_y, interface, *neighbours)
+    first_pairs = pair_part(0, None)
     incoming = lax.all_to_all(message, ("gx", "gy"), split_axis=0, concat_axis=0, tiled=True)
     gather = plan.gather_table()
     along_y, along_x = plan.line_tables()
@@ -809,20 +888,18 @@
     padded_y[0, :grid] = stiff
     tables = [
         table_triple(gather, 1),
-        table_triple(along_y, 0),
-        table_triple(along_x, 0),
+        f32(along_y),
+        f32(along_x),
         f32(table_triple(expand, 0)),
         table_triple(expand, 1),
         f32(stiff[:, None] * grid),
         f32(padded_y * grid),
-        table_triple(along_y.T, 0),
-        table_triple(along_x.T, 0),
         table_triple(gather.T, 1),
     ]
     outgoing = pl.pallas_call(
         functools.partial(interface_kernel, plan),
         out_shape=shaped(total, 1, 2 * half),
-        in_specs=[SMEM] * 2 + [HBM] * 12,
+        in_specs=[SMEM] * 2 + [HBM] * 10,
         out_specs=VMEM,
         scratch_shapes=[
             buffer(plan.modes, 2 * plan.parts, half),
@@ -831,16 +908,21 @@
             buffer(plan.modes, gather.shape[0], half),
             buffer(total, 1, 2 * half),
             *[like(table) for table in tables],
-            pltpu.SemaphoreType.DMA((11,)),
+            pltpu.VMEM((3 * along_y.shape[0], lanes), bf16),
+            pltpu.VMEM((3 * along_x.shape[0], lanes), bf16),
+            pltpu.VMEM((along_y.shape[0], 3 * lanes), bf16),
+            pltpu.VMEM((along_x.shape[0], 3 * lanes), bf16),
+            pltpu.SemaphoreType.DMA((9,)),
         ],
         compiler_params=limit(VMEM_MIB),
         name="interface_solve",
-    )(first_mode, f32((padded_z + SCREENING) * grid), earlier, incoming, *tables)
+    )(first_mode, f32((padded_z + SCREENING) * grid), first_pairs, incoming, *tables)
     returned = lax.all_to_all(outgoing, ("gx", "gy"), split_axis=0, concat_axis=0, tiled=True)
-    return pl.pallas_call(
+    pair_force = pair_part(1, first_pairs)
+    potential, values = pl.pallas_call(
         functools.partial(backward_kernel, plan, n_blocks, block_atoms),
         out_shape=(shaped(x_len, y_len, grid), shaped(plan.n_gx * n_blocks, 128)),
-        in_specs=[HBM] * 8,
+        in_specs=[HBM] * 9,
         out_specs=(HBM, VMEM),
         scratch_shapes=[
             buffer(plan.lane_tiles * plan.planes, 128),
@@ -854,18 +936,21 @@
             buffer(x_len, y_len, grid),
             pltpu.SMEM((n_rows, 2 * tile_atoms), jnp.int32),
             buffer(total, 1, 2 * half),
-            like(interface_back),
+            like(interface),
+            pltpu.VMEM((plan.stack_rows, 6 * half), bf16),
             like(diagonal),
             like(edge_y),
             buffer(x_len, y_pad, lanes),
             like(y_table),
-            like(z_table),
+            like(z_full),
+            pltpu.VMEM((3 * lanes, lanes), bf16),
             pltpu.SMEM((n_rows * n_blocks,), jnp.int32),
             pltpu.SemaphoreType.DMA((9,)),
         ],
         compiler_params=limit(VMEM_MIB),
         name="backward_solve",
-    )(places, returned, interface_back, diagonal, edge_y, spectrum, y_table, z_table)
+    )(places, returned, interface, diagonal, edge_y, spectrum, y_table, z_full, pair_force)
+    return potential, values, pair_force
 
 
 def shifted(block, axis, step):
@@ -901,46 +986,51 @@
         block_counts.reshape(1, n_blocks),
         block_owner.reshape(1, n_blocks),
         type_radius,
-        mm_coords,
+        mm_coords.transpose(0, 2, 1, 3),
         mm_charge,
         mm_types,
         mm_cells,
     )
     codes = lax.all_to_all(copies, "gx", split_axis=0, concat_axis=0, tiled=True)
-    codes = codes.reshape(n_gx, 2 * tile_atoms)
     first_code = (lax.axis_index("gx") * plan.span).astype(jnp.int32).reshape(1)
     triple = jnp.concatenate(
         [shifted(atom_rows, "gx", 1), atom_rows, shifted(atom_rows, "gx", -1)], axis=0
     )
     below, above = shifted(triple, "gy", 1), shifted(triple, "gy", -1)
     listed = neighbour_tiles.shape[3]
-    pair_force = pl.pallas_call(
-        functools.partial(pair_kernel, n_blocks, block_atoms, listed),
-        out_shape=shaped(3, tile_atoms),
-        in_specs=[SMEM] + [VMEM] * 3,
-        out_specs=VMEM,
-        scratch_shapes=[
-            buffer(9, 5, 8, tile_atoms),
-            buffer(128, tile_atoms),
-            buffer(tile_atoms, 128),
-        ],
-        compiler_params=limit(VMEM_MIB),
-        cost_estimate=pl.CostEstimate(
-            flops=21 * listed * tile_atoms * tile_atoms,
-            bytes_accessed=4 * 50 * tile_atoms,
-            transcendentals=listed * tile_atoms * tile_atoms,
-        ),
-        name="pair_forces",
-    )(neighbour_tiles.reshape(n_blocks, listed), below, triple, above)
-    potential, values = solve_poisson(
-        plan, qm_density, codes, first_code, n_blocks, block_atoms, pair_force
+    listing = neighbour_tiles.transpose(0, 3, 1, 2)
+
+    def pair_part(part, earlier):
+        if earlier is None:
+            earlier = jnp.zeros((3, 1, 128), jnp.float32)
+        return pl.pallas_call(
+            functools.partial(pair_kernel, n_blocks, block_atoms, listed, part, 2),
+            out_shape=shaped(3, 1, (part + 1) * tile_atoms // 2),
+            in_specs=[SMEM] + [VMEM] * 4,
+            out_specs=VMEM,
+            scratch_shapes=[
+                buffer(9, 5, 8, tile_atoms),
+                buffer(128, tile_atoms // 2),
+                buffer(tile_atoms // 2, 128),
+            ],
+            compiler_params=limit(VMEM_MIB),
+            cost_estimate=pl.CostEstimate(
+                flops=10 * listed * tile_atoms * tile_atoms,
+                bytes_accessed=4 * 50 * tile_atoms,
+                transcendentals=listed * tile_atoms * tile_atoms // 2,
+            ),
+            name="pair_forces",
+        )(listing, below, triple, above, earlier)
+
+    potential, values, pair_force = solve_poisson(
+        plan, qm_density, codes, first_code, n_blocks, block_atoms, (below, above), pair_part
     )
     values = lax.all_to_all(values, "gx", split_axis=0, concat_axis=0, tiled=True)
     sampled = jnp.sum(values.reshape(n_gx, n_blocks, 128), axis=0)[:, :block_atoms]
     lanes = jnp.arange(block_atoms, dtype=jnp.int32)
     live = lanes[None, :] < block_counts.reshape(n_blocks, 1)
     mm_potential = jnp.where(live, sampled, 0.0).reshape(1, 1, tile_atoms)
-    return (potential, mm_potential, pair_force.reshape(1, 1, 3, tile_atoms))
+    return (potential, mm_potential, pair_force[None].transpose(0, 2, 1, 3))
 
 
 def solution(mesh):

time: 145 us -> 143 us (0.986)
  Pallas kernels: 66.9 us -> 102 us
  starting transfers between devices: 39.9 us -> 21.4 us
  waiting for transfers between devices: 17.8 us -> 6.76 us
  blocking collectives: 13.9 us -> 8.82 us
    pallas_call x1, Pallas kernels: 18.3 us -> 35.1 us  [solve_poisson(): pl.pallas_call(functools.partial(forward_kernel, plan, n_blocks, block_at...]
    pallas_call x1, Pallas kernels: 16.4 us -> 27.4 us  [solve_poisson(): pl.pallas_call(functools.partial(backward_kernel, plan, n_blocks, block_a...]
    all_to_all x1, starting transfers between devices: 13.9 us -> 4.27 us  [solve_poisson(): lax.all_to_all(message, ('gx', 'gy'), split_axis=0, concat_axis=0, tiled=...]
    pallas_call x1 -> x2, Pallas kernels: 20.6 us -> 27.8 us  [pair_part(): pl.pallas_call(functools.partial(pair_kernel, n_blocks, block_atoms, list...]
    all_to_all x1, starting transfers between devices: 12.8 us -> 6.02 us  [solve_poisson(): lax.all_to_all(outgoing, ('gx', 'gy'), split_axis=0, concat_axis=0, tiled...]
    ppermute x4, waiting for transfers between devices: 7.82 us -> 1.81 us  [shifted(): lax.ppermute(block, axis, [(i, (i + step) % count) for i in range(count)])]
    all_to_all x1, blocking collectives: 13.9 us -> 8.82 us  [body(): lax.all_to_all(values, 'gx', split_axis=0, concat_axis=0, tiled=True)]
    all_to_all x1, waiting for transfers between devices: 4.91 us -> 0.01 us  [solve_poisson(): lax.all_to_all(outgoing, ('gx', 'gy'), split_axis=0, concat_axis=0, tiled...]
  transfers between devices with their start and end apart: 7 -> 7, of which waited for: 5 -> 2; matrix products, arithmetic and copies ran while one was open for 1% -> 1% of each run, Pallas kernels for 14% -> 19%
where the time goes in v2:
time: 143 us; the launch traced here: 144 us
  Pallas kernels  102 us (71%)
  starting transfers between devices  21.4 us (15%)
  blocking collectives  8.82 us (6%)
  waiting for transfers between devices  6.76 us (5%)
  local copies, waits for them, and re-layouts  4.17 us (3%)
    pallas_call x1, Pallas kernels, solve_poisson(): pl.pallas_call(functools.partial(forward_kernel, plan, n_blocks, block_at...  35.1 us
    pallas_call x2, Pallas kernels, pair_part(): pl.pallas_call(functools.partial(pair_kernel, n_blocks, block_atoms, list...  27.8 us
    pallas_call x1, Pallas kernels, solve_poisson(): pl.pallas_call(functools.partial(backward_kernel, plan, n_blocks, block_a...  27.4 us
    pallas_call x1, Pallas kernels, solve_poisson(): pl.pallas_call(functools.partial(interface_kernel, plan), out_shape=shape...  10.2 us
    all_to_all x1, blocking collectives, body(): lax.all_to_all(values, 'gx', split_axis=0, concat_axis=0, tiled=True)  8.82 us
    ppermute x4, starting transfers between devices, shifted(): lax.ppermute(block, axis, [(i, (i + step) % count) for i in range(count)])  7.75 us
    all_to_all x1, starting transfers between devices, solve_poisson(): lax.all_to_all(outgoing, ('gx', 'gy'), split_axis=0, concat_axis=0, tiled...  6.02 us
    all_to_all x1, waiting for transfers between devices, body(): lax.all_to_all(copies, 'gx', split_axis=0, concat_axis=0, tiled=True)  4.94 us
  transfers between devices with their start and end apart: 7, of which 2 were waited for; matrix products, arithmetic and copies ran while one was open for 1% of the time, Pallas kernels for 19%

profile of v2, /device:TPU:0, one launch (start us, length us, event | category | flops | bytes accessed | tf_op | source)
XLA Modules:
  0.0 144.1 jit_solution(3684943011716754531)
XLA Ops:
  0.6 1.5 %prepare_atoms.1 = (f32[8,1,2048]{2,1,0:T(1,128)}, f32[1,5,1024]{2,1,0:T(8,128)}) custom-call(s32[1,32]{1,0:T(1,128)} %bitcast.14, s32[1,32]{1,0:T(1,128)} %bitcast.16, f32[16]{0:T(128)} %type_radius.1, f32[1,3,1,1024]{3,2,1,0:T(1,128)} %bitcast.13, f32[1,1,1024]{2,1,0:T(1,128)} %charge.1, s32[1,1,1024]{2,1,0:T(1,128)} %types.1, s32[1,1,1024]{2,1,0:T(1,128)} %cells.1), custom_call_target="tpu_custom_call" | custom-call | tf_op jit(solution)/shard_map/prepare_atoms/pallas_call | solution.py:978
  2.2 0.5 collective-permute-start
  2.6 2.9 %collective-permute-start.1 = (f32[1,5,1024]{2,1,0:T(8,128)}, f32[1,5,1024]{2,1,0:T(8,128)S(1)}, u32[]{:S(2)}, u32[]{:S(2)}) collective-permute-start(f32[1,5,1024]{2,1,0:T(8,128)} %get-tuple-element.11), channel_id=1, source_target_pairs={{0,28},{4,0},{8,4},{12,8},{16,12},{20,16},{24,20},{28,24},{1,29},{... | collective-permute-start | bytes 61448 | tf_op jit(solution)/shard_map/ppermute | solution.py:958
  5.5 1.8 %collective-permute-done = f32[1,5,1024]{2,1,0:T(8,128)S(1)} collective-permute-done((f32[1,5,1024]{2,1,0:T(8,128)}, f32[1,5,1024]{2,1,0:T(8,128)S(1)}, u32[]{:S(2)}, u32[]{:S(2)}) %collective-permute-start) | collective-permute-done | bytes 20512 | tf_op jit(solution)/shard_map/ppermute | solution.py:958
  7.3 0.8 constant_dynamic-update-slice_fusion.1
  8.1 0.0 collective-permute-done.1
  8.1 0.0 copy-start.5
  8.1 4.4 %collective-permute-start.3 = (f32[3,5,1024]{2,1,0:T(8,128)S(1)}, f32[3,5,1024]{2,1,0:T(8,128)S(1)}, u32[]{:S(2)}, u32[]{:S(2)}) collective-permute-start(f32[3,5,1024]{2,1,0:T(8,128)S(1)} %constant_dynamic-update-slice_fusion.middle), channel_id=1, source_target_pairs={{0,3},{1,0},{2,1},{3,2},{4,7},{5,4},{6,5},{7,6},{8,11},{9,8},{10,9... | collective-permute-start | bytes 184328 | tf_op jit(solution)/shard_map/ppermute | solution.py:958
  12.5 0.0 collective-permute-start.2
  12.5 3.4 %all-to-all-start = ((f32[8,1,2048]{2,1,0:T(1,128)}), f32[8,1,2048]{2,1,0:T(1,128)S(1)}, u32[]{:S(2)}, u32[]{:S(2)}) async-start(f32[8,1,2048]{2,1,0:T(1,128)} %get-tuple-element.10), calls=%async_computation | async-start | bytes 131072 | tf_op jit(solution)/shard_map/all_to_all | solution.py:994
  15.9 4.9 %all-to-all-done.refs_0_ = f32[8,1,2048]{2,1,0:T(1,128)S(1)} async-done(((f32[8,1,2048]{2,1,0:T(1,128)}), f32[8,1,2048]{2,1,0:T(1,128)S(1)}, u32[]{:S(2)}, u32[]{:S(2)}) %all-to-all-start) | async-done | bytes 65568 | tf_op jit(solution)/shard_map/all_to_all | solution.py:994
  20.8 0.0 copy-start.2
  20.8 0.0 collective-permute-done.3.refs_8_.high
  20.8 0.0 copy-start.3
  20.8 0.0 collective-permute-done.2.refs_7_.low
  20.8 0.0 copy-start.4
  20.8 0.6 copy-done.2
  21.4 0.0 copy-done.3
  21.5 0.1 copy-done.4
  21.6 35.1 %forward_solve.1 = (f32[36,72,384]{2,1,0:T(8,128)}, s32[8,2048]{1,0:T(8,128)}, f32[288,1,256]{2,1,0:T(1,128)}) custom-call(s32[1]{0:T(128)} %bitcast.first_code, f32[8,1,2048]{2,1,0:T(1,128)} %copy-done.2, f32[36,72,288]{2,1,0:T(8,128)} %refs_1_.1, f32[384,384]{1,0:T(8,128)} %constant.46.clone.refs_2_.z_full_hbm, ...), custom_call_target="tpu_custom_call" | custom-call | tf_op jit(solution)/shard_map/forward_solve/pallas_call | solution.py:842
  56.7 4.3 %all-to-all-start.1 = ((f32[288,1,256]{2,1,0:T(1,128)}), f32[288,1,256]{2,1,0:T(1,128)S(1)}, u32[]{:S(2)}, u32[]{:S(2)}) async-start(f32[288,1,256]{2,1,0:T(1,128)} %get-tuple-element.13), calls=%async_computation.1 | async-start | bytes 589824 | tf_op jit(solution)/shard_map/all_to_all | solution.py:878
  61.0 0.6 broadcast_in_dim.8.earlier
  61.5 0.0 copy-done.5
  61.5 13.9 %pair_forces.2._.earlier = f32[3,1,512]{2,1,0:T(1,128)} custom-call(s32[1,3,1,32]{3,2,1,0:T(1,128)} %bitcast.17, f32[3,5,1024]{2,1,0:T(8,128)} %copy-done.4, f32[3,5,1024]{2,1,0:T(8,128)} %copy-done.5, f32[3,5,1024]{2,1,0:T(8,128)} %copy-done.3, f32[3,1,128]{2,1,0:T(1,128)} %broadcast_in_dim.8.earlier), custom_call_target="tpu_custom_call" | custom-call | flops 31457280 | bytes 204800 | tf_op jit(solution)/shard_map/pair_forces/pallas_call | solution.py:1006
  75.4 0.0 all-to-all-done.1.incoming_hbm
  75.4 0.0 copy-start
  75.4 0.7 copy-done
  76.2 10.2 %interface_solve.1 = f32[288,1,256]{2,1,0:T(1,128)} custom-call(s32[1]{0:T(128)} %bitcast.4.first_mode, f32[288]{0:T(512)} %constant.51.clone.stiff_z, f32[3,1,512]{2,1,0:T(1,128)} %pair_forces.2._.earlier, f32[288,1,256]{2,1,0:T(1,128)} %copy-done, bf16[96,192]{1,0:T(8,128)(2,1)} %constant.52.clone.gather_hbm, f32[512,384]{1,0:T(8,128)} %constant.53.clone.along_y_hbm, ...), custom_call_target="tpu_custom_call" | custom-call | tf_op jit(solution)/shard_map/interface_solve/pallas_call | solution.py:899
  86.4 6.0 %all-to-all-start.2 = ((f32[288,1,256]{2,1,0:T(1,128)}), f32[288,1,256]{2,1,0:T(1,128)S(1)}, u32[]{:S(2)}, u32[]{:S(2)}) async-start(f32[288,1,256]{2,1,0:T(1,128)} %interface_solve.1), calls=%async_computation.2 | async-start | bytes 589824 | tf_op jit(solution)/shard_map/all_to_all | solution.py:920
  92.4 0.0 copy-start.6
  92.4 13.9 %pair_forces.3._ = f32[3,1,1024]{2,1,0:T(1,128)} custom-call(s32[1,3,1,32]{3,2,1,0:T(1,128)} %bitcast.18, f32[3,5,1024]{2,1,0:T(8,128)} %copy-done.4, f32[3,5,1024]{2,1,0:T(8,128)} %copy-done.5, f32[3,5,1024]{2,1,0:T(8,128)} %copy-done.3, f32[3,1,512]{2,1,0:T(1,128)} %pair_forces.2._.earlier), custom_call_target="tpu_custom_call" | custom-call | flops 31457280 | bytes 204800 | tf_op jit(solution)/shard_map/pair_forces/pallas_call | solution.py:1006
  106.4 0.0 all-to-all-done.2.message_hbm
  106.4 0.0 copy-start.1
  106.4 0.7 copy-done.1
  107.1 27.4 %backward_solve.1 = (f32[36,72,288]{2,1,0:T(8,128)}, f32[256,128]{1,0:T(8,128)}) custom-call(s32[8,2048]{1,0:T(8,128)} %get-tuple-element.12.places_hbm, f32[288,1,256]{2,1,0:T(1,128)} %copy-done.1, f32[384,256]{1,0:T(8,128)} %constant.50.clone.refs_6_.interface_hbm, f32[72,384]{1,0:T(8,128)} %constant.48.clone.refs_4_.diagonal_hbm, ...), custom_call_target="tpu_custom_call" | custom-call | tf_op jit(solution)/shard_map/backward_solve/pallas_call | solution.py:922
  134.5 8.8 %all_to_all.24 = f32[8,32,128]{2,1,0:T(8,128)S(1)} all-to-all(f32[8,32,128]{2,1,0:T(8,128)} %bitcast.11), channel_id=1, replica_groups=mesh['gx'=8,'gy'=4] {'gx'}, dimensions={0} | all-to-all | bytes 262144 | tf_op jit(solution)/shard_map/all_to_all | solution.py:1028
  143.3 0.0 copy-done.6
  143.3 0.1 slice_select_fusion
  143.4 0.7 reshape.31
  (3 shorter events, 0.0 us)
Async XLA Ops:
  2.2 5.1 %collective-permute-start = (f32[1,5,1024]{2,1,0:T(8,128)}, f32[1,5,1024]{2,1,0:T(8,128)S(1)}, u32[]{:S(2)}, u32[]{:S(2)}) collective-permute-start(f32[1,5,1024]{2,1,0:T(8,128)} %get-tuple-element.11), channel_id=1, source_target_pairs={{0,4},{4,8},{8,12},{12,16},{16,20},{20,24},{24,28},{28,0},{1,5},{5... | collective-permute-start | bytes 61448 | tf_op jit(solution)/shard_map/ppermute | solution.py:958
  2.6 5.5 %collective-permute-start.1 = (f32[1,5,1024]{2,1,0:T(8,128)}, f32[1,5,1024]{2,1,0:T(8,128)S(1)}, u32[]{:S(2)}, u32[]{:S(2)}) collective-permute-start(f32[1,5,1024]{2,1,0:T(8,128)} %get-tuple-element.11), channel_id=1, source_target_pairs={{0,28},{4,0},{8,4},{12,8},{16,12},{20,16},{24,20},{28,24},{1,29},{... | collective-permute-start | bytes 61448 | tf_op jit(solution)/shard_map/ppermute | solution.py:958
  8.1 53.4 %copy-start.5 = (f32[3,5,1024]{2,1,0:T(8,128)}, f32[3,5,1024]{2,1,0:T(8,128)S(1)}, u32[]{:S(2)}) copy-start(f32[3,5,1024]{2,1,0:T(8,128)S(1)} %constant_dynamic-update-slice_fusion.middle) | copy-start | bytes 184324
  8.1 12.7 %collective-permute-start.3 = (f32[3,5,1024]{2,1,0:T(8,128)S(1)}, f32[3,5,1024]{2,1,0:T(8,128)S(1)}, u32[]{:S(2)}, u32[]{:S(2)}) collective-permute-start(f32[3,5,1024]{2,1,0:T(8,128)S(1)} %constant_dynamic-update-slice_fusion.middle), channel_id=1, source_target_pairs={{0,3},{1,0},{2,1},{3,2},{4,7},{5,4},{6,5},{7,6},{8,11},{9,8},{10,9... | collective-permute-start | bytes 184328 | tf_op jit(solution)/shard_map/ppermute | solution.py:958
  12.5 8.3 %collective-permute-start.2 = (f32[3,5,1024]{2,1,0:T(8,128)S(1)}, f32[3,5,1024]{2,1,0:T(8,128)S(1)}, u32[]{:S(2)}, u32[]{:S(2)}) collective-permute-start(f32[3,5,1024]{2,1,0:T(8,128)S(1)} %constant_dynamic-update-slice_fusion.middle), channel_id=1, source_target_pairs={{0,1},{1,2},{2,3},{3,0},{4,5},{5,6},{6,7},{7,4},{8,9},{9,10},{10,1... | collective-permute-start | bytes 184328 | tf_op jit(solution)/shard_map/ppermute | solution.py:958
  12.5 8.3 %all-to-all-start = ((f32[8,1,2048]{2,1,0:T(1,128)}), f32[8,1,2048]{2,1,0:T(1,128)S(1)}, u32[]{:S(2)}, u32[]{:S(2)}) async-start(f32[8,1,2048]{2,1,0:T(1,128)} %get-tuple-element.10), calls=%async_computation | async-start | bytes 131072 | tf_op jit(solution)/shard_map/all_to_all | solution.py:994
  20.8 0.6 copy-start.2
  20.8 0.7 copy-start.3
  20.8 0.7 copy-start.4
  56.7 18.8 %all-to-all-start.1 = ((f32[288,1,256]{2,1,0:T(1,128)}), f32[288,1,256]{2,1,0:T(1,128)S(1)}, u32[]{:S(2)}, u32[]{:S(2)}) async-start(f32[288,1,256]{2,1,0:T(1,128)} %get-tuple-element.13), calls=%async_computation.1 | async-start | bytes 589824 | tf_op jit(solution)/shard_map/all_to_all | solution.py:878
  75.4 0.7 copy-start
  86.4 20.0 %all-to-all-start.2 = ((f32[288,1,256]{2,1,0:T(1,128)}), f32[288,1,256]{2,1,0:T(1,128)S(1)}, u32[]{:S(2)}, u32[]{:S(2)}) async-start(f32[288,1,256]{2,1,0:T(1,128)} %interface_solve.1), calls=%async_computation.2 | async-start | bytes 589824 | tf_op jit(solution)/shard_map/all_to_all | solution.py:920
  92.4 50.9 %copy-start.6 = (s32[1,1,32]{2,1,0:T(1,128)S(1)}, s32[1,1,32]{2,1,0:T(1,128)}, u32[]{:S(2)}) copy-start(s32[1,1,32]{2,1,0:T(1,128)} %param.29) | copy-start | bytes 388
  106.4 0.7 copy-start.1

commit v3 on v2

--- a/solution.py
+++ b/solution.py
@@ -12,6 +12,7 @@
 SCREENING = 0.003
 HIGH_ACCURACY = lax.Precision.HIGHEST
 VMEM_MIB = 60
+BATCH = 8
 MIB = 1024 * 1024
 
 
@@ -188,17 +189,16 @@
     return copies
 
 
-def list_owned(plan, places, blocks, n_blocks, block_atoms):
-    rows = plan.lane_tiles * plan.planes
-
-    def tile(source, count):
-        for number in range(n_blocks):
-            lead = places[source, number * block_atoms]
-            blocks[count] = source * n_blocks + number
-            count = count + jnp.where((lead >= 0) & (lead < rows), 1, 0)
+def list_owned(plan, places, blocks, block_count):
+    def several(step, count):
+        for k in range(8):
+            number = step * 8 + k
+            lead = places[number, 0]
+            blocks[count] = number
+            count = count + jnp.where((lead >= 0) & (lead < plan.span), 1, 0)
         return count
 
-    return lax.fori_loop(0, plan.n_gx, tile, 0)
+    return lax.fori_loop(0, block_count // 8, several, 0)
 
 
 def chunked_loop(count, unroll, body, init):
@@ -213,23 +213,20 @@
     return lax.fori_loop(0, count // unroll, group, init)
 
 
-def mark_places(plan, codes, first_code, place_rows, tile_atoms, block_atoms):
-    lane = lax.broadcasted_iota(jnp.int32, (codes.shape[0], 128), 1) % block_atoms
-    for start in range(0, tile_atoms, 128):
-        lanes = slice(start, start + 128)
-        code = codes[:, lanes].astype(jnp.int32) - first_code
-        place = lax.shift_right_arithmetic(code, 7)
-        shared = jnp.zeros_like(place)
-        for step in range(1, block_atoms):
-            same = (pltpu.roll(place, step, 1) == place) & (lane >= step)
-            shared = jnp.where(same, 1, shared)
-        step = block_atoms // 2
-        while step:
-            shared = shared | pltpu.roll(shared, 128 - step, 1)
-            step //= 2
-        place_rows[:, lanes] = place
-        mark = jnp.where(lane == 0, shared * 128, 0)
-        place_rows[:, tile_atoms + start : tile_atoms + start + 128] = (code & 127) + mark
+def mark_places(codes, first_code, place_rows, block_atoms):
+    lane = lax.broadcasted_iota(jnp.int32, codes.shape, 1)
+    code = codes[...].astype(jnp.int32) - first_code
+    place = lax.shift_right_arithmetic(code, 7)
+    shared = jnp.zeros_like(place)
+    for step in range(1, BATCH):
+        same = (pltpu.roll(place, step, 1) == place) & (lane % BATCH >= step)
+        shared = jnp.where(same & (lane < block_atoms), 1, shared)
+    step = block_atoms // 2
+    while step:
+        shared = shared | pltpu.roll(shared, 128 - step, 1)
+        step //= 2
+    mark = pltpu.roll(shared, block_atoms, 1)
+    place_rows[...] = jnp.where(lane == block_atoms, mark, code)
 
 
 def forward_kernel(
@@ -259,7 +256,6 @@
         heads,
         edge_rows,
         turned,
-        codes_in,
         codes,
         density,
         z_full,
@@ -271,20 +267,17 @@
         interface,
         spectrum,
         place_rows,
-        charge_rows,
         places,
-        charges,
         blocks,
         sems,
     ) = refs
     x_len, y_len, y_pad, x_pad = plan.x_len, plan.y_len, plan.y_pad, plan.x_pad
     grid, lane_count, planes = plan.grid, plan.lanes, plan.planes
     slabs = slab_count(plan)
-    tile_atoms = n_blocks * block_atoms
     lane_ids = lax.broadcasted_iota(jnp.int32, (1, 128), 1)
     loads = start_copies(
         [
-            (codes_hbm, codes_in),
+            (codes_hbm, codes),
             (density_hbm, density),
             (z_full_hbm, z_full),
             (y_table_hbm, y_table),
@@ -295,12 +288,7 @@
         sems,
     )
     loads[0].wait()
-    for source in range(plan.n_gx):
-        codes[source : source + 1, :] = codes_in[source, :, :tile_atoms]
-        charge_rows[source : source + 1, :] = codes_in[source, :, tile_atoms:]
-    charge_copy = pltpu.make_async_copy(charge_rows, charges, sems.at[7])
-    charge_copy.start()
-    mark_places(plan, codes, first_code[0], place_rows, tile_atoms, block_atoms)
+    mark_places(codes, first_code[0], place_rows, block_atoms)
     place_copies = [
         pltpu.make_async_copy(place_rows, places, sems.at[8]),
         pltpu.make_async_copy(place_rows, places_hbm, sems.at[9]),
@@ -316,34 +304,33 @@
     chunked_loop(plan.lane_tiles * x_len, 4, clear, 0)
     loads[2].wait()
     split_table(z_full, z_table, 0)
-    charge_copy.wait()
     place_copies[0].wait()
-    count = list_owned(plan, places, blocks, n_blocks, block_atoms)
+    count = list_owned(plan, places, blocks, plan.n_gx * n_blocks)
 
     def deposit(slot, carry):
         block = blocks[slot]
-        source = block // n_blocks
-        start = (block - source * n_blocks) * block_atoms
-        lead = places[source, start + tile_atoms]
-
-        def row_of(k):
-            return pl.ds(places[source, start + k], 1)
-
-        def raised(k):
-            lane = places[source, start + k + tile_atoms] & 127
-            hit = jnp.where(lane_ids == lane, charges[source, start + k], 0.0)
-            return added[row_of(k), :] + hit
-
-        @pl.when(lead < 128)
+        row_codes = places.at[block]
+        charge_row = codes[pl.ds(block, 1), :]
+
+        def raised(code, k):
+            charge = charge_row[:, block_atoms + k : block_atoms + k + 1]
+            hit = jnp.where(lane_ids == (code & 127), charge, 0.0)
+            return added[pl.ds(lax.shift_right_logical(code, 7), 1), :] + hit
+
+        @pl.when(row_codes[block_atoms] == 0)
         def _():
-            rows = [raised(k) for k in range(block_atoms)]
-            for k in range(block_atoms):
-                added[row_of(k), :] = rows[k]
-
-        @pl.when(lead >= 128)
+            for start in range(0, block_atoms, BATCH):
+                local = [row_codes[start + k] for k in range(BATCH)]
+                rows = [raised(code, start + k) for k, code in enumerate(local)]
+                for code, row in zip(local, rows):
+                    added[pl.ds(lax.shift_right_logical(code, 7), 1), :] = row
+
+        @pl.when(row_codes[block_atoms] != 0)
         def _():
             for k in range(block_atoms):
-                added[row_of(k), :] = raised(k)
+                code = row_codes[k]
+                row = raised(code, k)
+                added[pl.ds(lax.shift_right_logical(code, 7), 1), :] = row
 
         return carry
 
@@ -358,7 +345,7 @@
         for tile in range(plan.lane_tiles):
             low = tile * 128
             width = min(128, grid - low)
-            piece = density[pl.ds(start, slabs), :, low : low + width]
+            piece = density.at[pl.ds(start, slabs)][:, :, low : low + width]
             if y_pad == y_len:
                 piece = piece.reshape(count, width)
             else:
@@ -368,14 +355,14 @@
                 rest = jnp.zeros((count, 128 - width), jnp.float32)
                 piece = jnp.concatenate([piece, rest], axis=1)
             place = pl.ds(pl.multiple_of(tile * planes + start * y_pad, 8), count)
-            pieces.append(piece + added[place, :])
+            pieces.append(piece + added.at[place][...])
         lines = right_apply(jnp.concatenate(pieces, axis=1), z_table[...])
         lines = lines.reshape(slabs, y_pad, lane_count)
         for slab in range(slabs):
             x = start + slab
             for tile in range(plan.lane_tiles):
                 heads[tile, pl.ds(x, 1), :] = lines[slab, 0:1, tile * 128 : tile * 128 + 128]
-            spectrum[x] = left_apply(y_table[...], lines[slab])
+            spectrum.at[x][...] = left_apply(y_table[...], lines[slab])
 
         @pl.when(step == 0)
         def _():
@@ -399,14 +386,14 @@
             factor, value = carry
             x = step + 1
             factor = inverse(diagonal[:, lanes] - factor)
-            value = (spectrum[x, :, lanes] + value) * factor
-            factors[x] = factor
-            solved[x] = value
+            value = (spectrum.at[x][:, lanes] + value) * factor
+            factors.at[x][...] = factor
+            solved.at[x][...] = value
             return factor, value
 
         def substitute(step, value):
             x = x_len - 1 - step
-            value = solved[x] + factors[x] * value
+            value = solved.at[x][...] + factors.at[x][...] * value
             near_row = jnp.sum(value * near_weight, axis=0, keepdims=True)
             far_row = jnp.sum(value * far_weight, axis=0, keepdims=True)
             edge_rows[0, pl.ds(x, 1), :] = near_row + heads[tile, pl.ds(x, 1), :]
@@ -485,7 +472,7 @@
 
     def collect(source, carry):
         for mode in range(modes):
-            both = incoming[source * modes + mode]
+            both = incoming.at[source * modes + mode][...]
             rows[mode, pl.ds(source, 1), :] = both[:, :half]
             rows[mode, pl.ds(parts + source, 1), :] = both[:, half:]
         return carry
@@ -595,7 +582,6 @@
     x_len, y_len, y_pad, x_pad = plan.x_len, plan.y_len, plan.y_pad, plan.x_pad
     grid, lane_count, planes = plan.grid, plan.lanes, plan.planes
     slabs = slab_count(plan)
-    tile_atoms = n_blocks * block_atoms
     loads = start_copies(
         [
             (message_hbm, message),
@@ -618,7 +604,7 @@
     split_table(interface_full, interface, 1)
     stack[...] = dot(interface[...], value_triple(turned[...], 1), ((1,), (1,)))
     loads[2].wait()
-    count = list_owned(plan, places, blocks, n_blocks, block_atoms)
+    count = list_owned(plan, places, blocks, plan.n_gx * n_blocks)
     for copy in loads[3:]:
         copy.wait()
     split_table(z_full, z_table, 0)
@@ -633,17 +619,17 @@
             factor, value = carry
             x = step + 1
             factor = inverse(diagonal[:, lanes] - factor)
-            load = spectrum[x, :, lanes] + near_weight * heads[tile, pl.ds(x, 1), :]
+            load = spectrum.at[x][:, lanes] + near_weight * heads[tile, pl.ds(x, 1), :]
             load = load + far_weight * edge_rows[pl.ds(x, 1), :]
             value = (load + value) * factor
-            factors[x] = factor
-            solved[x] = value
+            factors.at[x][...] = factor
+            solved.at[x][...] = value
             return factor, value
 
         def substitute(step, value):
             x = x_len - 1 - step
-            value = solved[x] + factors[x] * value
-            work[x, :, lanes] = value
+            value = solved.at[x][...] + factors.at[x][...] * value
+            work.at[x][:, lanes] = value
             return value
 
         zero = jnp.zeros((y_pad, 128), jnp.float32)
@@ -655,23 +641,24 @@
         start = step * slabs
         for slab in range(slabs):
             x = start + slab
-            work[x] = left_apply(y_table[...], work[x])
+            slab_work = work.at[x]
+            slab_work[...] = left_apply(y_table[...], slab_work[...])
             for tile in range(plan.lane_tiles):
                 lanes = slice(tile * 128, tile * 128 + 128)
-                work[x, 0:1, lanes] = heads[tile, pl.ds(x, 1), :]
+                slab_work[0:1, lanes] = heads[tile, pl.ds(x, 1), :]
 
         @pl.when(step == 0)
         def _():
             work[0] = stack[2 * y_pad : 3 * y_pad, :]
 
-        lines = work[pl.ds(start, slabs)].reshape(slabs * y_pad, lane_count)
+        lines = work.at[pl.ds(start, slabs)][...].reshape(slabs * y_pad, lane_count)
         lines = right_apply(lines, z_table[...])
         for tile in range(plan.lane_tiles):
             low = tile * 128
             place = pl.ds(pl.multiple_of(tile * planes + start * y_pad, 8), slabs * y_pad)
-            lookup[place, :] = lines[:, low : low + 128]
+            lookup.at[place][...] = lines[:, low : low + 128]
         lines = lines.reshape(slabs, y_pad, lane_count)
-        potential[pl.ds(start, slabs)] = lines[:, :y_len, :grid]
+        potential.at[pl.ds(start, slabs)][...] = lines[:, :y_len, :grid]
         return carry
 
     chunked_loop(x_len // slabs, 3, transform, 0)
@@ -686,14 +673,13 @@
 
     def sample(slot, carry):
         block = blocks[slot]
-        source = block // n_blocks
-        start = (block - source * n_blocks) * block_atoms
+        row_codes = places.at[block]
         for first in range(0, block_atoms, 16):
             rows = []
             for atom in range(first, first + 16):
-                row = lookup[pl.ds(places[source, start + atom], 1), :]
-                lane = places[source, start + atom + tile_atoms] & 127
-                rows.append(jnp.where(lane_ids == lane, row, 0.0))
+                code = row_codes[atom]
+                row = lookup[pl.ds(lax.shift_right_logical(code, 7), 1), :]
+                rows.append(jnp.where(lane_ids == (code & 127), row, 0.0))
             for k in range(16):
                 picked[first + k : first + k + 1, :] = rows[k]
         found = jnp.sum(picked[...], axis=1, keepdims=True)
@@ -707,7 +693,7 @@
 
 def prepare_kernel(
     plan, n_blocks, block_atoms, counts, owners, type_radius, coords, charge, types, cells,
-    copies, atom_rows,
+    copies, atom_rows, payload,
 ):
     tile_atoms = n_blocks * block_atoms
     lane = lax.broadcasted_iota(jnp.int32, (1, 128), 1)
@@ -730,24 +716,27 @@
         plane = x * plan.y_pad + (line - x * plan.y_len)
         code = ((depth >> 7) * plan.planes + plane) * 128 + (depth & 127)
         code = (owner * plan.span + code).astype(jnp.float32)
-        for target in range(plan.n_gx):
-            copies[target, :, lanes] = code
-            copies[target, :, tile_atoms + start : tile_atoms + start + 128] = live
+        for k in range(per_row):
+            shift = k * block_atoms
+            row = pltpu.roll(code, (128 - shift) % 128, 1)
+            charges = pltpu.roll(live, (128 + block_atoms - shift) % 128, 1)
+            row = jnp.where(lane < block_atoms, row, charges)
+            payload[first + k : first + k + 1, :] = jnp.where(lane < 2 * block_atoms, row, 0.0)
         radius = jnp.zeros((1, 128), jnp.float32)
         for kind in range(type_radius.shape[0]):
             radius = jnp.where(types[0, :, lanes] == kind, type_radius[kind], radius)
         atom_rows[0, 0:3, lanes] = coords[0, :, 0, lanes]
         atom_rows[0, 3:4, lanes] = live
         atom_rows[0, 4:5, lanes] = radius
+    for target in range(plan.n_gx):
+        copies[target * n_blocks : (target + 1) * n_blocks, :] = payload[...]
 
 
 def pair_kernel(
-    n_blocks, block_atoms, listed, part, n_parts, listing, low, middle, high, earlier, forces,
+    n_blocks, block_atoms, listed, first, part_atoms, listing, low, middle, high, earlier, forces,
     table, columns, results,
 ):
     tile_atoms = n_blocks * block_atoms
-    part_atoms = tile_atoms // n_parts
-    first = part * part_atoms
     sides = (low, middle, high)
     for step_x in range(3):
         for step_y in range(3):
@@ -761,38 +750,39 @@
     columns[0:5, :] = middle[1, :, first : first + part_atoms]
     columns[5:, :] = jnp.zeros((columns.shape[0] - 5, part_atoms), jnp.float32)
     results[...] = jnp.transpose(columns[...])
-    lane_ids = lax.broadcasted_iota(jnp.int32, (16, 128), 1)
+    lane_ids = lax.broadcasted_iota(jnp.int32, (block_atoms, 128), 1)
+    groups = block_atoms // 8
 
     def group(number, carry):
-        place = pl.ds(pl.multiple_of(number * 16, 16), 16)
-        block = (first + number * 16) // block_atoms
+        place = pl.ds(pl.multiple_of(number * block_atoms, block_atoms), block_atoms)
+        block = first // block_atoms + number
         own = results[place, :]
         mine = [
-            jnp.broadcast_to(own[:, k : k + 1], (16, 128)).reshape(2, 8, 128)
+            jnp.broadcast_to(own[:, k : k + 1], (block_atoms, 128)).reshape(groups, 8, 128)
             for k in (0, 1, 2, 4)
         ]
-        force_x = force_y = force_z = jnp.zeros((2, 8, 128), jnp.float32)
+        force_x = force_y = force_z = jnp.zeros((groups, 8, 128), jnp.float32)
         for slot in range(listed):
-            which = listing[0, slot, 0, block]
+            rows = table.at[listing[0, slot, 0, block]]
             for start in range(0, tile_atoms, 128):
                 lanes = slice(start, start + 128)
-                sep_x = mine[0] - table[which, 0, :, lanes][None]
-                sep_y = mine[1] - table[which, 1, :, lanes][None]
-                sep_z = mine[2] - table[which, 2, :, lanes][None]
-                reach = mine[3] + table[which, 4, :, lanes][None]
+                sep_x = mine[0] - rows[0, :, lanes][None]
+                sep_y = mine[1] - rows[1, :, lanes][None]
+                sep_z = mine[2] - rows[2, :, lanes][None]
+                reach = mine[3] + rows[4, :, lanes][None]
                 root = lax.rsqrt(sep_x * sep_x + sep_y * sep_y + sep_z * sep_z + reach * reach)
-                strength = table[which, 3, :, lanes][None] * root * (root * root)
+                strength = rows[3, :, lanes][None] * root * (root * root)
                 force_x = force_x + strength * sep_x
                 force_y = force_y + strength * sep_y
                 force_z = force_z + strength * sep_z
-        out = jnp.zeros((16, 128), jnp.float32)
+        out = jnp.zeros((block_atoms, 128), jnp.float32)
         for axis, total in enumerate((force_x, force_y, force_z)):
-            force = own[:, 3:4] * jnp.sum(total.reshape(16, 128), axis=1, keepdims=True)
-            out = jnp.where(lane_ids == axis, force, out)
+            total = jnp.sum(total.reshape(block_atoms, 128), axis=1, keepdims=True)
+            out = jnp.where(lane_ids == axis, own[:, 3:4] * total, out)
         results[place, :] = out
         return carry
 
-    lax.fori_loop(0, part_atoms // 16, group, 0)
+    lax.fori_loop(0, part_atoms // block_atoms, group, 0)
     columns[...] = jnp.transpose(results[...])
     if first:
         for axis in range(3):
@@ -832,7 +822,7 @@
     edge_y = f32(plan.edge_weights())
     interface = f32(plan.interface_table())
     bf16 = jnp.bfloat16
-    n_rows, tile_atoms = codes.shape[0], n_blocks * block_atoms
+    code_shape = codes.shape
     shared = [
         buffer(x_len, y_pad, 128),
         buffer(x_len, y_pad, 128),
@@ -843,7 +833,7 @@
         functools.partial(forward_kernel, plan, n_blocks, block_atoms),
         out_shape=(
             shaped(x_len, y_pad, lanes),
-            jax.ShapeDtypeStruct((n_rows, 2 * tile_atoms), jnp.int32),
+            jax.ShapeDtypeStruct(code_shape, jnp.int32),
             shaped(total, 1, 2 * half),
         ),
         in_specs=[SMEM] + [HBM] * 9,
@@ -853,8 +843,7 @@
         + [
             buffer(2, x_pad, 128),
             buffer(lanes, 2 * half),
-            buffer(n_rows, 1, 2 * tile_atoms),
-            buffer(n_rows, tile_atoms),
+            buffer(*code_shape),
             buffer(x_len, y_len, grid),
             like(z_full),
             pltpu.VMEM((3 * lanes, lanes), bf16),
@@ -864,17 +853,16 @@
             like(interface),
             pltpu.VMEM((3 * plan.stack_rows, 2 * half), bf16),
             buffer(x_len, y_pad, lanes),
-            pltpu.VMEM((n_rows, 2 * tile_atoms), jnp.int32),
-            buffer(n_rows, tile_atoms),
-            pltpu.SMEM((n_rows, 2 * tile_atoms), jnp.int32),
-            pltpu.SMEM((n_rows, tile_atoms), jnp.float32),
-            pltpu.SMEM((n_rows * n_blocks,), jnp.int32),
+            pltpu.VMEM(code_shape, jnp.int32),
+            pltpu.SMEM(code_shape, jnp.int32),
+            pltpu.SMEM((code_shape[0],), jnp.int32),
             pltpu.SemaphoreType.DMA((11,)),
         ],
         compiler_params=limit(VMEM_MIB),
         name="forward_solve",
     )(first_code, codes, density, z_full, y_table, diagonal, edge_y, interface, *neighbours)
-    first_pairs = pair_part(0, None)
+    half_tile = n_blocks * block_atoms // 2
+    first_pairs = pair_part(0, half_tile, None)
     incoming = lax.all_to_all(message, ("gx", "gy"), split_axis=0, concat_axis=0, tiled=True)
     gather = plan.gather_table()
     along_y, along_x = plan.line_tables()
@@ -918,7 +906,7 @@
         name="interface_solve",
     )(first_mode, f32((padded_z + SCREENING) * grid), first_pairs, incoming, *tables)
     returned = lax.all_to_all(outgoing, ("gx", "gy"), split_axis=0, concat_axis=0, tiled=True)
-    pair_force = pair_part(1, first_pairs)
+    more_pairs = pair_part(half_tile, half_tile // 2, first_pairs)
     potential, values = pl.pallas_call(
         functools.partial(backward_kernel, plan, n_blocks, block_atoms),
         out_shape=(shaped(x_len, y_len, grid), shaped(plan.n_gx * n_blocks, 128)),
@@ -934,7 +922,7 @@
             buffer(lanes, 2 * half),
             buffer(block_atoms, 128),
             buffer(x_len, y_len, grid),
-            pltpu.SMEM((n_rows, 2 * tile_atoms), jnp.int32),
+            pltpu.SMEM(code_shape, jnp.int32),
             buffer(total, 1, 2 * half),
             like(interface),
             pltpu.VMEM((plan.stack_rows, 6 * half), bf16),
@@ -944,12 +932,13 @@
             like(y_table),
             like(z_full),
             pltpu.VMEM((3 * lanes, lanes), bf16),
-            pltpu.SMEM((n_rows * n_blocks,), jnp.int32),
+            pltpu.SMEM((code_shape[0],), jnp.int32),
             pltpu.SemaphoreType.DMA((9,)),
         ],
         compiler_params=limit(VMEM_MIB),
         name="backward_solve",
-    )(places, returned, interface, diagonal, edge_y, spectrum, y_table, z_full, pair_force)
+    )(places, returned, interface, diagonal, edge_y, spectrum, y_table, z_full, more_pairs)
+    pair_force = pair_part(half_tile + half_tile // 2, half_tile // 2, more_pairs)
     return potential, values, pair_force
 
 
@@ -977,9 +966,10 @@
     plan = Plan(x_local, local_y_rows, grid_len, n_gx, lax.axis_size("gy"))
     copies, atom_rows = pl.pallas_call(
         functools.partial(prepare_kernel, plan, n_blocks, block_atoms),
-        out_shape=(shaped(n_gx, 1, 2 * tile_atoms), shaped(1, 5, tile_atoms)),
+        out_shape=(shaped(n_gx * n_blocks, 128), shaped(1, 5, tile_atoms)),
         in_specs=[SMEM] * 3 + [VMEM] * 4,
         out_specs=(VMEM, VMEM),
+        scratch_shapes=[buffer(n_blocks, 128)],
         compiler_params=limit(VMEM_MIB),
         name="prepare_atoms",
     )(
@@ -1000,24 +990,24 @@
     listed = neighbour_tiles.shape[3]
     listing = neighbour_tiles.transpose(0, 3, 1, 2)
 
-    def pair_part(part, earlier):
+    def pair_part(first, part_atoms, earlier):
         if earlier is None:
             earlier = jnp.zeros((3, 1, 128), jnp.float32)
         return pl.pallas_call(
-            functools.partial(pair_kernel, n_blocks, block_atoms, listed, part, 2),
-            out_shape=shaped(3, 1, (part + 1) * tile_atoms // 2),
+            functools.partial(pair_kernel, n_blocks, block_atoms, listed, first, part_atoms),
+            out_shape=shaped(3, 1, first + part_atoms),
             in_specs=[SMEM] + [VMEM] * 4,
             out_specs=VMEM,
             scratch_shapes=[
                 buffer(9, 5, 8, tile_atoms),
-                buffer(128, tile_atoms // 2),
-                buffer(tile_atoms // 2, 128),
+                buffer(128, part_atoms),
+                buffer(part_atoms, 128),
             ],
             compiler_params=limit(VMEM_MIB),
             cost_estimate=pl.CostEstimate(
-                flops=10 * listed * tile_atoms * tile_atoms,
+                flops=21 * listed * tile_atoms * part_atoms,
                 bytes_accessed=4 * 50 * tile_atoms,
-                transcendentals=listed * tile_atoms * tile_atoms // 2,
+                transcendentals=listed * tile_atoms * part_atoms,
             ),
             name="pair_forces",
         )(listing, below, triple, above, earlier)

time: 143 us -> 121 us (0.85)
  Pallas kernels: 102 us -> 82 us
  blocking collectives: 8.82 us -> 0 us
  waiting for transfers between devices: 6.76 us -> 11 us
  starting transfers between devices: 21.4 us -> 23.2 us
    pallas_call x1, Pallas kernels: 35.1 us -> 25.7 us  [solve_poisson(): pl.pallas_call(functools.partial(forward_kernel, plan, n_blocks, block_at...]
    all_to_all x1 -> x0, blocking collectives: 8.82 us -> none  [body(): lax.all_to_all(values, 'gx', split_axis=0, concat_axis=0, tiled=True)]
    pallas_call x2 -> x3, Pallas kernels: 27.8 us -> 22.2 us  [pair_part(): pl.pallas_call(functools.partial(pair_kernel, n_blocks, block_atoms, list...]
    pallas_call x1, Pallas kernels: 27.4 us -> 22.3 us  [solve_poisson(): pl.pallas_call(functools.partial(backward_kernel, plan, n_blocks, block_a...]
    all_to_all x1, waiting for transfers between devices: 4.94 us -> 0.01 us  [body(): lax.all_to_all(copies, 'gx', split_axis=0, concat_axis=0, tiled=True)]
    ppermute x4, waiting for transfers between devices: 1.81 us -> 6.58 us  [shifted(): lax.ppermute(block, axis, [(i, (i + step) % count) for i in range(count)])]
    all_to_all x1, waiting for transfers between devices: 0.01 us -> 4.44 us  [solve_poisson(): lax.all_to_all(outgoing, ('gx', 'gy'), split_axis=0, concat_axis=0, tiled...]
    all_to_all x0 -> x1, starting transfers between devices: none -> 3.38 us  [body(): lax.all_to_all(values, 'gx', split_axis=0, concat_axis=0, tiled=True)]
  transfers between devices with their start and end apart: 7 -> 8, of which waited for: 2 -> 3; matrix products, arithmetic and copies ran while one was open for 1% -> 1% of each run, Pallas kernels for 19% -> 18%
where the time goes in v3:
time: 121 us
  Pallas kernels  82 us (68%)
  starting transfers between devices  23.2 us (19%)
  waiting for transfers between devices  11 us (9%)
  local copies, waits for them, and re-layouts  4.12 us (3%)
    pallas_call x1, Pallas kernels, solve_poisson(): pl.pallas_call(functools.partial(forward_kernel, plan, n_blocks, block_at...  25.7 us
    pallas_call x1, Pallas kernels, solve_poisson(): pl.pallas_call(functools.partial(backward_kernel, plan, n_blocks, block_a...  22.3 us
    pallas_call x3, Pallas kernels, pair_part(): pl.pallas_call(functools.partial(pair_kernel, n_blocks, block_atoms, list...  22.2 us
    pallas_call x1, Pallas kernels, solve_poisson(): pl.pallas_call(functools.partial(interface_kernel, plan), out_shape=shape...  10.2 us
    ppermute x4, starting transfers between devices, shifted(): lax.ppermute(block, axis, [(i, (i + step) % count) for i in range(count)])  7.58 us
    ppermute x4, waiting for transfers between devices, shifted(): lax.ppermute(block, axis, [(i, (i + step) % count) for i in range(count)])  6.58 us
    all_to_all x1, starting transfers between devices, solve_poisson(): lax.all_to_all(outgoing, ('gx', 'gy'), split_axis=0, concat_axis=0, tiled...  6.02 us
    all_to_all x1, waiting for transfers between devices, solve_poisson(): lax.all_to_all(outgoing, ('gx', 'gy'), split_axis=0, concat_axis=0, tiled...  4.44 us
  transfers between devices with their start and end apart: 8, of which 3 were waited for; matrix products, arithmetic and copies ran while one was open for 1% of the time, Pallas kernels for 18%

profile of v3, /device:TPU:0, one launch (start us, length us, event | category | flops | bytes accessed | tf_op | source)
XLA Modules:
  0.0 121.1 jit_solution(7054035771767468151)
XLA Ops:
  0.6 1.6 %prepare_atoms.1 = (f32[256,128]{1,0:T(8,128)}, f32[1,5,1024]{2,1,0:T(8,128)}) custom-call(s32[1,32]{1,0:T(1,128)} %bitcast.17, s32[1,32]{1,0:T(1,128)} %bitcast.19, f32[16]{0:T(128)} %type_radius.1, f32[1,3,1,1024]{3,2,1,0:T(1,128)} %bitcast.16, f32[1,1,1024]{2,1,0:T(1,128)} %charge.1, s32[1,1,1024]{2,1,0:T(1,128)} %types.1, s32[1,1,1024]{2,1,0:T(1,128)} %cells.1), custom_call_target="tpu_custom_call" | custom-call | tf_op jit(solution)/shard_map/prepare_atoms/pallas_call | solution.py:967
  2.3 0.5 collective-permute-start
  2.7 2.9 %collective-permute-start.1 = (f32[1,5,1024]{2,1,0:T(8,128)}, f32[1,5,1024]{2,1,0:T(8,128)S(1)}, u32[]{:S(2)}, u32[]{:S(2)}) collective-permute-start(f32[1,5,1024]{2,1,0:T(8,128)} %get-tuple-element.11), channel_id=1, source_target_pairs={{0,28},{4,0},{8,4},{12,8},{16,12},{20,16},{24,20},{28,24},{1,29},{... | collective-permute-start | bytes 61448 | tf_op jit(solution)/shard_map/ppermute | solution.py:947
  5.6 3.6 %all-to-all-start = ((f32[8,32,128]{2,1,0:T(8,128)}), f32[8,32,128]{2,1,0:T(8,128)S(1)}, u32[]{:S(2)}, u32[]{:S(2)}) async-start(f32[8,32,128]{2,1,0:T(8,128)} %bitcast.14), calls=%async_computation | async-start | bytes 262144 | tf_op jit(solution)/shard_map/all_to_all | solution.py:984
  9.2 0.0 collective-permute-done
  9.2 0.8 constant_dynamic-update-slice_fusion.1
  10.0 0.0 collective-permute-done.1
  10.0 0.0 copy-start.5
  10.0 4.2 %collective-permute-start.3 = (f32[3,5,1024]{2,1,0:T(8,128)S(1)}, f32[3,5,1024]{2,1,0:T(8,128)S(1)}, u32[]{:S(2)}, u32[]{:S(2)}) collective-permute-start(f32[3,5,1024]{2,1,0:T(8,128)S(1)} %constant_dynamic-update-slice_fusion.middle), channel_id=1, source_target_pairs={{0,3},{1,0},{2,1},{3,2},{4,7},{5,4},{6,5},{7,6},{8,11},{9,8},{10,9... | collective-permute-start | bytes 184328 | tf_op jit(solution)/shard_map/ppermute | solution.py:947
  14.2 0.0 collective-permute-start.2
  14.2 3.2 %collective-permute-done.3.refs_8_.high = f32[3,5,1024]{2,1,0:T(8,128)S(1)} collective-permute-done((f32[3,5,1024]{2,1,0:T(8,128)S(1)}, f32[3,5,1024]{2,1,0:T(8,128)S(1)}, u32[]{:S(2)}, u32[]{:S(2)}) %collective-permute-start.3) | collective-permute-done | bytes 61472 | tf_op jit(solution)/shard_map/ppermute | solution.py:947
  17.4 0.0 copy-start.3
  17.4 3.4 %collective-permute-done.2.refs_7_.low = f32[3,5,1024]{2,1,0:T(8,128)S(1)} collective-permute-done((f32[3,5,1024]{2,1,0:T(8,128)S(1)}, f32[3,5,1024]{2,1,0:T(8,128)S(1)}, u32[]{:S(2)}, u32[]{:S(2)}) %collective-permute-start.2) | collective-permute-done | bytes 61472 | tf_op jit(solution)/shard_map/ppermute | solution.py:947
  20.8 0.0 copy-start.4
  20.8 0.0 all-to-all-done
  20.8 0.0 copy-start.2
  20.8 0.0 copy-done.3
  20.8 0.6 copy-done.4
  21.4 0.1 copy-done.2
  21.5 25.7 %forward_solve.1 = (f32[36,72,384]{2,1,0:T(8,128)}, s32[256,128]{1,0:T(8,128)}, f32[288,1,256]{2,1,0:T(1,128)}) custom-call(s32[1]{0:T(128)} %bitcast.first_code, f32[256,128]{1,0:T(8,128)} %bitcast.13, f32[36,72,288]{2,1,0:T(8,128)} %refs_1_.1, f32[384,384]{1,0:T(8,128)} %constant.46.clone.refs_2_.z_full_hbm, ...), custom_call_target="tpu_custom_call" | custom-call | tf_op jit(solution)/shard_map/forward_solve/pallas_call | solution.py:832
  47.1 2.6 %all-to-all-start.1 = ((f32[288,1,256]{2,1,0:T(1,128)}), f32[288,1,256]{2,1,0:T(1,128)S(1)}, u32[]{:S(2)}, u32[]{:S(2)}) async-start(f32[288,1,256]{2,1,0:T(1,128)} %get-tuple-element.13), calls=%async_computation.1 | async-start | bytes 589824 | tf_op jit(solution)/shard_map/all_to_all | solution.py:866
  49.8 0.6 broadcast_in_dim.8.earlier
  50.3 0.0 copy-done.5
  50.3 10.2 %pair_forces.3._.earlier = f32[3,1,512]{2,1,0:T(1,128)} custom-call(s32[1,3,1,32]{3,2,1,0:T(1,128)} %bitcast.20, f32[3,5,1024]{2,1,0:T(8,128)} %copy-done.4, f32[3,5,1024]{2,1,0:T(8,128)} %copy-done.5, f32[3,5,1024]{2,1,0:T(8,128)} %copy-done.3, f32[3,1,128]{2,1,0:T(1,128)} %broadcast_in_dim.8.earlier), custom_call_target="tpu_custom_call" | custom-call | flops 33030144 | bytes 204800 | tf_op jit(solution)/shard_map/pair_forces/pallas_call | solution.py:996
  60.5 0.0 all-to-all-done.1.incoming_hbm
  60.5 0.0 copy-start
  60.5 0.7 copy-done
  61.3 10.2 %interface_solve.1 = f32[288,1,256]{2,1,0:T(1,128)} custom-call(s32[1]{0:T(128)} %bitcast.6.first_mode, f32[288]{0:T(512)} %constant.51.clone.stiff_z, f32[3,1,512]{2,1,0:T(1,128)} %pair_forces.3._.earlier, f32[288,1,256]{2,1,0:T(1,128)} %copy-done, bf16[96,192]{1,0:T(8,128)(2,1)} %constant.52.clone.gather_hbm, f32[512,384]{1,0:T(8,128)} %constant.53.clone.along_y_hbm, ...), custom_call_target="tpu_custom_call" | custom-call | tf_op jit(solution)/shard_map/interface_solve/pallas_call | solution.py:887
  71.5 6.0 %all-to-all-start.2 = ((f32[288,1,256]{2,1,0:T(1,128)}), f32[288,1,256]{2,1,0:T(1,128)S(1)}, u32[]{:S(2)}, u32[]{:S(2)}) async-start(f32[288,1,256]{2,1,0:T(1,128)} %interface_solve.1), calls=%async_computation.2 | async-start | bytes 589824 | tf_op jit(solution)/shard_map/all_to_all | solution.py:908
  77.5 6.0 %pair_forces.4._.earlier = f32[3,1,768]{2,1,0:T(1,128)} custom-call(s32[1,3,1,32]{3,2,1,0:T(1,128)} %bitcast.21, f32[3,5,1024]{2,1,0:T(8,128)} %copy-done.4, f32[3,5,1024]{2,1,0:T(8,128)} %copy-done.5, f32[3,5,1024]{2,1,0:T(8,128)} %copy-done.3, f32[3,1,512]{2,1,0:T(1,128)} %pair_forces.3._.earlier), custom_call_target="tpu_custom_call" | custom-call | flops 16515072 | bytes 204800 | tf_op jit(solution)/shard_map/pair_forces/pallas_call | solution.py:996
  83.5 0.0 copy-start.6
  83.5 4.4 %all-to-all-done.2.message_hbm = f32[288,1,256]{2,1,0:T(1,128)S(1)} async-done(((f32[288,1,256]{2,1,0:T(1,128)}), f32[288,1,256]{2,1,0:T(1,128)S(1)}, u32[]{:S(2)}, u32[]{:S(2)}) %all-to-all-start.2) | async-done | bytes 294944 | tf_op jit(solution)/shard_map/all_to_all | solution.py:908
  87.9 0.0 copy-start.1
  87.9 0.7 copy-done.1
  88.7 22.3 %backward_solve.1 = (f32[36,72,288]{2,1,0:T(8,128)}, f32[256,128]{1,0:T(8,128)}) custom-call(s32[256,128]{1,0:T(8,128)} %get-tuple-element.12.places_hbm, f32[288,1,256]{2,1,0:T(1,128)} %copy-done.1, f32[384,256]{1,0:T(8,128)} %constant.50.clone.refs_6_.interface_hbm, f32[72,384]{1,0:T(8,128)} %constant.48.clone.refs_4_.diagonal_hbm, ...), custom_call_target="tpu_custom_call" | custom-call | tf_op jit(solution)/shard_map/backward_solve/pallas_call | solution.py:910
  110.9 3.4 %all-to-all-start.3 = ((f32[8,32,128]{2,1,0:T(8,128)}), f32[8,32,128]{2,1,0:T(8,128)S(1)}, u32[]{:S(2)}, u32[]{:S(2)}) async-start(f32[8,32,128]{2,1,0:T(8,128)} %bitcast.15), calls=%async_computation.3 | async-start | bytes 262144 | tf_op jit(solution)/shard_map/all_to_all | solution.py:1018
  114.3 6.0 %pair_forces.5 = f32[3,1,1024]{2,1,0:T(1,128)} custom-call(s32[1,3,1,32]{3,2,1,0:T(1,128)} %bitcast.22, f32[3,5,1024]{2,1,0:T(8,128)} %copy-done.4, f32[3,5,1024]{2,1,0:T(8,128)} %copy-done.5, f32[3,5,1024]{2,1,0:T(8,128)} %copy-done.3, f32[3,1,768]{2,1,0:T(1,128)} %pair_forces.4._.earlier), custom_call_target="tpu_custom_call" | custom-call | flops 16515072 | bytes 204800 | tf_op jit(solution)/shard_map/pair_forces/pallas_call | solution.py:996
  120.3 0.0 all-to-all-done.3
  120.3 0.0 copy-done.6
  120.3 0.1 slice_select_fusion
  120.4 0.7 reshape.33
  (3 shorter events, 0.0 us)
Async XLA Ops:
  2.3 6.9 %collective-permute-start = (f32[1,5,1024]{2,1,0:T(8,128)}, f32[1,5,1024]{2,1,0:T(8,128)S(1)}, u32[]{:S(2)}, u32[]{:S(2)}) collective-permute-start(f32[1,5,1024]{2,1,0:T(8,128)} %get-tuple-element.11), channel_id=1, source_target_pairs={{0,4},{4,8},{8,12},{12,16},{16,20},{20,24},{24,28},{28,0},{1,5},{5... | collective-permute-start | bytes 61448 | tf_op jit(solution)/shard_map/ppermute | solution.py:947
  2.7 7.2 %collective-permute-start.1 = (f32[1,5,1024]{2,1,0:T(8,128)}, f32[1,5,1024]{2,1,0:T(8,128)S(1)}, u32[]{:S(2)}, u32[]{:S(2)}) collective-permute-start(f32[1,5,1024]{2,1,0:T(8,128)} %get-tuple-element.11), channel_id=1, source_target_pairs={{0,28},{4,0},{8,4},{12,8},{16,12},{20,16},{24,20},{28,24},{1,29},{... | collective-permute-start | bytes 61448 | tf_op jit(solution)/shard_map/ppermute | solution.py:947
  5.6 15.2 %all-to-all-start = ((f32[8,32,128]{2,1,0:T(8,128)}), f32[8,32,128]{2,1,0:T(8,128)S(1)}, u32[]{:S(2)}, u32[]{:S(2)}) async-start(f32[8,32,128]{2,1,0:T(8,128)} %bitcast.14), calls=%async_computation | async-start | bytes 262144 | tf_op jit(solution)/shard_map/all_to_all | solution.py:984
  10.0 40.4 %copy-start.5 = (f32[3,5,1024]{2,1,0:T(8,128)}, f32[3,5,1024]{2,1,0:T(8,128)S(1)}, u32[]{:S(2)}) copy-start(f32[3,5,1024]{2,1,0:T(8,128)S(1)} %constant_dynamic-update-slice_fusion.middle) | copy-start | bytes 184324
  10.0 7.4 %collective-permute-start.3 = (f32[3,5,1024]{2,1,0:T(8,128)S(1)}, f32[3,5,1024]{2,1,0:T(8,128)S(1)}, u32[]{:S(2)}, u32[]{:S(2)}) collective-permute-start(f32[3,5,1024]{2,1,0:T(8,128)S(1)} %constant_dynamic-update-slice_fusion.middle), channel_id=1, source_target_pairs={{0,3},{1,0},{2,1},{3,2},{4,7},{5,4},{6,5},{7,6},{8,11},{9,8},{10,9... | collective-permute-start | bytes 184328 | tf_op jit(solution)/shard_map/ppermute | solution.py:947
  14.2 6.6 %collective-permute-start.2 = (f32[3,5,1024]{2,1,0:T(8,128)S(1)}, f32[3,5,1024]{2,1,0:T(8,128)S(1)}, u32[]{:S(2)}, u32[]{:S(2)}) collective-permute-start(f32[3,5,1024]{2,1,0:T(8,128)S(1)} %constant_dynamic-update-slice_fusion.middle), channel_id=1, source_target_pairs={{0,1},{1,2},{2,3},{3,0},{4,5},{5,6},{6,7},{7,4},{8,9},{9,10},{10,1... | collective-permute-start | bytes 184328 | tf_op jit(solution)/shard_map/ppermute | solution.py:947
  17.4 3.4 %copy-start.3 = (f32[3,5,1024]{2,1,0:T(8,128)}, f32[3,5,1024]{2,1,0:T(8,128)S(1)}, u32[]{:S(2)}) copy-start(f32[3,5,1024]{2,1,0:T(8,128)S(1)} %collective-permute-done.3.refs_8_.high) | copy-start | bytes 184324
  20.8 0.6 copy-start.4
  20.8 0.7 copy-start.2
  47.1 13.4 %all-to-all-start.1 = ((f32[288,1,256]{2,1,0:T(1,128)}), f32[288,1,256]{2,1,0:T(1,128)S(1)}, u32[]{:S(2)}, u32[]{:S(2)}) async-start(f32[288,1,256]{2,1,0:T(1,128)} %get-tuple-element.13), calls=%async_computation.1 | async-start | bytes 589824 | tf_op jit(solution)/shard_map/all_to_all | solution.py:866
  60.5 0.7 copy-start
  71.5 16.4 %all-to-all-start.2 = ((f32[288,1,256]{2,1,0:T(1,128)}), f32[288,1,256]{2,1,0:T(1,128)S(1)}, u32[]{:S(2)}, u32[]{:S(2)}) async-start(f32[288,1,256]{2,1,0:T(1,128)} %interface_solve.1), calls=%async_computation.2 | async-start | bytes 589824 | tf_op jit(solution)/shard_map/all_to_all | solution.py:908
  83.5 36.8 %copy-start.6 = (s32[1,1,32]{2,1,0:T(1,128)S(1)}, s32[1,1,32]{2,1,0:T(1,128)}, u32[]{:S(2)}) copy-start(s32[1,1,32]{2,1,0:T(1,128)} %param.29) | copy-start | bytes 388
  87.9 0.7 copy-start.1
  110.9 9.4 %all-to-all-start.3 = ((f32[8,32,128]{2,1,0:T(8,128)}), f32[8,32,128]{2,1,0:T(8,128)S(1)}, u32[]{:S(2)}, u32[]{:S(2)}) async-start(f32[8,32,128]{2,1,0:T(8,128)} %bitcast.15), calls=%async_computation.3 | async-start | bytes 262144 | tf_op jit(solution)/shard_map/all_to_all | solution.py:1018

commit v4 on v3

--- a/solution.py
+++ b/solution.py
@@ -12,7 +12,7 @@
 SCREENING = 0.003
 HIGH_ACCURACY = lax.Precision.HIGHEST
 VMEM_MIB = 60
-BATCH = 8
+BATCH = 16
 MIB = 1024 * 1024
 
 
@@ -78,11 +78,15 @@
         out[: self.grid, : self.grid] = cas_matrix(self.grid) / np.sqrt(self.grid)
         return out
 
-    def diagonal(self):
+    def elimination_factors(self):
         z_part = np.zeros(self.lanes)
         z_part[: self.grid] = stiffness(self.grid, self.grid)
         y_part = stiffness(self.y_pad, 2 * self.y_len)
-        return 2.0 + y_part[:, None] + z_part[None, :] + SCREENING
+        diagonal = 2.0 + y_part[:, None] + z_part[None, :] + SCREENING
+        out = np.zeros((self.x_len, self.y_pad, self.lanes))
+        for x in range(1, self.x_len):
+            out[x] = 1.0 / (diagonal - out[x - 1])
+        return out
 
     def edge_weights(self):
         sine_y = self.y_matrix()
@@ -138,13 +142,25 @@
         out = np.zeros((self.j_pad, self.lanes))
         for j in range(self.n_gy):
             out[j, : self.grid] = full[(j * ratio) % self.grid]
-        return out
+        return np.where(np.abs(out - np.round(out)) < 1e-9, np.round(out), out)
 
 
 def dot(a, b, dims=((1,), (0,)), precision=None):
     return lax.dot_general(
         a, b, (dims, ((), ())), precision=precision, preferred_element_type=jnp.float32
     )
+
+
+def value_parts(value, axis, count):
+    high = value.astype(jnp.bfloat16).astype(jnp.float32)
+    return jnp.concatenate([high] * (count - 1) + [value - high], axis=axis)
+
+
+def table_parts(matrix, axis):
+    high, low = split_pair(matrix)
+    if low.astype(np.float32).any():
+        return np.concatenate([high, low, high], axis=axis)
+    return np.concatenate([high, high], axis=axis)
 
 
 def value_triple(value, axis):
@@ -241,7 +257,7 @@
         density_hbm,
         z_full_hbm,
         y_table_hbm,
-        diagonal_hbm,
+        factors_hbm,
         edge_y_hbm,
         interface_hbm,
         _,
@@ -251,7 +267,6 @@
         message,
         added,
         solved,
-        factors,
         stack,
         heads,
         edge_rows,
@@ -261,7 +276,7 @@
         z_full,
         z_table,
         y_table,
-        diagonal,
+        factors,
         edge_y,
         interface_full,
         interface,
@@ -281,7 +296,7 @@
             (density_hbm, density),
             (z_full_hbm, z_full),
             (y_table_hbm, y_table),
-            (diagonal_hbm, diagonal),
+            (factors_hbm, factors),
             (edge_y_hbm, edge_y),
             (interface_hbm, interface_full),
         ],
@@ -383,17 +398,14 @@
         far_weight = edge_y[1]
 
         def eliminate(step, carry):
-            factor, value = carry
             x = step + 1
-            factor = inverse(diagonal[:, lanes] - factor)
-            value = (spectrum.at[x][:, lanes] + value) * factor
-            factors.at[x][...] = factor
+            value = (spectrum.at[x][:, lanes] + carry) * factors.at[x][:, lanes]
             solved.at[x][...] = value
-            return factor, value
+            return value
 
         def substitute(step, value):
             x = x_len - 1 - step
-            value = solved.at[x][...] + factors.at[x][...] * value
+            value = solved.at[x][...] + factors.at[x][:, lanes] * value
             near_row = jnp.sum(value * near_weight, axis=0, keepdims=True)
             far_row = jnp.sum(value * far_weight, axis=0, keepdims=True)
             edge_rows[0, pl.ds(x, 1), :] = near_row + heads[tile, pl.ds(x, 1), :]
@@ -401,7 +413,7 @@
             return value
 
         zero = jnp.zeros((y_pad, 128), jnp.float32)
-        chunked_loop(x_len - 1, 5, eliminate, (zero, zero))
+        chunked_loop(x_len - 1, 5, eliminate, zero)
         stack[y_pad : 2 * y_pad, lanes] = solved[x_len - 1]
         stack[0:y_pad, lanes] = chunked_loop(x_len - 1, 5, substitute, zero)
         for side in range(2):
@@ -503,15 +515,14 @@
     )
 
     def solve(mode, carry):
-        across = folded_x[mode, :, :grid]
-        high = across.astype(jnp.bfloat16).astype(jnp.float32)
-        across = jnp.concatenate([high, high, across - high], axis=0)
+        across = value_parts(folded_x[mode, :, :grid], 0, expand.shape[0] // j_pad)
         spread = dot(across, expand[...], ((0,), (0,)))
         number = spread.reshape(groups, kx_pad, lane_count) + folded_y[mode][None]
         bottom = stiff_x[...] + (stiff_y[...] + stiff_z[first_mode[0] + mode])
         value = number * inverse(bottom).reshape(groups, kx_pad, lane_count)
         folded_y[mode] = jnp.sum(value, axis=0)
-        value = value_triple(value.reshape(grid, lane_count), 1)
+        value = value_parts(value.reshape(grid, lane_count), 1, expand.shape[0] // j_pad)
+        value = value.astype(jnp.bfloat16)
         folded_x[mode, :, :grid] = dot(expand_back[...], value, ((1,), (1,)))
         return carry
 
@@ -548,7 +559,7 @@
     places_hbm,
     message_hbm,
     interface_hbm,
-    diagonal_hbm,
+    factors_hbm,
     edge_y_hbm,
     spectrum_hbm,
     y_table_hbm,
@@ -559,7 +570,6 @@
     lookup,
     work,
     solved,
-    factors,
     stack,
     heads,
     edge_rows,
@@ -570,7 +580,7 @@
     message,
     interface_full,
     interface,
-    diagonal,
+    factors,
     edge_y,
     spectrum,
     y_table,
@@ -587,7 +597,7 @@
             (message_hbm, message),
             (interface_hbm, interface_full),
             (places_hbm, places),
-            (diagonal_hbm, diagonal),
+            (factors_hbm, factors),
             (edge_y_hbm, edge_y),
             (spectrum_hbm, spectrum),
             (y_table_hbm, y_table),
@@ -616,24 +626,20 @@
         edge_rows[...] = stack[3 * y_pad + x_pad : 3 * y_pad + 2 * x_pad, lanes]
 
         def eliminate(step, carry):
-            factor, value = carry
             x = step + 1
-            factor = inverse(diagonal[:, lanes] - factor)
             load = spectrum.at[x][:, lanes] + near_weight * heads[tile, pl.ds(x, 1), :]
             load = load + far_weight * edge_rows[pl.ds(x, 1), :]
-            value = (load + value) * factor
-            factors.at[x][...] = factor
+            value = (load + carry) * factors.at[x][:, lanes]
             solved.at[x][...] = value
-            return factor, value
+            return value
 
         def substitute(step, value):
             x = x_len - 1 - step
-            value = solved.at[x][...] + factors.at[x][...] * value
+            value = solved.at[x][...] + factors.at[x][:, lanes] * value
             work.at[x][:, lanes] = value
             return value
 
-        zero = jnp.zeros((y_pad, 128), jnp.float32)
-        chunked_loop(x_len - 1, 5, eliminate, (zero, stack[0:y_pad, lanes]))
+        chunked_loop(x_len - 1, 5, eliminate, stack[0:y_pad, lanes])
         chunked_loop(x_len - 1, 5, substitute, stack[y_pad : 2 * y_pad, lanes])
     work[0] = jnp.zeros((y_pad, lane_count), jnp.float32)
 
@@ -671,9 +677,15 @@
         jnp.int32, shape, 1
     )
 
-    def sample(slot, carry):
+    def reduce_rows(rows, block):
+        found = jnp.sum(rows, axis=1, keepdims=True)
+        found = jnp.sum(jnp.where(own_lane, found, 0.0), axis=0, keepdims=True)
+        values[pl.ds(block, 1), :] = found
+
+    def sample(slot, before):
         block = blocks[slot]
         row_codes = places.at[block]
+        rows_before = picked[...]
         for first in range(0, block_atoms, 16):
             rows = []
             for atom in range(first, first + 16):
@@ -682,12 +694,16 @@
                 rows.append(jnp.where(lane_ids == (code & 127), row, 0.0))
             for k in range(16):
                 picked[first + k : first + k + 1, :] = rows[k]
-        found = jnp.sum(picked[...], axis=1, keepdims=True)
-        found = jnp.sum(jnp.where(own_lane, found, 0.0), axis=0, keepdims=True)
-        values[pl.ds(block, 1), :] = found
-        return carry
-
-    lax.fori_loop(0, count, sample, 0)
+        reduce_rows(rows_before, before)
+        return block
+
+    picked[...] = jnp.zeros(picked.shape, jnp.float32)
+    last = lax.fori_loop(0, count, sample, blocks[0])
+
+    @pl.when(count > 0)
+    def _():
+        reduce_rows(picked[...], last)
+
     potential_copy.wait()
 
 
@@ -818,13 +834,12 @@
     total = plan.parts * plan.modes
     z_full = f32(plan.z_matrix())
     y_table = table_triple(plan.y_matrix(), 1)
-    diagonal = f32(plan.diagonal())
+    factors = f32(plan.elimination_factors())
     edge_y = f32(plan.edge_weights())
     interface = f32(plan.interface_table())
     bf16 = jnp.bfloat16
     code_shape = codes.shape
     shared = [
-        buffer(x_len, y_pad, 128),
         buffer(x_len, y_pad, 128),
         buffer(plan.stack_rows, lanes),
         buffer(plan.lane_tiles, x_pad, 128),
@@ -848,7 +863,7 @@
             like(z_full),
             pltpu.VMEM((3 * lanes, lanes), bf16),
             like(y_table),
-            like(diagonal),
+            like(factors),
             like(edge_y),
             like(interface),
             pltpu.VMEM((3 * plan.stack_rows, 2 * half), bf16),
@@ -860,9 +875,9 @@
         ],
         compiler_params=limit(VMEM_MIB),
         name="forward_solve",
-    )(first_code, codes, density, z_full, y_table, diagonal, edge_y, interface, *neighbours)
-    half_tile = n_blocks * block_atoms // 2
-    first_pairs = pair_part(0, half_tile, None)
+    )(first_code, codes, density, z_full, y_table, factors, edge_y, interface, *neighbours)
+    eighth = n_blocks * block_atoms // 8
+    first_pairs = pair_part(0, 4 * eighth, None)
     incoming = lax.all_to_all(message, ("gx", "gy"), split_axis=0, concat_axis=0, tiled=True)
     gather = plan.gather_table()
     along_y, along_x = plan.line_tables()
@@ -878,8 +893,8 @@
         table_triple(gather, 1),
         f32(along_y),
         f32(along_x),
-        f32(table_triple(expand, 0)),
-        table_triple(expand, 1),
+        f32(table_parts(expand, 0)),
+        table_parts(expand, 1),
         f32(stiff[:, None] * grid),
         f32(padded_y * grid),
         table_triple(gather.T, 1),
@@ -906,7 +921,7 @@
         name="interface_solve",
     )(first_mode, f32((padded_z + SCREENING) * grid), first_pairs, incoming, *tables)
     returned = lax.all_to_all(outgoing, ("gx", "gy"), split_axis=0, concat_axis=0, tiled=True)
-    more_pairs = pair_part(half_tile, half_tile // 2, first_pairs)
+    more_pairs = pair_part(4 * eighth, 3 * eighth, first_pairs)
     potential, values = pl.pallas_call(
         functools.partial(backward_kernel, plan, n_blocks, block_atoms),
         out_shape=(shaped(x_len, y_len, grid), shaped(plan.n_gx * n_blocks, 128)),
@@ -926,7 +941,7 @@
             buffer(total, 1, 2 * half),
             like(interface),
             pltpu.VMEM((plan.stack_rows, 6 * half), bf16),
-            like(diagonal),
+            like(factors),
             like(edge_y),
             buffer(x_len, y_pad, lanes),
             like(y_table),
@@ -937,8 +952,8 @@
         ],
         compiler_params=limit(VMEM_MIB),
         name="backward_solve",
-    )(places, returned, interface, diagonal, edge_y, spectrum, y_table, z_full, more_pairs)
-    pair_force = pair_part(half_tile + half_tile // 2, half_tile // 2, more_pairs)
+    )(places, returned, interface, factors, edge_y, spectrum, y_table, z_full, more_pairs)
+    pair_force = pair_part(7 * eighth, eighth, more_pairs)
     return potential, values, pair_force
 
 

time: 121 us -> 114 us (0.942)
  Pallas kernels: 82 us -> 71.1 us
  starting transfers between devices: 23.2 us -> 26.9 us
    pallas_call x1, Pallas kernels: 22.3 us -> 16.2 us  [solve_poisson(): pl.pallas_call(functools.partial(backward_kernel, plan, n_blocks, block_a...]
    pallas_call x1, Pallas kernels: 25.7 us -> 21.4 us  [solve_poisson(): pl.pallas_call(functools.partial(forward_kernel, plan, n_blocks, block_at...]
    all_to_all x1, starting transfers between devices: 2.61 us -> 5.14 us  [solve_poisson(): lax.all_to_all(message, ('gx', 'gy'), split_axis=0, concat_axis=0, tiled=...]
    all_to_all x1, waiting for transfers between devices: 4.44 us -> 2.47 us  [solve_poisson(): lax.all_to_all(outgoing, ('gx', 'gy'), split_axis=0, concat_axis=0, tiled...]
    all_to_all x1, waiting for transfers between devices: 0.01 us -> 1.55 us  [body(): lax.all_to_all(values, 'gx', split_axis=0, concat_axis=0, tiled=True)]
    all_to_all x1, starting transfers between devices: 3.38 us -> 4.76 us  [body(): lax.all_to_all(values, 'gx', split_axis=0, concat_axis=0, tiled=True)]
  transfers between devices with their start and end apart: 8 -> 8, of which waited for: 3 -> 4; matrix products, arithmetic and copies ran while one was open for 1% -> 1% of each run, Pallas kernels for 18% -> 20%
where the time goes in v4:
time: 114 us
  Pallas kernels  71.1 us (62%)
  starting transfers between devices  26.9 us (24%)
  waiting for transfers between devices  10.6 us (9%)
  local copies, waits for them, and re-layouts  4.12 us (4%)
    pallas_call x3, Pallas kernels, pair_part(): pl.pallas_call(functools.partial(pair_kernel, n_blocks, block_atoms, list...  22.3 us
    pallas_call x1, Pallas kernels, solve_poisson(): pl.pallas_call(functools.partial(forward_kernel, plan, n_blocks, block_at...  21.4 us
    pallas_call x1, Pallas kernels, solve_poisson(): pl.pallas_call(functools.partial(backward_kernel, plan, n_blocks, block_a...  16.2 us
    pallas_call x1, Pallas kernels, solve_poisson(): pl.pallas_call(functools.partial(interface_kernel, plan), out_shape=shape...  9.54 us
    ppermute x4, starting transfers between devices, shifted(): lax.ppermute(block, axis, [(i, (i + step) % count) for i in range(count)])  7.58 us
    ppermute x4, waiting for transfers between devices, shifted(): lax.ppermute(block, axis, [(i, (i + step) % count) for i in range(count)])  6.58 us
    all_to_all x1, starting transfers between devices, solve_poisson(): lax.all_to_all(outgoing, ('gx', 'gy'), split_axis=0, concat_axis=0, tiled...  5.84 us
    all_to_all x1, starting transfers between devices, solve_poisson(): lax.all_to_all(message, ('gx', 'gy'), split_axis=0, concat_axis=0, tiled=...  5.14 us
  transfers between devices with their start and end apart: 8, of which 4 were waited for; matrix products, arithmetic and copies ran while one was open for 1% of the time, Pallas kernels for 20%

profile of v4, /device:TPU:0, one launch (start us, length us, event | category | flops | bytes accessed | tf_op | source)
XLA Modules:
  0.0 113.6 jit_solution(11501205431906926272)
XLA Ops:
  0.6 1.6 %prepare_atoms.1 = (f32[256,128]{1,0:T(8,128)}, f32[1,5,1024]{2,1,0:T(8,128)}) custom-call(s32[1,32]{1,0:T(1,128)} %bitcast.17, s32[1,32]{1,0:T(1,128)} %bitcast.19, f32[16]{0:T(128)} %type_radius.1, f32[1,3,1,1024]{3,2,1,0:T(1,128)} %bitcast.16, f32[1,1,1024]{2,1,0:T(1,128)} %charge.1, s32[1,1,1024]{2,1,0:T(1,128)} %types.1, s32[1,1,1024]{2,1,0:T(1,128)} %cells.1), custom_call_target="tpu_custom_call" | custom-call | tf_op jit(solution)/shard_map/prepare_atoms/pallas_call | solution.py:982
  2.3 0.5 collective-permute-start
  2.7 2.9 %collective-permute-start.1 = (f32[1,5,1024]{2,1,0:T(8,128)}, f32[1,5,1024]{2,1,0:T(8,128)S(1)}, u32[]{:S(2)}, u32[]{:S(2)}) collective-permute-start(f32[1,5,1024]{2,1,0:T(8,128)} %get-tuple-element.11), channel_id=1, source_target_pairs={{0,28},{4,0},{8,4},{12,8},{16,12},{20,16},{24,20},{28,24},{1,29},{... | collective-permute-start | bytes 61448 | tf_op jit(solution)/shard_map/ppermute | solution.py:962
  5.6 3.6 %all-to-all-start = ((f32[8,32,128]{2,1,0:T(8,128)}), f32[8,32,128]{2,1,0:T(8,128)S(1)}, u32[]{:S(2)}, u32[]{:S(2)}) async-start(f32[8,32,128]{2,1,0:T(8,128)} %bitcast.14), calls=%async_computation | async-start | bytes 262144 | tf_op jit(solution)/shard_map/all_to_all | solution.py:999
  9.2 0.0 collective-permute-done
  9.2 0.8 constant_dynamic-update-slice_fusion.1
  10.0 0.0 collective-permute-done.1
  10.0 0.0 copy-start.5
  10.0 4.2 %collective-permute-start.3 = (f32[3,5,1024]{2,1,0:T(8,128)S(1)}, f32[3,5,1024]{2,1,0:T(8,128)S(1)}, u32[]{:S(2)}, u32[]{:S(2)}) collective-permute-start(f32[3,5,1024]{2,1,0:T(8,128)S(1)} %constant_dynamic-update-slice_fusion.middle), channel_id=1, source_target_pairs={{0,3},{1,0},{2,1},{3,2},{4,7},{5,4},{6,5},{7,6},{8,11},{9,8},{10,9... | collective-permute-start | bytes 184328 | tf_op jit(solution)/shard_map/ppermute | solution.py:962
  14.2 0.0 collective-permute-start.2
  14.2 3.2 %collective-permute-done.3.refs_8_.high = f32[3,5,1024]{2,1,0:T(8,128)S(1)} collective-permute-done((f32[3,5,1024]{2,1,0:T(8,128)S(1)}, f32[3,5,1024]{2,1,0:T(8,128)S(1)}, u32[]{:S(2)}, u32[]{:S(2)}) %collective-permute-start.3) | collective-permute-done | bytes 61472 | tf_op jit(solution)/shard_map/ppermute | solution.py:962
  17.4 0.0 copy-start.3
  17.4 3.4 %collective-permute-done.2.refs_7_.low = f32[3,5,1024]{2,1,0:T(8,128)S(1)} collective-permute-done((f32[3,5,1024]{2,1,0:T(8,128)S(1)}, f32[3,5,1024]{2,1,0:T(8,128)S(1)}, u32[]{:S(2)}, u32[]{:S(2)}) %collective-permute-start.2) | collective-permute-done | bytes 61472 | tf_op jit(solution)/shard_map/ppermute | solution.py:962
  20.8 0.0 copy-start.4
  20.8 0.0 all-to-all-done
  20.8 0.0 copy-start.2
  20.8 0.0 copy-done.3
  20.8 0.6 copy-done.4
  21.4 0.1 copy-done.2
  21.5 21.4 %forward_solve.1 = (f32[36,72,384]{2,1,0:T(8,128)}, s32[256,128]{1,0:T(8,128)}, f32[288,1,256]{2,1,0:T(1,128)}) custom-call(s32[1]{0:T(128)} %bitcast.first_code, f32[256,128]{1,0:T(8,128)} %bitcast.13, f32[36,72,288]{2,1,0:T(8,128)} %refs_1_.1, f32[384,384]{1,0:T(8,128)} %constant.46.clone.refs_2_.z_full_hbm, ...), custom_call_target="tpu_custom_call" | custom-call | tf_op jit(solution)/shard_map/forward_solve/pallas_call | solution.py:847
  42.9 5.1 %all-to-all-start.1 = ((f32[288,1,256]{2,1,0:T(1,128)}), f32[288,1,256]{2,1,0:T(1,128)S(1)}, u32[]{:S(2)}, u32[]{:S(2)}) async-start(f32[288,1,256]{2,1,0:T(1,128)} %get-tuple-element.13), calls=%async_computation.1 | async-start | bytes 589824 | tf_op jit(solution)/shard_map/all_to_all | solution.py:881
  48.1 0.6 broadcast_in_dim.8.earlier
  48.7 0.0 copy-done.5
  48.7 10.2 %pair_forces.3._.earlier = f32[3,1,512]{2,1,0:T(1,128)} custom-call(s32[1,3,1,32]{3,2,1,0:T(1,128)} %bitcast.20, f32[3,5,1024]{2,1,0:T(8,128)} %copy-done.4, f32[3,5,1024]{2,1,0:T(8,128)} %copy-done.5, f32[3,5,1024]{2,1,0:T(8,128)} %copy-done.3, f32[3,1,128]{2,1,0:T(1,128)} %broadcast_in_dim.8.earlier), custom_call_target="tpu_custom_call" | custom-call | flops 33030144 | bytes 204800 | tf_op jit(solution)/shard_map/pair_forces/pallas_call | solution.py:1011
  58.9 0.0 all-to-all-done.1.incoming_hbm
  58.9 0.0 copy-start.1
  58.9 0.7 copy-done.1
  59.6 9.5 %interface_solve.1 = f32[288,1,256]{2,1,0:T(1,128)} custom-call(s32[1]{0:T(128)} %bitcast.6.first_mode, f32[288]{0:T(512)} %constant.51.clone.stiff_z, f32[3,1,512]{2,1,0:T(1,128)} %pair_forces.3._.earlier, f32[288,1,256]{2,1,0:T(1,128)} %copy-done.1, bf16[96,192]{1,0:T(8,128)(2,1)} %constant.52.clone.gather_hbm, f32[512,384]{1,0:T(8,128)} %constant.53.clone.along_y_hbm, ...), custom_call_target="tpu_custom_call" | custom-call | tf_op jit(solution)/shard_map/interface_solve/pallas_call | solution.py:902
  69.1 5.8 %all-to-all-start.2 = ((f32[288,1,256]{2,1,0:T(1,128)}), f32[288,1,256]{2,1,0:T(1,128)S(1)}, u32[]{:S(2)}, u32[]{:S(2)}) async-start(f32[288,1,256]{2,1,0:T(1,128)} %interface_solve.1), calls=%async_computation.2 | async-start | bytes 589824 | tf_op jit(solution)/shard_map/all_to_all | solution.py:923
  75.0 8.1 %pair_forces.4._.earlier = f32[3,1,896]{2,1,0:T(1,128)} custom-call(s32[1,3,1,32]{3,2,1,0:T(1,128)} %bitcast.21, f32[3,5,1024]{2,1,0:T(8,128)} %copy-done.4, f32[3,5,1024]{2,1,0:T(8,128)} %copy-done.5, f32[3,5,1024]{2,1,0:T(8,128)} %copy-done.3, f32[3,1,512]{2,1,0:T(1,128)} %pair_forces.3._.earlier), custom_call_target="tpu_custom_call" | custom-call | flops 24772608 | bytes 204800 | tf_op jit(solution)/shard_map/pair_forces/pallas_call | solution.py:1011
  83.1 2.5 %all-to-all-done.2.message_hbm = f32[288,1,256]{2,1,0:T(1,128)S(1)} async-done(((f32[288,1,256]{2,1,0:T(1,128)}), f32[288,1,256]{2,1,0:T(1,128)S(1)}, u32[]{:S(2)}, u32[]{:S(2)}) %all-to-all-start.2) | async-done | bytes 294944 | tf_op jit(solution)/shard_map/all_to_all | solution.py:923
  85.6 0.0 copy-start
  85.6 0.7 copy-done
  86.3 0.0 copy-start.6
  86.3 16.2 %backward_solve.1 = (f32[36,72,288]{2,1,0:T(8,128)}, f32[256,128]{1,0:T(8,128)}) custom-call(s32[256,128]{1,0:T(8,128)} %get-tuple-element.12.places_hbm, f32[288,1,256]{2,1,0:T(1,128)} %copy-done, f32[384,256]{1,0:T(8,128)} %constant.50.clone.refs_6_.interface_hbm, f32[36,72,384]{2,1,0:T(8,128)} %constant.48.clone.refs_4_.factors_hbm, ...), custom_call_target="tpu_custom_call" | custom-call | tf_op jit(solution)/shard_map/backward_solve/pallas_call | solution.py:925
  102.5 4.8 %all-to-all-start.3 = ((f32[8,32,128]{2,1,0:T(8,128)}), f32[8,32,128]{2,1,0:T(8,128)S(1)}, u32[]{:S(2)}, u32[]{:S(2)}) async-start(f32[8,32,128]{2,1,0:T(8,128)} %bitcast.15), calls=%async_computation.3 | async-start | bytes 262144 | tf_op jit(solution)/shard_map/all_to_all | solution.py:1033
  107.3 4.0 %pair_forces.5 = f32[3,1,1024]{2,1,0:T(1,128)} custom-call(s32[1,3,1,32]{3,2,1,0:T(1,128)} %bitcast.22, f32[3,5,1024]{2,1,0:T(8,128)} %copy-done.4, f32[3,5,1024]{2,1,0:T(8,128)} %copy-done.5, f32[3,5,1024]{2,1,0:T(8,128)} %copy-done.3, f32[3,1,896]{2,1,0:T(1,128)} %pair_forces.4._.earlier), custom_call_target="tpu_custom_call" | custom-call | flops 8257536 | bytes 204800 | tf_op jit(solution)/shard_map/pair_forces/pallas_call | solution.py:1011
  111.3 1.5 %all-to-all-done.3 = f32[8,32,128]{2,1,0:T(8,128)S(1)} async-done(((f32[8,32,128]{2,1,0:T(8,128)}), f32[8,32,128]{2,1,0:T(8,128)S(1)}, u32[]{:S(2)}, u32[]{:S(2)}) %all-to-all-start.3) | async-done | bytes 131104 | tf_op jit(solution)/shard_map/all_to_all | solution.py:1033
  112.8 0.0 copy-done.6
  112.8 0.1 slice_select_fusion
  112.9 0.7 reshape.33
  (3 shorter events, 0.0 us)
Async XLA Ops:
  2.3 6.9 %collective-permute-start = (f32[1,5,1024]{2,1,0:T(8,128)}, f32[1,5,1024]{2,1,0:T(8,128)S(1)}, u32[]{:S(2)}, u32[]{:S(2)}) collective-permute-start(f32[1,5,1024]{2,1,0:T(8,128)} %get-tuple-element.11), channel_id=1, source_target_pairs={{0,4},{4,8},{8,12},{12,16},{16,20},{20,24},{24,28},{28,0},{1,5},{5... | collective-permute-start | bytes 61448 | tf_op jit(solution)/shard_map/ppermute | solution.py:962
  2.7 7.2 %collective-permute-start.1 = (f32[1,5,1024]{2,1,0:T(8,128)}, f32[1,5,1024]{2,1,0:T(8,128)S(1)}, u32[]{:S(2)}, u32[]{:S(2)}) collective-permute-start(f32[1,5,1024]{2,1,0:T(8,128)} %get-tuple-element.11), channel_id=1, source_target_pairs={{0,28},{4,0},{8,4},{12,8},{16,12},{20,16},{24,20},{28,24},{1,29},{... | collective-permute-start | bytes 61448 | tf_op jit(solution)/shard_map/ppermute | solution.py:962
  5.6 15.2 %all-to-all-start = ((f32[8,32,128]{2,1,0:T(8,128)}), f32[8,32,128]{2,1,0:T(8,128)S(1)}, u32[]{:S(2)}, u32[]{:S(2)}) async-start(f32[8,32,128]{2,1,0:T(8,128)} %bitcast.14), calls=%async_computation | async-start | bytes 262144 | tf_op jit(solution)/shard_map/all_to_all | solution.py:999
  10.0 38.7 %copy-start.5 = (f32[3,5,1024]{2,1,0:T(8,128)}, f32[3,5,1024]{2,1,0:T(8,128)S(1)}, u32[]{:S(2)}) copy-start(f32[3,5,1024]{2,1,0:T(8,128)S(1)} %constant_dynamic-update-slice_fusion.middle) | copy-start | bytes 184324
  10.0 7.4 %collective-permute-start.3 = (f32[3,5,1024]{2,1,0:T(8,128)S(1)}, f32[3,5,1024]{2,1,0:T(8,128)S(1)}, u32[]{:S(2)}, u32[]{:S(2)}) collective-permute-start(f32[3,5,1024]{2,1,0:T(8,128)S(1)} %constant_dynamic-update-slice_fusion.middle), channel_id=1, source_target_pairs={{0,3},{1,0},{2,1},{3,2},{4,7},{5,4},{6,5},{7,6},{8,11},{9,8},{10,9... | collective-permute-start | bytes 184328 | tf_op jit(solution)/shard_map/ppermute | solution.py:962
  14.2 6.6 %collective-permute-start.2 = (f32[3,5,1024]{2,1,0:T(8,128)S(1)}, f32[3,5,1024]{2,1,0:T(8,128)S(1)}, u32[]{:S(2)}, u32[]{:S(2)}) collective-permute-start(f32[3,5,1024]{2,1,0:T(8,128)S(1)} %constant_dynamic-update-slice_fusion.middle), channel_id=1, source_target_pairs={{0,1},{1,2},{2,3},{3,0},{4,5},{5,6},{6,7},{7,4},{8,9},{9,10},{10,1... | collective-permute-start | bytes 184328 | tf_op jit(solution)/shard_map/ppermute | solution.py:962
  17.4 3.4 %copy-start.3 = (f32[3,5,1024]{2,1,0:T(8,128)}, f32[3,5,1024]{2,1,0:T(8,128)S(1)}, u32[]{:S(2)}) copy-start(f32[3,5,1024]{2,1,0:T(8,128)S(1)} %collective-permute-done.3.refs_8_.high) | copy-start | bytes 184324
  20.8 0.6 copy-start.4
  20.8 0.7 copy-start.2
  42.9 15.9 %all-to-all-start.1 = ((f32[288,1,256]{2,1,0:T(1,128)}), f32[288,1,256]{2,1,0:T(1,128)S(1)}, u32[]{:S(2)}, u32[]{:S(2)}) async-start(f32[288,1,256]{2,1,0:T(1,128)} %get-tuple-element.13), calls=%async_computation.1 | async-start | bytes 589824 | tf_op jit(solution)/shard_map/all_to_all | solution.py:881
  58.9 0.7 copy-start.1
  69.1 16.4 %all-to-all-start.2 = ((f32[288,1,256]{2,1,0:T(1,128)}), f32[288,1,256]{2,1,0:T(1,128)S(1)}, u32[]{:S(2)}, u32[]{:S(2)}) async-start(f32[288,1,256]{2,1,0:T(1,128)} %interface_solve.1), calls=%async_computation.2 | async-start | bytes 589824 | tf_op jit(solution)/shard_map/all_to_all | solution.py:923
  85.6 0.7 copy-start
  86.3 26.5 %copy-start.6 = (s32[1,1,32]{2,1,0:T(1,128)S(1)}, s32[1,1,32]{2,1,0:T(1,128)}, u32[]{:S(2)}) copy-start(s32[1,1,32]{2,1,0:T(1,128)} %param.29) | copy-start | bytes 388
  102.5 10.3 %all-to-all-start.3 = ((f32[8,32,128]{2,1,0:T(8,128)}), f32[8,32,128]{2,1,0:T(8,128)S(1)}, u32[]{:S(2)}, u32[]{:S(2)}) async-start(f32[8,32,128]{2,1,0:T(8,128)} %bitcast.15), calls=%async_computation.3 | async-start | bytes 262144 | tf_op jit(solution)/shard_map/all_to_all | solution.py:1033

commit v5 on v4

--- a/solution.py
+++ b/solution.py
@@ -260,7 +260,6 @@
         factors_hbm,
         edge_y_hbm,
         interface_hbm,
-        _,
         _,
         spectrum_hbm,
         places_hbm,
@@ -285,6 +284,7 @@
         places,
         blocks,
         sems,
+        *charges,
     ) = refs
     x_len, y_len, y_pad, x_pad = plan.x_len, plan.y_len, plan.y_pad, plan.x_pad
     grid, lane_count, planes = plan.grid, plan.lanes, plan.planes
@@ -303,6 +303,9 @@
         sems,
     )
     loads[0].wait()
+    charge_copies = [pltpu.make_async_copy(codes, target, sems.at[7]) for target in charges]
+    for copy in charge_copies:
+        copy.start()
     mark_places(codes, first_code[0], place_rows, block_atoms)
     place_copies = [
         pltpu.make_async_copy(place_rows, places, sems.at[8]),
@@ -319,16 +322,18 @@
     chunked_loop(plan.lane_tiles * x_len, 4, clear, 0)
     loads[2].wait()
     split_table(z_full, z_table, 0)
-    place_copies[0].wait()
+    for copy in [*charge_copies, place_copies[0]]:
+        copy.wait()
     count = list_owned(plan, places, blocks, plan.n_gx * n_blocks)
 
     def deposit(slot, carry):
         block = blocks[slot]
         row_codes = places.at[block]
-        charge_row = codes[pl.ds(block, 1), :]
+        charge_row = charges[0].at[block] if charges else codes[pl.ds(block, 1), :]
 
         def raised(code, k):
-            charge = charge_row[:, block_atoms + k : block_atoms + k + 1]
+            lane = block_atoms + k
+            charge = charge_row[lane] if charges else charge_row[:, lane : lane + 1]
             hit = jnp.where(lane_ids == (code & 127), charge, 0.0)
             return added[pl.ds(lax.shift_right_logical(code, 7), 1), :] + hit
 
@@ -828,6 +833,12 @@
     return pltpu.CompilerParams(vmem_limit_bytes=mib * MIB)
 
 
+def after(message, others):
+    lane = message.shape[2] - len(others)
+    marks = jnp.stack([other[0, 0, 0] for other in others]).reshape(1, 1, -1)
+    return lax.dynamic_update_slice(message, marks, (0, 0, lane))
+
+
 def solve_poisson(plan, density, codes, first_code, n_blocks, block_atoms, neighbours, pair_part):
     x_len, y_len, grid = density.shape
     y_pad, x_pad, half, lanes = plan.y_pad, plan.x_pad, plan.half, plan.lanes
@@ -851,7 +862,7 @@
             jax.ShapeDtypeStruct(code_shape, jnp.int32),
             shaped(total, 1, 2 * half),
         ),
-        in_specs=[SMEM] + [HBM] * 9,
+        in_specs=[SMEM] + [HBM] * 8,
         out_specs=(HBM, HBM, VMEM),
         scratch_shapes=[buffer(plan.lane_tiles * plan.planes, 128)]
         + shared
@@ -872,10 +883,12 @@
             pltpu.SMEM(code_shape, jnp.int32),
             pltpu.SMEM((code_shape[0],), jnp.int32),
             pltpu.SemaphoreType.DMA((11,)),
-        ],
+        ]
+        + [pltpu.SMEM(code_shape, jnp.float32)] * (code_shape[0] <= 512),
         compiler_params=limit(VMEM_MIB),
         name="forward_solve",
-    )(first_code, codes, density, z_full, y_table, factors, edge_y, interface, *neighbours)
+    )(first_code, codes, density, z_full, y_table, factors, edge_y, interface, neighbours[0])
+    message = after(message, neighbours[1:])
     eighth = n_blocks * block_atoms // 8
     first_pairs = pair_part(0, 4 * eighth, None)
     incoming = lax.all_to_all(message, ("gx", "gy"), split_axis=0, concat_axis=0, tiled=True)
@@ -1028,7 +1041,7 @@
         )(listing, below, triple, above, earlier)
 
     potential, values, pair_force = solve_poisson(
-        plan, qm_density, codes, first_code, n_blocks, block_atoms, (below, above), pair_part
+        plan, qm_density, codes, first_code, n_blocks, block_atoms, (triple, below, above), pair_part
     )
     values = lax.all_to_all(values, "gx", split_axis=0, concat_axis=0, tiled=True)
     sampled = jnp.sum(values.reshape(n_gx, n_blocks, 128), axis=0)[:, :block_atoms]

time: 114 us -> 117 us (1.026)
  local copies, waits for them, and re-layouts: 4.12 us -> 6.5 us
  starting transfers between devices: 26.9 us -> 28.9 us
  waiting for transfers between devices: 10.6 us -> 8.71 us
  other arithmetic: 0.08 us -> 1.49 us
    ppermute x4, waiting for transfers between devices: 6.58 us -> 4.28 us  [shifted(): lax.ppermute(block, axis, [(i, (i + step) % count) for i in range(count)])]
    all_to_all x1, starting transfers between devices: 5.14 us -> 6.84 us  [solve_poisson(): lax.all_to_all(message, ('gx', 'gy'), split_axis=0, concat_axis=0, tiled=...]
    reshape x0 -> x1, other arithmetic: none -> 1.41 us  [after(): marks = jnp.stack([other[0, 0, 0] for other in others]).reshape(1, 1, -1)]
    dynamic_update_slice x0 -> x1, local copies, waits for them, and re-layouts: none -> 1.28 us  [after(): return lax.dynamic_update_slice(message, marks, (0, 0, lane))]
  transfers between devices with their start and end apart: 8 -> 8, of which waited for: 4 -> 5; matrix products, arithmetic and copies ran while one was open for 1% -> 3% of each run, Pallas kernels for 20% -> 19%
where the time goes in v5:
time: 117 us
  Pallas kernels  70.2 us (60%)
  starting transfers between devices  28.9 us (25%)
  waiting for transfers between devices  8.71 us (7%)
  local copies, waits for them, and re-layouts  6.5 us (6%)
  other arithmetic  1.49 us (1%)
    pallas_call x3, Pallas kernels, pair_part(): pl.pallas_call(functools.partial(pair_kernel, n_blocks, block_atoms, list...  22.3 us
    pallas_call x1, Pallas kernels, solve_poisson(): pl.pallas_call(functools.partial(forward_kernel, plan, n_blocks, block_at...  20.8 us
    pallas_call x1, Pallas kernels, solve_poisson(): pl.pallas_call(functools.partial(backward_kernel, plan, n_blocks, block_a...  15.9 us
    pallas_call x1, Pallas kernels, solve_poisson(): pl.pallas_call(functools.partial(interface_kernel, plan), out_shape=shape...  9.54 us
    ppermute x4, starting transfers between devices, shifted(): lax.ppermute(block, axis, [(i, (i + step) % count) for i in range(count)])  7.75 us
    all_to_all x1, starting transfers between devices, solve_poisson(): lax.all_to_all(message, ('gx', 'gy'), split_axis=0, concat_axis=0, tiled=...  6.84 us
    all_to_all x1, starting transfers between devices, solve_poisson(): lax.all_to_all(outgoing, ('gx', 'gy'), split_axis=0, concat_axis=0, tiled...  5.84 us
    all_to_all x1, starting transfers between devices, body(): lax.all_to_all(values, 'gx', split_axis=0, concat_axis=0, tiled=True)  5.1 us
  transfers between devices with their start and end apart: 8, of which 5 were waited for; matrix products, arithmetic and copies ran while one was open for 3% of the time, Pallas kernels for 19%

profile of v5, /device:TPU:0, one launch (start us, length us, event | category | flops | bytes accessed | tf_op | source)
XLA Modules:
  0.0 116.6 jit_solution(8454314353789519713)
XLA Ops:
  0.6 1.6 %prepare_atoms.1 = (f32[256,128]{1,0:T(8,128)}, f32[1,5,1024]{2,1,0:T(8,128)}) custom-call(s32[1,32]{1,0:T(1,128)} %bitcast.21, s32[1,32]{1,0:T(1,128)} %bitcast.23, f32[16]{0:T(128)} %type_radius.1, f32[1,3,1,1024]{3,2,1,0:T(1,128)} %bitcast.20, f32[1,1,1024]{2,1,0:T(1,128)} %charge.1, s32[1,1,1024]{2,1,0:T(1,128)} %types.1, s32[1,1,1024]{2,1,0:T(1,128)} %cells.1), custom_call_target="tpu_custom_call" | custom-call | tf_op jit(solution)/shard_map/prepare_atoms/pallas_call | solution.py:995
  2.3 0.5 collective-permute-start
  2.7 2.9 %collective-permute-start.1 = (f32[1,5,1024]{2,1,0:T(8,128)}, f32[1,5,1024]{2,1,0:T(8,128)S(1)}, u32[]{:S(2)}, u32[]{:S(2)}) collective-permute-start(f32[1,5,1024]{2,1,0:T(8,128)} %get-tuple-element.11), channel_id=1, source_target_pairs={{0,28},{4,0},{8,4},{12,8},{16,12},{20,16},{24,20},{28,24},{1,29},{... | collective-permute-start | bytes 61448 | tf_op jit(solution)/shard_map/ppermute | solution.py:975
  5.6 1.8 %collective-permute-done = f32[1,5,1024]{2,1,0:T(8,128)S(1)} collective-permute-done((f32[1,5,1024]{2,1,0:T(8,128)}, f32[1,5,1024]{2,1,0:T(8,128)S(1)}, u32[]{:S(2)}, u32[]{:S(2)}) %collective-permute-start) | collective-permute-done | bytes 20512 | tf_op jit(solution)/shard_map/ppermute | solution.py:975
  7.4 0.8 constant_dynamic-update-slice_fusion.1
  8.2 0.0 collective-permute-done.1
  8.2 0.0 copy-start.3
  8.2 4.4 %collective-permute-start.3 = (f32[3,5,1024]{2,1,0:T(8,128)S(1)}, f32[3,5,1024]{2,1,0:T(8,128)S(1)}, u32[]{:S(2)}, u32[]{:S(2)}) collective-permute-start(f32[3,5,1024]{2,1,0:T(8,128)S(1)} %constant_dynamic-update-slice_fusion.refs_7_.middle), channel_id=1, source_target_pairs={{0,3},{1,0},{2,1},{3,2},{4,7},{5,4},{6,5},{7,6},{8,11},{9,8},{10,9... | collective-permute-start | bytes 184328 | tf_op jit(solution)/shard_map/ppermute | solution.py:975
  12.6 0.0 collective-permute-start.2
  12.6 3.4 %all-to-all-start = ((f32[8,32,128]{2,1,0:T(8,128)}), f32[8,32,128]{2,1,0:T(8,128)S(1)}, u32[]{:S(2)}, u32[]{:S(2)}) async-start(f32[8,32,128]{2,1,0:T(8,128)} %bitcast.18), calls=%async_computation | async-start | bytes 262144 | tf_op jit(solution)/shard_map/all_to_all | solution.py:1012
  16.0 0.0 collective-permute-done.3.high
  16.0 0.0 copy-start.5
  16.0 0.5 slice.13
  16.5 2.5 %collective-permute-done.2.low = f32[3,5,1024]{2,1,0:T(8,128)S(1)} collective-permute-done((f32[3,5,1024]{2,1,0:T(8,128)S(1)}, f32[3,5,1024]{2,1,0:T(8,128)S(1)}, u32[]{:S(2)}, u32[]{:S(2)}) %collective-permute-start.2) | collective-permute-done | bytes 61472 | tf_op jit(solution)/shard_map/ppermute | solution.py:975
  19.0 0.0 copy-start.6
  19.0 0.6 slice.12
  19.6 1.4 %maximum_bitcast_fusion = f32[1,1,2]{2,1,0:T(1,128)S(1)} fusion(f32[1]{0:T(128)} %bitcast.9, f32[1]{0:T(128)} %bitcast.8), kind=kLoop, calls=%fused_computation.5 | loop fusion | flops 2 | bytes 16 | tf_op jit(solution)/shard_map/reshape | solution.py:838
  21.0 0.4 all-to-all-done
  21.4 0.0 copy-start.2
  21.4 0.0 copy-done.3
  21.4 0.6 copy-done.2
  22.1 20.8 %forward_solve.1 = (f32[36,72,384]{2,1,0:T(8,128)}, s32[256,128]{1,0:T(8,128)}, f32[288,1,256]{2,1,0:T(1,128)}) custom-call(s32[1]{0:T(128)} %bitcast.first_code, f32[256,128]{1,0:T(8,128)} %bitcast.17, f32[36,72,288]{2,1,0:T(8,128)} %refs_1_.1, f32[384,384]{1,0:T(8,128)} %constant.50.clone.refs_2_.z_full_hbm, ...), custom_call_target="tpu_custom_call" | custom-call | tf_op jit(solution)/shard_map/forward_solve/pallas_call | solution.py:858
  42.9 1.3 %dynamic_update_slice.3 = f32[288,1,256]{2,1,0:T(1,128)} dynamic-update-slice(f32[288,1,256]{2,1,0:T(1,128)} %get-tuple-element.13, f32[1,1,2]{2,1,0:T(1,128)S(1)} %maximum_bitcast_fusion, s32[]{:T(128)} %constant.48.clone.1, s32[]{:T(128)} %constant.48.clone.1, s32[]{:T(128)} %constant.49.clone.1) | dynamic-update-slice | bytes 20 | tf_op jit(solution)/shard_map/dynamic_update_slice | solution.py:839
  44.2 6.8 %all-to-all-start.1 = ((f32[288,1,256]{2,1,0:T(1,128)}), f32[288,1,256]{2,1,0:T(1,128)S(1)}, u32[]{:S(2)}, u32[]{:S(2)}) async-start(f32[288,1,256]{2,1,0:T(1,128)} %dynamic_update_slice.3), calls=%async_computation.1 | async-start | bytes 589824 | tf_op jit(solution)/shard_map/all_to_all | solution.py:894
  51.1 0.6 broadcast_in_dim.8.earlier
  51.6 0.0 copy-done.5
  51.6 0.0 copy-done.6
  51.6 10.2 %pair_forces.3._.earlier = f32[3,1,512]{2,1,0:T(1,128)} custom-call(s32[1,3,1,32]{3,2,1,0:T(1,128)} %bitcast.24, f32[3,5,1024]{2,1,0:T(8,128)} %copy-done.6, f32[3,5,1024]{2,1,0:T(8,128)} %copy-done.3, f32[3,5,1024]{2,1,0:T(8,128)} %copy-done.5, f32[3,1,128]{2,1,0:T(1,128)} %broadcast_in_dim.8.earlier), custom_call_target="tpu_custom_call" | custom-call | flops 33030144 | bytes 204800 | tf_op jit(solution)/shard_map/pair_forces/pallas_call | solution.py:1024
  61.8 0.0 all-to-all-done.1.incoming_hbm
  61.9 0.0 copy-start.1
  61.9 0.7 copy-done.1
  62.6 9.5 %interface_solve.1 = f32[288,1,256]{2,1,0:T(1,128)} custom-call(s32[1]{0:T(128)} %bitcast.6.first_mode, f32[288]{0:T(512)} %constant.55.clone.stiff_z, f32[3,1,512]{2,1,0:T(1,128)} %pair_forces.3._.earlier, f32[288,1,256]{2,1,0:T(1,128)} %copy-done.1, bf16[96,192]{1,0:T(8,128)(2,1)} %constant.56.clone.gather_hbm, f32[512,384]{1,0:T(8,128)} %constant.57.clone.along_y_hbm, ...), custom_call_target="tpu_custom_call" | custom-call | tf_op jit(solution)/shard_map/interface_solve/pallas_call | solution.py:915
  72.1 5.8 %all-to-all-start.2 = ((f32[288,1,256]{2,1,0:T(1,128)}), f32[288,1,256]{2,1,0:T(1,128)S(1)}, u32[]{:S(2)}, u32[]{:S(2)}) async-start(f32[288,1,256]{2,1,0:T(1,128)} %interface_solve.1), calls=%async_computation.2 | async-start | bytes 589824 | tf_op jit(solution)/shard_map/all_to_all | solution.py:936
  78.0 8.1 %pair_forces.4._.earlier = f32[3,1,896]{2,1,0:T(1,128)} custom-call(s32[1,3,1,32]{3,2,1,0:T(1,128)} %bitcast.25, f32[3,5,1024]{2,1,0:T(8,128)} %copy-done.6, f32[3,5,1024]{2,1,0:T(8,128)} %copy-done.3, f32[3,5,1024]{2,1,0:T(8,128)} %copy-done.5, f32[3,1,512]{2,1,0:T(1,128)} %pair_forces.3._.earlier), custom_call_target="tpu_custom_call" | custom-call | flops 24772608 | bytes 204800 | tf_op jit(solution)/shard_map/pair_forces/pallas_call | solution.py:1024
  86.1 2.5 %all-to-all-done.2.message_hbm = f32[288,1,256]{2,1,0:T(1,128)S(1)} async-done(((f32[288,1,256]{2,1,0:T(1,128)}), f32[288,1,256]{2,1,0:T(1,128)S(1)}, u32[]{:S(2)}, u32[]{:S(2)}) %all-to-all-start.2) | async-done | bytes 294944 | tf_op jit(solution)/shard_map/all_to_all | solution.py:936
  88.6 0.0 copy-start
  88.6 0.7 copy-done
  89.3 0.0 copy-start.4
  89.3 15.9 %backward_solve.1 = (f32[36,72,288]{2,1,0:T(8,128)}, f32[256,128]{1,0:T(8,128)}) custom-call(s32[256,128]{1,0:T(8,128)} %get-tuple-element.12.places_hbm, f32[288,1,256]{2,1,0:T(1,128)} %copy-done, f32[384,256]{1,0:T(8,128)} %constant.54.clone.refs_6_.interface_hbm, f32[36,72,384]{2,1,0:T(8,128)} %constant.52.clone.refs_4_.factors_hbm, ...), custom_call_target="tpu_custom_call" | custom-call | tf_op jit(solution)/shard_map/backward_solve/pallas_call | solution.py:938
  105.1 5.1 %all-to-all-start.3 = ((f32[8,32,128]{2,1,0:T(8,128)}), f32[8,32,128]{2,1,0:T(8,128)S(1)}, u32[]{:S(2)}, u32[]{:S(2)}) async-start(f32[8,32,128]{2,1,0:T(8,128)} %bitcast.19), calls=%async_computation.3 | async-start | bytes 262144 | tf_op jit(solution)/shard_map/all_to_all | solution.py:1046
  110.2 4.0 %pair_forces.5 = f32[3,1,1024]{2,1,0:T(1,128)} custom-call(s32[1,3,1,32]{3,2,1,0:T(1,128)} %bitcast.26, f32[3,5,1024]{2,1,0:T(8,128)} %copy-done.6, f32[3,5,1024]{2,1,0:T(8,128)} %copy-done.3, f32[3,5,1024]{2,1,0:T(8,128)} %copy-done.5, f32[3,1,896]{2,1,0:T(1,128)} %pair_forces.4._.earlier), custom_call_target="tpu_custom_call" | custom-call | flops 8257536 | bytes 204800 | tf_op jit(solution)/shard_map/pair_forces/pallas_call | solution.py:1024
  114.2 1.5 %all-to-all-done.3 = f32[8,32,128]{2,1,0:T(8,128)S(1)} async-done(((f32[8,32,128]{2,1,0:T(8,128)}), f32[8,32,128]{2,1,0:T(8,128)S(1)}, u32[]{:S(2)}, u32[]{:S(2)}) %all-to-all-start.3) | async-done | bytes 131104 | tf_op jit(solution)/shard_map/all_to_all | solution.py:1046
  115.8 0.0 copy-done.4
  115.8 0.1 slice_select_fusion
  115.9 0.7 reshape.37
  (3 shorter events, 0.0 us)
Async XLA Ops:
  2.3 5.1 %collective-permute-start = (f32[1,5,1024]{2,1,0:T(8,128)}, f32[1,5,1024]{2,1,0:T(8,128)S(1)}, u32[]{:S(2)}, u32[]{:S(2)}) collective-permute-start(f32[1,5,1024]{2,1,0:T(8,128)} %get-tuple-element.11), channel_id=1, source_target_pairs={{0,4},{4,8},{8,12},{12,16},{16,20},{20,24},{24,28},{28,0},{1,5},{5... | collective-permute-start | bytes 61448 | tf_op jit(solution)/shard_map/ppermute | solution.py:975
  2.7 5.5 %collective-permute-start.1 = (f32[1,5,1024]{2,1,0:T(8,128)}, f32[1,5,1024]{2,1,0:T(8,128)S(1)}, u32[]{:S(2)}, u32[]{:S(2)}) collective-permute-start(f32[1,5,1024]{2,1,0:T(8,128)} %get-tuple-element.11), channel_id=1, source_target_pairs={{0,28},{4,0},{8,4},{12,8},{16,12},{20,16},{24,20},{28,24},{1,29},{... | collective-permute-start | bytes 61448 | tf_op jit(solution)/shard_map/ppermute | solution.py:975
  8.2 13.3 %copy-start.3 = (f32[3,5,1024]{2,1,0:T(8,128)}, f32[3,5,1024]{2,1,0:T(8,128)S(1)}, u32[]{:S(2)}) copy-start(f32[3,5,1024]{2,1,0:T(8,128)S(1)} %constant_dynamic-update-slice_fusion.refs_7_.middle) | copy-start | bytes 184324
  8.2 7.8 %collective-permute-start.3 = (f32[3,5,1024]{2,1,0:T(8,128)S(1)}, f32[3,5,1024]{2,1,0:T(8,128)S(1)}, u32[]{:S(2)}, u32[]{:S(2)}) collective-permute-start(f32[3,5,1024]{2,1,0:T(8,128)S(1)} %constant_dynamic-update-slice_fusion.refs_7_.middle), channel_id=1, source_target_pairs={{0,3},{1,0},{2,1},{3,2},{4,7},{5,4},{6,5},{7,6},{8,11},{9,8},{10,9... | collective-permute-start | bytes 184328 | tf_op jit(solution)/shard_map/ppermute | solution.py:975
  12.6 6.4 %collective-permute-start.2 = (f32[3,5,1024]{2,1,0:T(8,128)S(1)}, f32[3,5,1024]{2,1,0:T(8,128)S(1)}, u32[]{:S(2)}, u32[]{:S(2)}) collective-permute-start(f32[3,5,1024]{2,1,0:T(8,128)S(1)} %constant_dynamic-update-slice_fusion.refs_7_.middle), channel_id=1, source_target_pairs={{0,1},{1,2},{2,3},{3,0},{4,5},{5,6},{6,7},{7,4},{8,9},{9,10},{10,1... | collective-permute-start | bytes 184328 | tf_op jit(solution)/shard_map/ppermute | solution.py:975
  12.6 8.8 %all-to-all-start = ((f32[8,32,128]{2,1,0:T(8,128)}), f32[8,32,128]{2,1,0:T(8,128)S(1)}, u32[]{:S(2)}, u32[]{:S(2)}) async-start(f32[8,32,128]{2,1,0:T(8,128)} %bitcast.18), calls=%async_computation | async-start | bytes 262144 | tf_op jit(solution)/shard_map/all_to_all | solution.py:1012
  16.0 35.6 %copy-start.5 = (f32[3,5,1024]{2,1,0:T(8,128)}, f32[3,5,1024]{2,1,0:T(8,128)S(1)}, u32[]{:S(2)}) copy-start(f32[3,5,1024]{2,1,0:T(8,128)S(1)} %collective-permute-done.3.high) | copy-start | bytes 184324
  19.0 32.6 %copy-start.6 = (f32[3,5,1024]{2,1,0:T(8,128)}, f32[3,5,1024]{2,1,0:T(8,128)S(1)}, u32[]{:S(2)}) copy-start(f32[3,5,1024]{2,1,0:T(8,128)S(1)} %collective-permute-done.2.low) | copy-start | bytes 184324
  21.4 0.6 copy-start.2
  44.2 17.6 %all-to-all-start.1 = ((f32[288,1,256]{2,1,0:T(1,128)}), f32[288,1,256]{2,1,0:T(1,128)S(1)}, u32[]{:S(2)}, u32[]{:S(2)}) async-start(f32[288,1,256]{2,1,0:T(1,128)} %dynamic_update_slice.3), calls=%async_computation.1 | async-start | bytes 589824 | tf_op jit(solution)/shard_map/all_to_all | solution.py:894
  61.9 0.7 copy-start.1
  72.1 16.4 %all-to-all-start.2 = ((f32[288,1,256]{2,1,0:T(1,128)}), f32[288,1,256]{2,1,0:T(1,128)S(1)}, u32[]{:S(2)}, u32[]{:S(2)}) async-start(f32[288,1,256]{2,1,0:T(1,128)} %interface_solve.1), calls=%async_computation.2 | async-start | bytes 589824 | tf_op jit(solution)/shard_map/all_to_all | solution.py:936
  88.6 0.7 copy-start
  89.3 26.5 %copy-start.4 = (s32[1,1,32]{2,1,0:T(1,128)S(1)}, s32[1,1,32]{2,1,0:T(1,128)}, u32[]{:S(2)}) copy-start(s32[1,1,32]{2,1,0:T(1,128)} %param.29) | copy-start | bytes 388
  105.1 10.6 %all-to-all-start.3 = ((f32[8,32,128]{2,1,0:T(8,128)}), f32[8,32,128]{2,1,0:T(8,128)S(1)}, u32[]{:S(2)}, u32[]{:S(2)}) async-start(f32[8,32,128]{2,1,0:T(8,128)} %bitcast.19), calls=%async_computation.3 | async-start | bytes 262144 | tf_op jit(solution)/shard_map/all_to_all | solution.py:1046

commit v6 on v5

--- a/solution.py
+++ b/solution.py
@@ -833,10 +833,20 @@
     return pltpu.CompilerParams(vmem_limit_bytes=mib * MIB)
 
 
+def order_kernel(*refs):
+    pass
+
+
 def after(message, others):
-    lane = message.shape[2] - len(others)
-    marks = jnp.stack([other[0, 0, 0] for other in others]).reshape(1, 1, -1)
-    return lax.dynamic_update_slice(message, marks, (0, 0, lane))
+    return pl.pallas_call(
+        order_kernel,
+        out_shape=shaped(*message.shape),
+        in_specs=[HBM] + [VMEM] * len(others),
+        out_specs=HBM,
+        input_output_aliases={0: 0},
+        compiler_params=limit(VMEM_MIB),
+        name="order_message",
+    )(message, *others)
 
 
 def solve_poisson(plan, density, codes, first_code, n_blocks, block_atoms, neighbours, pair_part):
@@ -862,7 +872,7 @@
             jax.ShapeDtypeStruct(code_shape, jnp.int32),
             shaped(total, 1, 2 * half),
         ),
-        in_specs=[SMEM] + [HBM] * 8,
+        in_specs=[SMEM] + [HBM] * 7 + [VMEM],
         out_specs=(HBM, HBM, VMEM),
         scratch_shapes=[buffer(plan.lane_tiles * plan.planes, 128)]
         + shared
@@ -915,7 +925,7 @@
     outgoing = pl.pallas_call(
         functools.partial(interface_kernel, plan),
         out_shape=shaped(total, 1, 2 * half),
-        in_specs=[SMEM] * 2 + [HBM] * 10,
+        in_specs=[SMEM] * 2 + [VMEM] + [HBM] * 9,
         out_specs=VMEM,
         scratch_shapes=[
             buffer(plan.modes, 2 * plan.parts, half),
@@ -938,7 +948,7 @@
     potential, values = pl.pallas_call(
         functools.partial(backward_kernel, plan, n_blocks, block_atoms),
         out_shape=(shaped(x_len, y_len, grid), shaped(plan.n_gx * n_blocks, 128)),
-        in_specs=[HBM] * 9,
+        in_specs=[HBM] * 8 + [VMEM],
         out_specs=(HBM, VMEM),
         scratch_shapes=[
             buffer(plan.lane_tiles * plan.planes, 128),

time: 117 us -> 113 us (0.966)
  waiting for transfers between devices: 8.71 us -> 4.51 us
  starting transfers between devices: 28.9 us -> 31.7 us
  local copies, waits for them, and re-layouts: 6.5 us -> 4.75 us
  other arithmetic: 1.49 us -> 0.08 us
    ppermute x4, waiting for transfers between devices: 4.28 us -> 0.01 us  [shifted(): lax.ppermute(block, axis, [(i, (i + step) % count) for i in range(count)])]
    all_to_all x1, starting transfers between devices: 6.84 us -> 8.98 us  [solve_poisson(): lax.all_to_all(message, ('gx', 'gy'), split_axis=0, concat_axis=0, tiled=...]
    reshape x1 -> x0, other arithmetic: 1.41 us -> none  [after(): marks = jnp.stack([other[0, 0, 0] for other in others]).reshape(1, 1, -1)]
    dynamic_update_slice x1 -> x0, local copies, waits for them, and re-layouts: 1.28 us -> none  [after(): return lax.dynamic_update_slice(message, marks, (0, 0, lane))]
  transfers between devices with their start and end apart: 8 -> 8, of which waited for: 5 -> 3; matrix products, arithmetic and copies ran while one was open for 3% -> 1% of each run, Pallas kernels for 19% -> 38%
where the time goes in v6:
time: 113 us; the launch traced here: 112 us
  Pallas kernels  69.8 us (62%)
  starting transfers between devices  31.7 us (28%)
  local copies, waits for them, and re-layouts  4.75 us (4%)
  waiting for transfers between devices  4.51 us (4%)
    pallas_call x3, Pallas kernels, pair_part(): pl.pallas_call(functools.partial(pair_kernel, n_blocks, block_atoms, list...  22.3 us
    pallas_call x1, Pallas kernels, solve_poisson(): pl.pallas_call(functools.partial(forward_kernel, plan, n_blocks, block_at...  19.9 us
    pallas_call x1, Pallas kernels, solve_poisson(): pl.pallas_call(functools.partial(backward_kernel, plan, n_blocks, block_a...  15.4 us
    pallas_call x1, Pallas kernels, solve_poisson(): pl.pallas_call(functools.partial(interface_kernel, plan), out_shape=shape...  9.55 us
    all_to_all x1, starting transfers between devices, solve_poisson(): lax.all_to_all(message, ('gx', 'gy'), split_axis=0, concat_axis=0, tiled=...  8.98 us
    ppermute x4, starting transfers between devices, shifted(): lax.ppermute(block, axis, [(i, (i + step) % count) for i in range(count)])  7.58 us
    all_to_all x1, starting transfers between devices, solve_poisson(): lax.all_to_all(outgoing, ('gx', 'gy'), split_axis=0, concat_axis=0, tiled...  5.84 us
    all_to_all x1, starting transfers between devices, body(): lax.all_to_all(values, 'gx', split_axis=0, concat_axis=0, tiled=True)  5.69 us
  transfers between devices with their start and end apart: 8, of which 3 were waited for; matrix products, arithmetic and copies ran while one was open for 1% of the time, Pallas kernels for 38%

profile of v6, /device:TPU:0, one launch (start us, length us, event | category | flops | bytes accessed | tf_op | source)
XLA Modules:
  0.0 111.5 jit_solution(518900712300511071)
XLA Ops:
  0.6 1.6 %prepare_atoms.1 = (f32[256,128]{1,0:T(8,128)}, f32[1,5,1024]{2,1,0:T(8,128)}) custom-call(s32[1,32]{1,0:T(1,128)} %bitcast.17, s32[1,32]{1,0:T(1,128)} %bitcast.19, f32[16]{0:T(128)} %type_radius.1, f32[1,3,1,1024]{3,2,1,0:T(1,128)} %bitcast.16, f32[1,1,1024]{2,1,0:T(1,128)} %charge.1, s32[1,1,1024]{2,1,0:T(1,128)} %types.1, s32[1,1,1024]{2,1,0:T(1,128)} %cells.1), custom_call_target="tpu_custom_call" | custom-call | tf_op jit(solution)/shard_map/prepare_atoms/pallas_call | solution.py:1005
  2.3 0.5 collective-permute-start
  2.7 2.9 %collective-permute-start.1 = (f32[1,5,1024]{2,1,0:T(8,128)}, f32[1,5,1024]{2,1,0:T(8,128)S(1)}, u32[]{:S(2)}, u32[]{:S(2)}) collective-permute-start(f32[1,5,1024]{2,1,0:T(8,128)} %get-tuple-element.11), channel_id=1, source_target_pairs={{0,28},{4,0},{8,4},{12,8},{16,12},{20,16},{24,20},{28,24},{1,29},{... | collective-permute-start | bytes 61448 | tf_op jit(solution)/shard_map/ppermute | solution.py:985
  5.6 3.6 %all-to-all-start = ((f32[8,32,128]{2,1,0:T(8,128)}), f32[8,32,128]{2,1,0:T(8,128)S(1)}, u32[]{:S(2)}, u32[]{:S(2)}) async-start(f32[8,32,128]{2,1,0:T(8,128)} %bitcast.14), calls=%async_computation | async-start | bytes 262144 | tf_op jit(solution)/shard_map/all_to_all | solution.py:1022
  9.2 0.0 collective-permute-done
  9.2 0.8 constant_dynamic-update-slice_fusion.1
  10.0 0.0 collective-permute-done.1
  10.0 0.0 copy-start.3
  10.0 4.2 %collective-permute-start.3 = (f32[3,5,1024]{2,1,0:T(8,128)S(1)}, f32[3,5,1024]{2,1,0:T(8,128)S(1)}, u32[]{:S(2)}, u32[]{:S(2)}) collective-permute-start(f32[3,5,1024]{2,1,0:T(8,128)S(1)} %constant_dynamic-update-slice_fusion.refs_7_.middle), channel_id=1, source_target_pairs={{0,3},{1,0},{2,1},{3,2},{4,7},{5,4},{6,5},{7,6},{8,11},{9,8},{10,9... | collective-permute-start | bytes 184328 | tf_op jit(solution)/shard_map/ppermute | solution.py:985
  14.2 0.0 collective-permute-start.2
  14.2 0.5 all-to-all-done
  14.7 0.0 copy-start.2
  14.7 0.0 copy-done.3
  14.7 0.6 copy-done.2
  15.4 19.9 %forward_solve.1 = (f32[36,72,384]{2,1,0:T(8,128)}, s32[256,128]{1,0:T(8,128)}, f32[288,1,256]{2,1,0:T(1,128)}) custom-call(s32[1]{0:T(128)} %bitcast.first_code, f32[256,128]{1,0:T(8,128)} %bitcast.13, f32[36,72,288]{2,1,0:T(8,128)} %refs_1_.1, f32[384,384]{1,0:T(8,128)} %constant.46.clone.refs_2_.z_full_hbm, ...), custom_call_target="tpu_custom_call" | custom-call | tf_op jit(solution)/shard_map/forward_solve/pallas_call | solution.py:868
  35.3 0.0 collective-permute-done.3.high.refs_2_
  35.3 0.0 copy-start.4
  35.3 0.0 collective-permute-done.2.low.refs_1_
  35.3 0.0 copy-start.5
  35.3 0.6 copy-done.4
  35.9 0.0 copy-done.5
  36.0 0.9 order_message.1
  36.9 9.0 %all-to-all-start.1 = ((f32[288,1,256]{2,1,0:T(1,128)}), f32[288,1,256]{2,1,0:T(1,128)S(1)}, u32[]{:S(2)}, u32[]{:S(2)}) async-start(f32[288,1,256]{2,1,0:T(1,128)} %order_message.1), calls=%async_computation.1 | async-start | bytes 589824 | tf_op jit(solution)/shard_map/all_to_all | solution.py:904
  45.9 0.6 broadcast_in_dim.8.earlier
  46.5 10.2 %pair_forces.3._.earlier = f32[3,1,512]{2,1,0:T(1,128)} custom-call(s32[1,3,1,32]{3,2,1,0:T(1,128)} %bitcast.20, f32[3,5,1024]{2,1,0:T(8,128)} %copy-done.5, f32[3,5,1024]{2,1,0:T(8,128)} %copy-done.3, f32[3,5,1024]{2,1,0:T(8,128)} %copy-done.4, f32[3,1,128]{2,1,0:T(1,128)} %broadcast_in_dim.8.earlier), custom_call_target="tpu_custom_call" | custom-call | flops 33030144 | bytes 204800 | tf_op jit(solution)/shard_map/pair_forces/pallas_call | solution.py:1034
  56.7 0.0 all-to-all-done.1.incoming_hbm
  56.7 0.0 copy-start.1
  56.7 0.7 copy-done.1
  57.4 9.5 %interface_solve.1 = f32[288,1,256]{2,1,0:T(1,128)} custom-call(s32[1]{0:T(128)} %bitcast.6.first_mode, f32[288]{0:T(512)} %constant.51.clone.stiff_z, f32[3,1,512]{2,1,0:T(1,128)} %pair_forces.3._.earlier, f32[288,1,256]{2,1,0:T(1,128)} %copy-done.1, bf16[96,192]{1,0:T(8,128)(2,1)} %constant.52.clone.gather_hbm, f32[512,384]{1,0:T(8,128)} %constant.53.clone.along_y_hbm, ...), custom_call_target="tpu_custom_call" | custom-call | tf_op jit(solution)/shard_map/interface_solve/pallas_call | solution.py:925
  66.9 5.8 %all-to-all-start.2 = ((f32[288,1,256]{2,1,0:T(1,128)}), f32[288,1,256]{2,1,0:T(1,128)S(1)}, u32[]{:S(2)}, u32[]{:S(2)}) async-start(f32[288,1,256]{2,1,0:T(1,128)} %interface_solve.1), calls=%async_computation.2 | async-start | bytes 589824 | tf_op jit(solution)/shard_map/all_to_all | solution.py:946
  72.8 8.1 %pair_forces.4._.earlier = f32[3,1,896]{2,1,0:T(1,128)} custom-call(s32[1,3,1,32]{3,2,1,0:T(1,128)} %bitcast.21, f32[3,5,1024]{2,1,0:T(8,128)} %copy-done.5, f32[3,5,1024]{2,1,0:T(8,128)} %copy-done.3, f32[3,5,1024]{2,1,0:T(8,128)} %copy-done.4, f32[3,1,512]{2,1,0:T(1,128)} %pair_forces.3._.earlier), custom_call_target="tpu_custom_call" | custom-call | flops 24772608 | bytes 204800 | tf_op jit(solution)/shard_map/pair_forces/pallas_call | solution.py:1034
  80.9 2.5 %all-to-all-done.2.message_hbm = f32[288,1,256]{2,1,0:T(1,128)S(1)} async-done(((f32[288,1,256]{2,1,0:T(1,128)}), f32[288,1,256]{2,1,0:T(1,128)S(1)}, u32[]{:S(2)}, u32[]{:S(2)}) %all-to-all-start.2) | async-done | bytes 294944 | tf_op jit(solution)/shard_map/all_to_all | solution.py:946
  83.4 0.0 copy-start
  83.4 0.7 copy-done
  84.1 0.0 copy-start.6
  84.1 15.4 %backward_solve.1 = (f32[36,72,288]{2,1,0:T(8,128)}, f32[256,128]{1,0:T(8,128)}) custom-call(s32[256,128]{1,0:T(8,128)} %get-tuple-element.12.places_hbm, f32[288,1,256]{2,1,0:T(1,128)} %copy-done, f32[384,256]{1,0:T(8,128)} %constant.50.clone.refs_6_.interface_hbm, f32[36,72,384]{2,1,0:T(8,128)} %constant.48.clone.refs_4_.factors_hbm, ...), custom_call_target="tpu_custom_call" | custom-call | tf_op jit(solution)/shard_map/backward_solve/pallas_call | solution.py:948
  99.5 5.7 %all-to-all-start.3 = ((f32[8,32,128]{2,1,0:T(8,128)}), f32[8,32,128]{2,1,0:T(8,128)S(1)}, u32[]{:S(2)}, u32[]{:S(2)}) async-start(f32[8,32,128]{2,1,0:T(8,128)} %bitcast.15), calls=%async_computation.3 | async-start | bytes 262144 | tf_op jit(solution)/shard_map/all_to_all | solution.py:1056
  105.2 4.0 %pair_forces.5 = f32[3,1,1024]{2,1,0:T(1,128)} custom-call(s32[1,3,1,32]{3,2,1,0:T(1,128)} %bitcast.22, f32[3,5,1024]{2,1,0:T(8,128)} %copy-done.5, f32[3,5,1024]{2,1,0:T(8,128)} %copy-done.3, f32[3,5,1024]{2,1,0:T(8,128)} %copy-done.4, f32[3,1,896]{2,1,0:T(1,128)} %pair_forces.4._.earlier), custom_call_target="tpu_custom_call" | custom-call | flops 8257536 | bytes 204800 | tf_op jit(solution)/shard_map/pair_forces/pallas_call | solution.py:1034
  109.2 1.5 %all-to-all-done.3 = f32[8,32,128]{2,1,0:T(8,128)S(1)} async-done(((f32[8,32,128]{2,1,0:T(8,128)}), f32[8,32,128]{2,1,0:T(8,128)S(1)}, u32[]{:S(2)}, u32[]{:S(2)}) %all-to-all-start.3) | async-done | bytes 131104 | tf_op jit(solution)/shard_map/all_to_all | solution.py:1056
  110.8 0.0 copy-done.6
  110.8 0.1 slice_select_fusion
  110.9 0.7 reshape.33
  (3 shorter events, 0.0 us)
Async XLA Ops:
  2.3 6.9 %collective-permute-start = (f32[1,5,1024]{2,1,0:T(8,128)}, f32[1,5,1024]{2,1,0:T(8,128)S(1)}, u32[]{:S(2)}, u32[]{:S(2)}) collective-permute-start(f32[1,5,1024]{2,1,0:T(8,128)} %get-tuple-element.11), channel_id=1, source_target_pairs={{0,4},{4,8},{8,12},{12,16},{16,20},{20,24},{24,28},{28,0},{1,5},{5... | collective-permute-start | bytes 61448 | tf_op jit(solution)/shard_map/ppermute | solution.py:985
  2.7 7.2 %collective-permute-start.1 = (f32[1,5,1024]{2,1,0:T(8,128)}, f32[1,5,1024]{2,1,0:T(8,128)S(1)}, u32[]{:S(2)}, u32[]{:S(2)}) collective-permute-start(f32[1,5,1024]{2,1,0:T(8,128)} %get-tuple-element.11), channel_id=1, source_target_pairs={{0,28},{4,0},{8,4},{12,8},{16,12},{20,16},{24,20},{28,24},{1,29},{... | collective-permute-start | bytes 61448 | tf_op jit(solution)/shard_map/ppermute | solution.py:985
  5.6 9.1 %all-to-all-start = ((f32[8,32,128]{2,1,0:T(8,128)}), f32[8,32,128]{2,1,0:T(8,128)S(1)}, u32[]{:S(2)}, u32[]{:S(2)}) async-start(f32[8,32,128]{2,1,0:T(8,128)} %bitcast.14), calls=%async_computation | async-start | bytes 262144 | tf_op jit(solution)/shard_map/all_to_all | solution.py:1022
  10.0 4.7 %copy-start.3 = (f32[3,5,1024]{2,1,0:T(8,128)}, f32[3,5,1024]{2,1,0:T(8,128)S(1)}, u32[]{:S(2)}) copy-start(f32[3,5,1024]{2,1,0:T(8,128)S(1)} %constant_dynamic-update-slice_fusion.refs_7_.middle) | copy-start | bytes 184324
  10.0 25.3 %collective-permute-start.3 = (f32[3,5,1024]{2,1,0:T(8,128)S(1)}, f32[3,5,1024]{2,1,0:T(8,128)S(1)}, u32[]{:S(2)}, u32[]{:S(2)}) collective-permute-start(f32[3,5,1024]{2,1,0:T(8,128)S(1)} %constant_dynamic-update-slice_fusion.refs_7_.middle), channel_id=1, source_target_pairs={{0,3},{1,0},{2,1},{3,2},{4,7},{5,4},{6,5},{7,6},{8,11},{9,8},{10,9... | collective-permute-start | bytes 184328 | tf_op jit(solution)/shard_map/ppermute | solution.py:985
  14.2 21.1 %collective-permute-start.2 = (f32[3,5,1024]{2,1,0:T(8,128)S(1)}, f32[3,5,1024]{2,1,0:T(8,128)S(1)}, u32[]{:S(2)}, u32[]{:S(2)}) collective-permute-start(f32[3,5,1024]{2,1,0:T(8,128)S(1)} %constant_dynamic-update-slice_fusion.refs_7_.middle), channel_id=1, source_target_pairs={{0,1},{1,2},{2,3},{3,0},{4,5},{5,6},{6,7},{7,4},{8,9},{9,10},{10,1... | collective-permute-start | bytes 184328 | tf_op jit(solution)/shard_map/ppermute | solution.py:985
  14.7 0.6 copy-start.2
  35.3 0.7 copy-start.4
  35.3 0.7 copy-start.5
  36.9 19.8 %all-to-all-start.1 = ((f32[288,1,256]{2,1,0:T(1,128)}), f32[288,1,256]{2,1,0:T(1,128)S(1)}, u32[]{:S(2)}, u32[]{:S(2)}) async-start(f32[288,1,256]{2,1,0:T(1,128)} %order_message.1), calls=%async_computation.1 | async-start | bytes 589824 | tf_op jit(solution)/shard_map/all_to_all | solution.py:904
  56.7 0.7 copy-start.1
  66.9 16.4 %all-to-all-start.2 = ((f32[288,1,256]{2,1,0:T(1,128)}), f32[288,1,256]{2,1,0:T(1,128)S(1)}, u32[]{:S(2)}, u32[]{:S(2)}) async-start(f32[288,1,256]{2,1,0:T(1,128)} %interface_solve.1), calls=%async_computation.2 | async-start | bytes 589824 | tf_op jit(solution)/shard_map/all_to_all | solution.py:946
  83.4 0.7 copy-start
  84.1 26.7 %copy-start.6 = (s32[1,1,32]{2,1,0:T(1,128)S(1)}, s32[1,1,32]{2,1,0:T(1,128)}, u32[]{:S(2)}) copy-start(s32[1,1,32]{2,1,0:T(1,128)} %param.29) | copy-start | bytes 388
  99.5 11.2 %all-to-all-start.3 = ((f32[8,32,128]{2,1,0:T(8,128)}), f32[8,32,128]{2,1,0:T(8,128)S(1)}, u32[]{:S(2)}, u32[]{:S(2)}) async-start(f32[8,32,128]{2,1,0:T(8,128)} %bitcast.15), calls=%async_computation.3 | async-start | bytes 262144 | tf_op jit(solution)/shard_map/all_to_all | solution.py:1056

commit v7 on v6

--- a/solution.py
+++ b/solution.py
@@ -753,10 +753,8 @@
         copies[target * n_blocks : (target + 1) * n_blocks, :] = payload[...]
 
 
-def pair_kernel(
-    n_blocks, block_atoms, listed, first, part_atoms, listing, low, middle, high, earlier, forces,
-    table, columns, results,
-):
+def pair_kernel(n_blocks, block_atoms, listed, first, part_atoms, listing, low, middle, high, *rest):
+    *earlier, forces, table, columns, results = rest
     tile_atoms = n_blocks * block_atoms
     sides = (low, middle, high)
     for step_x in range(3):
@@ -807,7 +805,7 @@
     columns[...] = jnp.transpose(results[...])
     if first:
         for axis in range(3):
-            forces[axis, :, :first] = earlier[axis, :, :first]
+            forces[axis, :, :first] = earlier[0][axis, :, :first]
     for axis in range(3):
         forces[axis, :, first : first + part_atoms] = columns[axis : axis + 1, :]
 
@@ -841,7 +839,7 @@
     return pl.pallas_call(
         order_kernel,
         out_shape=shaped(*message.shape),
-        in_specs=[HBM] + [VMEM] * len(others),
+        in_specs=[HBM] * (1 + len(others)),
         out_specs=HBM,
         input_output_aliases={0: 0},
         compiler_params=limit(VMEM_MIB),
@@ -872,7 +870,7 @@
             jax.ShapeDtypeStruct(code_shape, jnp.int32),
             shaped(total, 1, 2 * half),
         ),
-        in_specs=[SMEM] + [HBM] * 7 + [VMEM],
+        in_specs=[SMEM] + [HBM] * 8,
         out_specs=(HBM, HBM, VMEM),
         scratch_shapes=[buffer(plan.lane_tiles * plan.planes, 128)]
         + shared
@@ -900,7 +898,7 @@
     )(first_code, codes, density, z_full, y_table, factors, edge_y, interface, neighbours[0])
     message = after(message, neighbours[1:])
     eighth = n_blocks * block_atoms // 8
-    first_pairs = pair_part(0, 4 * eighth, None)
+    first_pairs = pair_part(0, 4 * eighth)
     incoming = lax.all_to_all(message, ("gx", "gy"), split_axis=0, concat_axis=0, tiled=True)
     gather = plan.gather_table()
     along_y, along_x = plan.line_tables()
@@ -925,7 +923,7 @@
     outgoing = pl.pallas_call(
         functools.partial(interface_kernel, plan),
         out_shape=shaped(total, 1, 2 * half),
-        in_specs=[SMEM] * 2 + [VMEM] + [HBM] * 9,
+        in_specs=[SMEM] * 2 + [HBM] * 10,
         out_specs=VMEM,
         scratch_shapes=[
             buffer(plan.modes, 2 * plan.parts, half),
@@ -948,7 +946,7 @@
     potential, values = pl.pallas_call(
         functools.partial(backward_kernel, plan, n_blocks, block_atoms),
         out_shape=(shaped(x_len, y_len, grid), shaped(plan.n_gx * n_blocks, 128)),
-        in_specs=[HBM] * 8 + [VMEM],
+        in_specs=[HBM] * 9,
         out_specs=(HBM, VMEM),
         scratch_shapes=[
             buffer(plan.lane_tiles * plan.planes, 128),
@@ -1028,13 +1026,11 @@
     listed = neighbour_tiles.shape[3]
     listing = neighbour_tiles.transpose(0, 3, 1, 2)
 
-    def pair_part(first, part_atoms, earlier):
-        if earlier is None:
-            earlier = jnp.zeros((3, 1, 128), jnp.float32)
+    def pair_part(first, part_atoms, *earlier):
         return pl.pallas_call(
             functools.partial(pair_kernel, n_blocks, block_atoms, listed, first, part_atoms),
             out_shape=shaped(3, 1, first + part_atoms),
-            in_specs=[SMEM] + [VMEM] * 4,
+            in_specs=[SMEM] + [VMEM] * (3 + len(earlier)),
             out_specs=VMEM,
             scratch_shapes=[
                 buffer(9, 5, 8, tile_atoms),
@@ -1048,7 +1044,7 @@
                 transcendentals=listed * tile_atoms * part_atoms,
             ),
             name="pair_forces",
-        )(listing, below, triple, above, earlier)
+        )(listing, below, triple, above, *earlier)
 
     potential, values, pair_force = solve_poisson(
         plan, qm_density, codes, first_code, n_blocks, block_atoms, (triple, below, above), pair_part

time: 113 us -> 111 us (0.982)
  Pallas kernels: 69.8 us -> 67.9 us
  transfers between devices with their start and end apart: 8 -> 8, of which waited for: 3 -> 4; matrix products, arithmetic and copies ran while one was open for 1% -> 1% of each run, Pallas kernels for 38% -> 38%
where the time goes in v7:
time: 111 us; the launch traced here: 110 us
  Pallas kernels  67.9 us (61%)
  starting transfers between devices  32 us (29%)
  waiting for transfers between devices  4.88 us (4%)
  local copies, waits for them, and re-layouts  4.18 us (4%)
    pallas_call x3, Pallas kernels, pair_part(): pl.pallas_call(functools.partial(pair_kernel, n_blocks, block_atoms, list...  22.3 us
    pallas_call x1, Pallas kernels, solve_poisson(): pl.pallas_call(functools.partial(forward_kernel, plan, n_blocks, block_at...  19.5 us
    pallas_call x1, Pallas kernels, solve_poisson(): pl.pallas_call(functools.partial(backward_kernel, plan, n_blocks, block_a...  14.9 us
    pallas_call x1, Pallas kernels, solve_poisson(): pl.pallas_call(functools.partial(interface_kernel, plan), out_shape=shape...  9.53 us
    all_to_all x1, starting transfers between devices, solve_poisson(): lax.all_to_all(message, ('gx', 'gy'), split_axis=0, concat_axis=0, tiled=...  9.25 us
    ppermute x4, starting transfers between devices, shifted(): lax.ppermute(block, axis, [(i, (i + step) % count) for i in range(count)])  7.58 us
    all_to_all x1, starting transfers between devices, body(): lax.all_to_all(values, 'gx', split_axis=0, concat_axis=0, tiled=True)  6.08 us
    all_to_all x1, starting transfers between devices, solve_poisson(): lax.all_to_all(outgoing, ('gx', 'gy'), split_axis=0, concat_axis=0, tiled...  5.48 us
  transfers between devices with their start and end apart: 8, of which 4 were waited for; matrix products, arithmetic and copies ran while one was open for 1% of the time, Pallas kernels for 38%

profile of v7, /device:TPU:0, one launch (start us, length us, event | category | flops | bytes accessed | tf_op | source)
XLA Modules:
  0.0 109.7 jit_solution(12431713373121602576)
XLA Ops:
  0.6 1.6 %prepare_atoms.1 = (f32[256,128]{1,0:T(8,128)}, f32[1,5,1024]{2,1,0:T(8,128)}) custom-call(s32[1,32]{1,0:T(1,128)} %bitcast.17, s32[1,32]{1,0:T(1,128)} %bitcast.19, f32[16]{0:T(128)} %type_radius.1, f32[1,3,1,1024]{3,2,1,0:T(1,128)} %bitcast.16, f32[1,1,1024]{2,1,0:T(1,128)} %charge.1, s32[1,1,1024]{2,1,0:T(1,128)} %types.1, s32[1,1,1024]{2,1,0:T(1,128)} %cells.1), custom_call_target="tpu_custom_call" | custom-call | tf_op jit(solution)/shard_map/prepare_atoms/pallas_call | solution.py:1003
  2.3 0.5 collective-permute-start
  2.7 2.9 %collective-permute-start.1 = (f32[1,5,1024]{2,1,0:T(8,128)}, f32[1,5,1024]{2,1,0:T(8,128)S(1)}, u32[]{:S(2)}, u32[]{:S(2)}) collective-permute-start(f32[1,5,1024]{2,1,0:T(8,128)} %get-tuple-element.11), channel_id=1, source_target_pairs={{0,28},{4,0},{8,4},{12,8},{16,12},{20,16},{24,20},{28,24},{1,29},{... | collective-permute-start | bytes 61448 | tf_op jit(solution)/shard_map/ppermute | solution.py:983
  5.6 3.6 %all-to-all-start = ((f32[8,32,128]{2,1,0:T(8,128)}), f32[8,32,128]{2,1,0:T(8,128)S(1)}, u32[]{:S(2)}, u32[]{:S(2)}) async-start(f32[8,32,128]{2,1,0:T(8,128)} %bitcast.14), calls=%async_computation | async-start | bytes 262144 | tf_op jit(solution)/shard_map/all_to_all | solution.py:1020
  9.2 0.0 collective-permute-done
  9.2 0.8 constant_dynamic-update-slice_fusion.1
  10.0 0.0 collective-permute-done.1
  10.0 0.0 copy-start.3
  10.0 4.2 %collective-permute-start.3 = (f32[3,5,1024]{2,1,0:T(8,128)S(1)}, f32[3,5,1024]{2,1,0:T(8,128)S(1)}, u32[]{:S(2)}, u32[]{:S(2)}) collective-permute-start(f32[3,5,1024]{2,1,0:T(8,128)S(1)} %constant_dynamic-update-slice_fusion.refs_7_.middle), channel_id=1, source_target_pairs={{0,3},{1,0},{2,1},{3,2},{4,7},{5,4},{6,5},{7,6},{8,11},{9,8},{10,9... | collective-permute-start | bytes 184328 | tf_op jit(solution)/shard_map/ppermute | solution.py:983
  14.2 0.0 collective-permute-start.2
  14.2 0.5 all-to-all-done
  14.7 0.0 copy-start.2
  14.7 0.0 copy-done.3
  14.7 0.6 copy-done.2
  15.4 19.5 %forward_solve.1 = (f32[36,72,384]{2,1,0:T(8,128)}, s32[256,128]{1,0:T(8,128)}, f32[288,1,256]{2,1,0:T(1,128)}) custom-call(s32[1]{0:T(128)} %bitcast.first_code, f32[256,128]{1,0:T(8,128)} %bitcast.13, f32[36,72,288]{2,1,0:T(8,128)} %refs_1_.1, f32[384,384]{1,0:T(8,128)} %constant.45.clone.refs_2_.z_full_hbm, ...), custom_call_target="tpu_custom_call" | custom-call | tf_op jit(solution)/shard_map/forward_solve/pallas_call | solution.py:866
  34.8 0.0 collective-permute-done.3.high.refs_2_
  34.9 0.0 copy-start.4
  34.9 0.0 collective-permute-done.2.low.refs_1_
  34.9 0.0 copy-start.5
  34.9 0.6 copy-done.4
  35.5 0.0 copy-done.5
  35.5 9.3 %all-to-all-start.1 = ((f32[288,1,256]{2,1,0:T(1,128)}), f32[288,1,256]{2,1,0:T(1,128)S(1)}, u32[]{:S(2)}, u32[]{:S(2)}) async-start(f32[288,1,256]{2,1,0:T(1,128)} %order_message.1), calls=%async_computation.1 | async-start | bytes 589824 | tf_op jit(solution)/shard_map/all_to_all | solution.py:902
  44.8 10.2 %pair_forces.3._.rest_0_ = f32[3,1,512]{2,1,0:T(1,128)} custom-call(s32[1,3,1,32]{3,2,1,0:T(1,128)} %bitcast.20, f32[3,5,1024]{2,1,0:T(8,128)} %copy-done.5, f32[3,5,1024]{2,1,0:T(8,128)} %copy-done.3, f32[3,5,1024]{2,1,0:T(8,128)} %copy-done.4), custom_call_target="tpu_custom_call" | custom-call | flops 33030144 | bytes 204800 | tf_op jit(solution)/shard_map/pair_forces/pallas_call | solution.py:1030
  55.0 0.4 all-to-all-done.1.incoming_hbm
  55.4 0.0 copy-start.1
  55.4 0.7 copy-done.1
  56.1 9.5 %interface_solve.1 = f32[288,1,256]{2,1,0:T(1,128)} custom-call(s32[1]{0:T(128)} %bitcast.6.first_mode, f32[288]{0:T(512)} %constant.50.clone.stiff_z, f32[3,1,512]{2,1,0:T(1,128)} %pair_forces.3._.rest_0_, f32[288,1,256]{2,1,0:T(1,128)} %copy-done.1, bf16[96,192]{1,0:T(8,128)(2,1)} %constant.51.clone.gather_hbm, f32[512,384]{1,0:T(8,128)} %constant.52.clone.along_y_hbm, ...), custom_call_target="tpu_custom_call" | custom-call | tf_op jit(solution)/shard_map/interface_solve/pallas_call | solution.py:923
  65.7 5.5 %all-to-all-start.2 = ((f32[288,1,256]{2,1,0:T(1,128)}), f32[288,1,256]{2,1,0:T(1,128)S(1)}, u32[]{:S(2)}, u32[]{:S(2)}) async-start(f32[288,1,256]{2,1,0:T(1,128)} %interface_solve.1), calls=%async_computation.2 | async-start | bytes 589824 | tf_op jit(solution)/shard_map/all_to_all | solution.py:944
  71.1 8.1 %pair_forces.4._.rest_0_ = f32[3,1,896]{2,1,0:T(1,128)} custom-call(s32[1,3,1,32]{3,2,1,0:T(1,128)} %bitcast.21, f32[3,5,1024]{2,1,0:T(8,128)} %copy-done.5, f32[3,5,1024]{2,1,0:T(8,128)} %copy-done.3, f32[3,5,1024]{2,1,0:T(8,128)} %copy-done.4, f32[3,1,512]{2,1,0:T(1,128)} %pair_forces.3._.rest_0_), custom_call_target="tpu_custom_call" | custom-call | flops 24772608 | bytes 204800 | tf_op jit(solution)/shard_map/pair_forces/pallas_call | solution.py:1030
  79.3 2.5 %all-to-all-done.2.message_hbm = f32[288,1,256]{2,1,0:T(1,128)S(1)} async-done(((f32[288,1,256]{2,1,0:T(1,128)}), f32[288,1,256]{2,1,0:T(1,128)S(1)}, u32[]{:S(2)}, u32[]{:S(2)}) %all-to-all-start.2) | async-done | bytes 294944 | tf_op jit(solution)/shard_map/all_to_all | solution.py:944
  81.7 0.0 copy-start
  81.7 0.7 copy-done
  82.4 0.0 copy-start.6
  82.4 14.9 %backward_solve.1 = (f32[36,72,288]{2,1,0:T(8,128)}, f32[256,128]{1,0:T(8,128)}) custom-call(s32[256,128]{1,0:T(8,128)} %get-tuple-element.12.places_hbm, f32[288,1,256]{2,1,0:T(1,128)} %copy-done, f32[384,256]{1,0:T(8,128)} %constant.49.clone.refs_6_.interface_hbm, f32[36,72,384]{2,1,0:T(8,128)} %constant.47.clone.refs_4_.factors_hbm, ...), custom_call_target="tpu_custom_call" | custom-call | tf_op jit(solution)/shard_map/backward_solve/pallas_call | solution.py:946
  97.4 6.1 %all-to-all-start.3 = ((f32[8,32,128]{2,1,0:T(8,128)}), f32[8,32,128]{2,1,0:T(8,128)S(1)}, u32[]{:S(2)}, u32[]{:S(2)}) async-start(f32[8,32,128]{2,1,0:T(8,128)} %bitcast.15), calls=%async_computation.3 | async-start | bytes 262144 | tf_op jit(solution)/shard_map/all_to_all | solution.py:1052
  103.4 4.0 %pair_forces.5 = f32[3,1,1024]{2,1,0:T(1,128)} custom-call(s32[1,3,1,32]{3,2,1,0:T(1,128)} %bitcast.22, f32[3,5,1024]{2,1,0:T(8,128)} %copy-done.5, f32[3,5,1024]{2,1,0:T(8,128)} %copy-done.3, f32[3,5,1024]{2,1,0:T(8,128)} %copy-done.4, f32[3,1,896]{2,1,0:T(1,128)} %pair_forces.4._.rest_0_), custom_call_target="tpu_custom_call" | custom-call | flops 8257536 | bytes 204800 | tf_op jit(solution)/shard_map/pair_forces/pallas_call | solution.py:1030
  107.4 1.5 %all-to-all-done.3 = f32[8,32,128]{2,1,0:T(8,128)S(1)} async-done(((f32[8,32,128]{2,1,0:T(8,128)}), f32[8,32,128]{2,1,0:T(8,128)S(1)}, u32[]{:S(2)}, u32[]{:S(2)}) %all-to-all-start.3) | async-done | bytes 131104 | tf_op jit(solution)/shard_map/all_to_all | solution.py:1052
  109.0 0.0 copy-done.6
  109.0 0.1 slice_select_fusion
  109.1 0.7 reshape.33
  (4 shorter events, 0.0 us)
Async XLA Ops:
  2.3 6.9 %collective-permute-start = (f32[1,5,1024]{2,1,0:T(8,128)}, f32[1,5,1024]{2,1,0:T(8,128)S(1)}, u32[]{:S(2)}, u32[]{:S(2)}) collective-permute-start(f32[1,5,1024]{2,1,0:T(8,128)} %get-tuple-element.11), channel_id=1, source_target_pairs={{0,4},{4,8},{8,12},{12,16},{16,20},{20,24},{24,28},{28,0},{1,5},{5... | collective-permute-start | bytes 61448 | tf_op jit(solution)/shard_map/ppermute | solution.py:983
  2.7 7.2 %collective-permute-start.1 = (f32[1,5,1024]{2,1,0:T(8,128)}, f32[1,5,1024]{2,1,0:T(8,128)S(1)}, u32[]{:S(2)}, u32[]{:S(2)}) collective-permute-start(f32[1,5,1024]{2,1,0:T(8,128)} %get-tuple-element.11), channel_id=1, source_target_pairs={{0,28},{4,0},{8,4},{12,8},{16,12},{20,16},{24,20},{28,24},{1,29},{... | collective-permute-start | bytes 61448 | tf_op jit(solution)/shard_map/ppermute | solution.py:983
  5.6 9.1 %all-to-all-start = ((f32[8,32,128]{2,1,0:T(8,128)}), f32[8,32,128]{2,1,0:T(8,128)S(1)}, u32[]{:S(2)}, u32[]{:S(2)}) async-start(f32[8,32,128]{2,1,0:T(8,128)} %bitcast.14), calls=%async_computation | async-start | bytes 262144 | tf_op jit(solution)/shard_map/all_to_all | solution.py:1020
  10.0 4.7 %copy-start.3 = (f32[3,5,1024]{2,1,0:T(8,128)}, f32[3,5,1024]{2,1,0:T(8,128)S(1)}, u32[]{:S(2)}) copy-start(f32[3,5,1024]{2,1,0:T(8,128)S(1)} %constant_dynamic-update-slice_fusion.refs_7_.middle) | copy-start | bytes 184324
  10.0 24.9 %collective-permute-start.3 = (f32[3,5,1024]{2,1,0:T(8,128)S(1)}, f32[3,5,1024]{2,1,0:T(8,128)S(1)}, u32[]{:S(2)}, u32[]{:S(2)}) collective-permute-start(f32[3,5,1024]{2,1,0:T(8,128)S(1)} %constant_dynamic-update-slice_fusion.refs_7_.middle), channel_id=1, source_target_pairs={{0,3},{1,0},{2,1},{3,2},{4,7},{5,4},{6,5},{7,6},{8,11},{9,8},{10,9... | collective-permute-start | bytes 184328 | tf_op jit(solution)/shard_map/ppermute | solution.py:983
  14.2 20.6 %collective-permute-start.2 = (f32[3,5,1024]{2,1,0:T(8,128)S(1)}, f32[3,5,1024]{2,1,0:T(8,128)S(1)}, u32[]{:S(2)}, u32[]{:S(2)}) collective-permute-start(f32[3,5,1024]{2,1,0:T(8,128)S(1)} %constant_dynamic-update-slice_fusion.refs_7_.middle), channel_id=1, source_target_pairs={{0,1},{1,2},{2,3},{3,0},{4,5},{5,6},{6,7},{7,4},{8,9},{9,10},{10,1... | collective-permute-start | bytes 184328 | tf_op jit(solution)/shard_map/ppermute | solution.py:983
  14.7 0.6 copy-start.2
  34.9 0.7 copy-start.4
  34.9 0.7 copy-start.5
  35.5 19.9 %all-to-all-start.1 = ((f32[288,1,256]{2,1,0:T(1,128)}), f32[288,1,256]{2,1,0:T(1,128)S(1)}, u32[]{:S(2)}, u32[]{:S(2)}) async-start(f32[288,1,256]{2,1,0:T(1,128)} %order_message.1), calls=%async_computation.1 | async-start | bytes 589824 | tf_op jit(solution)/shard_map/all_to_all | solution.py:902
  55.4 0.7 copy-start.1
  65.7 16.1 %all-to-all-start.2 = ((f32[288,1,256]{2,1,0:T(1,128)}), f32[288,1,256]{2,1,0:T(1,128)S(1)}, u32[]{:S(2)}, u32[]{:S(2)}) async-start(f32[288,1,256]{2,1,0:T(1,128)} %interface_solve.1), calls=%async_computation.2 | async-start | bytes 589824 | tf_op jit(solution)/shard_map/all_to_all | solution.py:944
  81.7 0.7 copy-start
  82.4 26.5 %copy-start.6 = (s32[1,1,32]{2,1,0:T(1,128)S(1)}, s32[1,1,32]{2,1,0:T(1,128)}, u32[]{:S(2)}) copy-start(s32[1,1,32]{2,1,0:T(1,128)} %param.29) | copy-start | bytes 388
  97.4 11.6 %all-to-all-start.3 = ((f32[8,32,128]{2,1,0:T(8,128)}), f32[8,32,128]{2,1,0:T(8,128)S(1)}, u32[]{:S(2)}, u32[]{:S(2)}) async-start(f32[8,32,128]{2,1,0:T(8,128)} %bitcast.15), calls=%async_computation.3 | async-start | bytes 262144 | tf_op jit(solution)/shard_map/all_to_all | solution.py:1052
